TPU v7x, 256 devices: a whole 4x4x8 slice. The times are simulated.
256 devices in a mesh: lat: 16 (over y, x_hi, core), lon: 16 (over z, x_lo).
Axes of the slice: x: 4 (x_hi: 2, x_lo: 2; x = x_hi * 2 + x_lo), y: 4, z: 8, core: 2. Of those that a mesh axis runs over, the one named last changes fastest.
Arguments:
- tracers: float32 [2, 8, 2432, 4096], P(None, None, 'lat', 'lon'), may hold values from -6 to 6
- east_faces: float32 [2, 8, 2432, 4096], P(None, None, 'lat', 'lon'), may hold values from -0.5 to 0.5, as said below
- north_faces: float32 [2, 8, 2432, 4096], P(None, None, 'lat', 'lon'), may hold values from -0.5 to 0.5, as said below
- land_mask: int32 [8, 2432, 4096], P(None, 'lat', 'lon'), may hold values from 0 to 1, as said below
- fold_partner: int32 [4096], P('lon'), may hold values from 0 to 4095, as said below
- vert_mix: float32 [7], replicated, may hold values from 0.05 to 0.3
Outputs:
- tracers_out: float32 [2, 8, 2432, 4096], P(None, None, 'lat', 'lon')
- density: float32 [8, 2432, 4096], P(None, 'lat', 'lon')
Inputs may be any that keep to these rules, and one draw needn't show every extreme that they name: `land_mask`: A column is sea from the top level down to some depth and land below it; whole columns may be land. `fold_partner`: the partner of column i lies in the longitude tile of number (tiles along longitude) - 1 - (i // 256); the partners of one tile's columns are all distinct. `east_faces`: index 1 lies between 0 and 0.06. Both components are zero on every face with land on either side; the east face of the last column joins it to column 0, and the faces stand on sea cells only. `north_faces`: index 1 lies between 0 and 0.06. Both components are zero on every face with land on either side; the north face of the top row joins a cell to the top-row cell at its fold partner.
All inputs are finite; a program needn't handle non-finite values.
Results may differ from a plain program's by a relative error of at most 0.0003.
Values sent between devices are 32-bit elements; how exact they have to be, the bound alone decides.
No kernel may reach another device: no remote copies, remote signals or barrier semaphores. Data moves between devices by JAX's collectives and lax.ppermute only.
A program may use at most 128 MiB of HBM per device.

v0:
```python
import jax
import jax.numpy as jnp
from jax import lax
from jax.sharding import PartitionSpec as P

STEPS = 2


def shifted(x, axis, by):
    count = lax.axis_size(axis)
    return lax.ppermute(x, axis, [(i, (i + by) % count) for i in range(count)])


def passed_along(x, axis, by):
    count = lax.axis_size(axis)
    pairs = [(i, i + by) for i in range(count) if 0 <= i + by < count]
    return lax.ppermute(x, axis, pairs)


def extended(block, sides, width, periodic):
    for axis, dim in sides:
        count = lax.axis_size(axis)
        forward = [(i, i + 1) for i in range(count - 1)]
        if periodic:
            forward.append((count - 1, 0))
        backward = [(target, source) for source, target in forward]
        low = lax.ppermute(
            lax.slice_in_dim(block, block.shape[dim] - width, None, axis=dim), axis, forward
        )
        high = lax.ppermute(lax.slice_in_dim(block, 0, width, axis=dim), axis, backward)
        block = jnp.concatenate([low, block, high], axis=dim)
    return block


def partner(x, axis, apart):
    return lax.ppermute(x, axis, [(i, i ^ 1 << apart) for i in range(lax.axis_size(axis))])


def quick_flux(c_minus, c_zero, c_plus, c_plus2, flow_number, spread_number):
    upwind = 0.75 * c_zero + 0.375 * c_plus - 0.125 * c_minus
    downwind = 0.75 * c_plus + 0.375 * c_zero - 0.125 * c_plus2
    return flow_number * jnp.where(flow_number > 0.0, upwind, downwind) - spread_number * (
        c_plus - c_zero
    )


def on_device(tracers, east_faces, north_faces, land_mask, fold_partner, vert_mix):
    tile_rows = tracers.shape[2]
    tile_cols = tracers.shape[3]
    west_edge = shifted(east_faces[:, :, :, tile_cols - 1 :], "lon", 1)
    south_edge = passed_along(north_faces[:, :, tile_rows - 1 :, :], "lat", 1)
    east_all = jnp.concatenate([west_edge, east_faces], axis=3)
    north_all = jnp.concatenate([south_edge, north_faces], axis=2)
    wet_cells = land_mask.astype(jnp.float32)
    vert_open = vert_mix[:, None, None] * wet_cells[:-1] * wet_cells[1:]
    at_top = lax.axis_index("lat") == lax.axis_size("lat") - 1
    lon_count = lax.axis_size("lon")
    offset = (lon_count - 1 - lax.axis_index("lon")) * tile_cols
    local_index = fold_partner - offset
    fields = tracers
    for turn_index in range(STEPS):
        lon_padded = extended(fields, (("lon", 3),), 2, True)
        lat_padded = extended(fields, (("lat", 2),), 2, False)
        mirror_rows = fields[:, :, tile_rows - 2 :, :]
        for bit_index in range(lon_count.bit_length() - 1):
            mirror_rows = partner(mirror_rows, "lon", bit_index)
        fold_ghost = jnp.take(mirror_rows[:, :, ::-1, :], local_index, axis=3)
        lat_padded = jnp.concatenate(
            [
                lat_padded[:, :, : tile_rows + 2, :],
                jnp.where(at_top, fold_ghost, lat_padded[:, :, tile_rows + 2 :, :]),
            ],
            axis=2,
        )
        flux_east = quick_flux(
            lon_padded[..., 0 : tile_cols + 1],
            lon_padded[..., 1 : tile_cols + 2],
            lon_padded[..., 2 : tile_cols + 3],
            lon_padded[..., 3 : tile_cols + 4],
            east_all[0],
            east_all[1],
        )
        flux_north = quick_flux(
            lat_padded[:, :, 0 : tile_rows + 1],
            lat_padded[:, :, 1 : tile_rows + 2],
            lat_padded[:, :, 2 : tile_rows + 3],
            lat_padded[:, :, 3 : tile_rows + 4],
            north_all[0],
            north_all[1],
        )
        horizontal = (
            flux_east[..., :-1]
            - flux_east[..., 1:]
            + (flux_north[:, :, :-1] - flux_north[:, :, 1:])
        )
        vertical = vert_open * (fields[:, 1:] - fields[:, :-1])
        zero_layer = jnp.zeros_like(fields[:, :1])
        change = horizontal + (
            jnp.concatenate([vertical, zero_layer], axis=1)
            - jnp.concatenate([zero_layer, vertical], axis=1)
        )
        fields = fields + wet_cells * change
    potential = fields[0]
    salinity = fields[1]
    density = wet_cells * (0.8 * salinity - 0.2 * potential - 0.05 * potential * potential)
    return (fields, density)


def solution(mesh):
    in_specs = (
        P(None, None, "lat", "lon"),
        P(None, None, "lat", "lon"),
        P(None, None, "lat", "lon"),
        P(None, "lat", "lon"),
        P("lon"),
        P(),
    )
    out_specs = (P(None, None, "lat", "lon"), P(None, "lat", "lon"))
    return jax.shard_map(
        on_device, mesh=mesh, in_specs=in_specs, out_specs=out_specs, check_vma=False
    )
```

profile of v0, /device:TPU:1, one launch (start us, length us, event | category | flops | bytes accessed | tf_op | source)
XLA Modules:
  0.0 128.5 jit_solution(5831187649731300934)
XLA Ops:
  0.6 0.0 copy-start
  0.6 1.8 %fusion.52 = (f32[2,8,2,256]{3,2,1,0:T(2,128)S(1)}, f32[2,8,2,256]{3,2,1,0:T(2,128)}) fusion(f32[2,8,152,256]{3,2,1,0:T(8,128)} %param.8), kind=kLoop, calls=%fused_computation.92 | loop fusion | bytes 131072 | tf_op jit(solution)/shard_map/slice | solution.py:28
  2.4 2.0 %collective-permute-start.5 = (f32[2,8,2,256]{3,2,1,0:T(2,128)S(1)}, f32[2,8,2,256]{3,2,1,0:T(2,128)}, u32[]{:S(2)}, u32[]{:S(2)}) collective-permute-start(f32[2,8,2,256]{3,2,1,0:T(2,128)S(1)} %get-tuple-element.23), channel_id=1, source_target_pairs={{0,1},{1,0},{2,3},{3,2},{4,5},{5,4},{6,7},{7,6},{8,9},{9,8},{10,11... | collective-permute-start | bytes 98312 | tf_op jit(solution)/shard_map/ppermute | solution.py:36
  4.4 5.2 %collective-permute-start.4 = (f32[2,8,2,256]{3,2,1,0:T(2,128)S(1)}, f32[2,8,2,256]{3,2,1,0:T(2,128)S(1)}, u32[]{:S(2)}, u32[]{:S(2)}) collective-permute-start(f32[2,8,2,256]{3,2,1,0:T(2,128)S(1)} %get-tuple-element.23), channel_id=1, source_target_pairs={{0,16},{16,32},{32,48},{48,64},{64,80},{80,96},{96,112},{112,128},... | collective-permute-start | bytes 98312 | tf_op jit(solution)/shard_map/ppermute | solution.py:27
  9.6 0.9 slice.167
  10.6 1.9 %collective-permute-start.3 = (f32[2,8,1,256]{3,2,1,0:T(1,128)S(1)}, f32[2,8,1,256]{3,2,1,0:T(1,128)S(1)}, u32[]{:S(2)}, u32[]{:S(2)}) collective-permute-start(f32[2,8,1,256]{3,2,1,0:T(1,128)S(1)} %slice.167), channel_id=1, source_target_pairs={{0,16},{16,32},{32,48},{48,64},{64,80},{80,96},{96,112},{112,128},... | collective-permute-start | bytes 49160 | tf_op jit(solution)/shard_map/ppermute | solution.py:17
  12.5 2.4 %collective-permute-start.9 = (f32[2,8,2,256]{3,2,1,0:T(2,128)}, f32[2,8,2,256]{3,2,1,0:T(2,128)S(1)}, u32[]{:S(2)}, u32[]{:S(2)}) collective-permute-start(f32[2,8,2,256]{3,2,1,0:T(2,128)} %get-tuple-element.24), channel_id=1, source_target_pairs={{16,0},{32,16},{48,32},{64,48},{80,64},{96,80},{112,96},{128,112},... | collective-permute-start | bytes 98312 | tf_op jit(solution)/shard_map/ppermute | solution.py:30
  14.9 2.7 %slice.156 = f32[2,8,152,1]{3,2,1,0:T(8,128)} slice(f32[2,8,152,256]{3,2,1,0:T(8,128)} %param.9), slice={[0:2], [0:8], [0:152], [255:256]} | slice | bytes 19456 | tf_op jit(solution)/shard_map/slice | solution.py:50
  17.6 1.9 %copy.214 = f32[2,8,152,1]{2,1,3,0:T(8,128)S(1)} copy(f32[2,8,152,1]{3,2,1,0:T(8,128)} %slice.156) | data formatting | bytes 19456
  19.5 0.1 collective-permute-start
  19.6 0.0 copy-start.17
  19.6 1.8 %fusion.51 = (f32[2,8,152,2]{3,2,1,0:T(8,128)}, f32[2,8,152,2]{3,2,1,0:T(8,128)}) fusion(f32[2,8,152,256]{3,2,1,0:T(8,128)S(1)} %copy-done), kind=kLoop, calls=%fused_computation.91 | loop fusion | bytes 77824 | tf_op jit(solution)/shard_map/slice | solution.py:28
  21.4 1.4 %convert_element_type.3 = f32[8,152,256]{2,1,0:T(8,128)S(1)} convert(s32[8,152,256]{2,1,0:T(8,128)} %param.11) | non-fusion elementwise | flops 311296 | bytes 2490368 | tf_op jit(solution)/shard_map/convert_element_type | solution.py:54
  22.8 1.1 copy-done.2
  23.9 0.2 slice_multiply_fusion.1
  24.1 1.0 copy-done.9
  25.1 1.6 %subtract_multiply_fusion = f32[2,7,152,256]{3,2,1,0:T(8,128)} fusion(f32[2,8,152,256]{3,2,1,0:T(8,128)S(1)} %copy-done, f32[7,152,256]{2,1,0:T(8,128)S(1)} %slice_multiply_fusion.1), kind=kLoop, calls=%fused_computation.64 | loop fusion | flops 1089536 | bytes 7626752 | tf_op jit(solution)/shard_map/mul | solution.py:96
  26.7 0.5 compare_and_fusion
  27.2 1.9 %copy.215 = f32[2,8,152,2]{2,1,3,0:T(8,128)S(1)} copy(f32[2,8,152,2]{3,2,1,0:T(8,128)} %get-tuple-element.21) | data formatting | bytes 38912
  29.1 1.9 %copy.216 = f32[2,8,152,2]{2,1,3,0:T(8,128)S(1)} copy(f32[2,8,152,2]{3,2,1,0:T(8,128)} %get-tuple-element.22) | data formatting | bytes 38912
  31.0 5.3 %collective-permute-start.2 = (f32[2,8,152,2]{2,1,3,0:T(8,128)S(1)}, f32[2,8,152,2]{2,1,3,0:T(8,128)S(1)}, u32[]{:S(2)}, u32[]{:S(2)}) collective-permute-start(f32[2,8,152,2]{2,1,3,0:T(8,128)S(1)} %copy.216), channel_id=1, source_target_pairs={{1,0},{2,1},{3,2},{4,3},{5,4},{6,5},{7,6},{8,7},{9,8},{10,9},{11,1... | collective-permute-start | bytes 58376 | tf_op jit(solution)/shard_map/ppermute | solution.py:30
  36.3 1.5 %copy.201 = f32[2,8,152,1]{3,2,1,0:T(8,128)} copy(f32[2,8,152,1]{2,1,3,0:T(8,128)S(1)} %collective-permute-done) | data formatting | bytes 19456 | tf_op jit(solution)/shard_map/ppermute | solution.py:11
  37.8 3.4 %broadcast_compare_fusion = (pred[8,152,257]{2,1,0:T(8,128)(4,1)S(1)}, f32[8,152,257]{2,1,0:T(8,128)}) fusion(f32[2,8,152,256]{3,2,1,0:T(8,128)} %param.9, f32[2,8,152,1]{3,2,1,0:T(8,128)} %copy.201), kind=kLoop, calls=%fused_computation.82 | loop fusion | flops 625024 | bytes 4062656 | tf_op jit(solution)/shard_map/gt | solution.py:42
  41.2 0.0 copy-start.8
  41.3 1.8 %fusion.39 = f32[8,152,257]{2,1,0:T(8,128)} fusion(f32[2,8,152,256]{3,2,1,0:T(8,128)S(1)} %copy-done.6, f32[2,8,152,1]{3,2,1,0:T(8,128)S(1)} %copy-done.7), kind=kLoop, calls=%fused_computation.68 | loop fusion | flops 312512 | bytes 3750144 | tf_op jit(solution)/shard_map/mul | solution.py:42
  43.1 0.1 collective-permute-start.6
  43.2 0.6 copy-done.8
  43.8 1.3 %broadcast_compare_fusion.1 = (pred[8,153,256]{2,1,0:T(8,128)(4,1)S(1)}, f32[8,153,256]{2,1,0:T(8,128)}) fusion(f32[2,8,152,256]{3,2,1,0:T(8,128)S(1)} %copy-done.8, f32[2,8,1,256]{3,2,1,0:T(1,128)S(1)} %collective-permute-done.3), kind=kLoop, calls=%fused_computation.83 | loop fusion | flops 626688 | bytes 4073472 | tf_op jit(solution)/shard_map/gt | solution.py:42
  45.1 1.7 %collective-permute-done.6 = f32[2,8,2,256]{3,2,1,0:T(2,128)} collective-permute-done((f32[2,8,2,256]{3,2,1,0:T(2,128)}, f32[2,8,2,256]{3,2,1,0:T(2,128)}, u32[]{:S(2)}, u32[]{:S(2)}) %collective-permute-start.6) | collective-permute-done | bytes 32800 | tf_op jit(solution)/shard_map/ppermute | solution.py:36
  46.8 1.9 %collective-permute-start.7 = (f32[2,8,2,256]{3,2,1,0:T(2,128)}, f32[2,8,2,256]{3,2,1,0:T(2,128)}, u32[]{:S(2)}, u32[]{:S(2)}) collective-permute-start(f32[2,8,2,256]{3,2,1,0:T(2,128)} %collective-permute-done.6), channel_id=1, source_target_pairs={{0,4},{1,5},{2,6},{3,7},{4,0},{5,1},{6,2},{7,3},{8,12},{9,13},{10,... | collective-permute-start | bytes 98312 | tf_op jit(solution)/shard_map/ppermute | solution.py:36
  48.7 1.2 fusion.42
  49.9 1.5 %copy.203 = f32[2,8,152,2]{3,2,1,0:T(8,128)} copy(f32[2,8,152,2]{2,1,3,0:T(8,128)S(1)} %collective-permute-done.1) | data formatting | bytes 38912 | tf_op jit(solution)/shard_map/ppermute | solution.py:27
  51.4 1.5 %copy.205 = f32[2,8,152,2]{3,2,1,0:T(8,128)} copy(f32[2,8,152,2]{2,1,3,0:T(8,128)S(1)} %collective-permute-done.2) | data formatting | bytes 38912 | tf_op jit(solution)/shard_map/ppermute | solution.py:30
  52.9 3.3 %collective-permute-start.8 = (f32[2,8,2,256]{3,2,1,0:T(2,128)}, f32[2,8,2,256]{3,2,1,0:T(2,128)S(1)}, u32[]{:S(2)}, u32[]{:S(2)}) collective-permute-start(f32[2,8,2,256]{3,2,1,0:T(2,128)} %collective-permute-done.7), channel_id=1, source_target_pairs={{0,8},{1,9},{2,10},{3,11},{4,12},{5,13},{6,14},{7,15},{8,0},{9,1},... | collective-permute-start | bytes 98312 | tf_op jit(solution)/shard_map/ppermute | solution.py:36
  56.2 7.5 %fusion.11 = f32[2,8,152,257]{3,2,1,0:T(8,128)} fusion(f32[2,8,152,2]{3,2,1,0:T(8,128)} %copy.205, f32[2,8,152,256]{3,2,1,0:T(8,128)S(1)} %copy-done, f32[2,8,152,2]{3,2,1,0:T(8,128)} %copy.203, f32[8,152,257]{2,1,0:T(8,128)} %fusion.39, f32[8,152,257]{2,1,0:T(8,128)} %get-tuple-element.12, pred[8,152,257]{2,1,0:T(8,128)(4,1)S(1)} %get-tuple-element.11), kind=kLoop, calls=%fused_computation.18 | loop fusion | flops 11875456 | bytes 7841984 | tf_op jit(solution)/shard_map/sub | solution.py:42
  63.7 0.1 rev.6
  63.9 0.2 copy.206
  64.1 2.1 %gather_fusion = f32[256,2,8,2]{2,3,1,0:T(2,128)} fusion(f32[2,8,2,256]{1,2,3,0:T(2,128)S(1)} %copy.206, s32[1024]{0:T(1024)S(1)} %pad_clamp_fusion), kind=kCustom, calls=%fused_computation.clone | custom fusion | bytes 66560 | tf_op jit(solution)/shard_map/jit(_take)/gather | solution.py:67
  66.2 1.2 copy.207
  67.5 3.5 %fusion.25 = f32[2,8,153,256]{3,2,1,0:T(8,128)S(1)} fusion(f32[2,8,2,256]{3,2,1,0:T(2,128)S(1)} %bitcast_select_fusion.1, f32[2,8,152,256]{3,2,1,0:T(8,128)S(1)} %copy-done, f32[2,8,2,256]{3,2,1,0:T(2,128)S(1)} %collective-permute-done.4, f32[8,153,256]{2,1,0:T(8,128)} %fusion.42, f32[8,153,256]{2,1,0:T(8,128)} %get-tuple-element.14, ...), kind=kLoop, calls=%fused_computation.42 | loop fusion | flops 11907072 | bytes 7882752 | tf_op jit(solution)/shard_map/sub | solution.py:42
  71.1 4.0 %fusion.35 = f32[2,8,152,256]{3,2,1,0:T(8,128)S(1)} fusion(f32[2,8,152,256]{3,2,1,0:T(8,128)S(1)} %copy-done.1, f32[2,8,153,256]{3,2,1,0:T(8,128)S(1)} %fusion.25, f32[2,8,152,257]{3,2,1,0:T(8,128)} %fusion.11, f32[2,7,152,256]{3,2,1,0:T(8,128)S(1)} %copy-done.10, f32[8,152,256]{2,1,0:T(8,128)S(1)} %copy-done.3), kind=kLoop, calls=%fused_computation.60 | loop fusion | flops 4358144 | bytes 18366464 | tf_op jit(solution)/shard_map/add | solution.py:102
  75.1 0.6 fusion.50
  75.7 1.3 %collective-permute-start.13 = (f32[2,8,2,256]{3,2,1,0:T(2,128)S(1)}, f32[2,8,2,256]{3,2,1,0:T(2,128)S(1)}, u32[]{:S(2)}, u32[]{:S(2)}) collective-permute-start(f32[2,8,2,256]{3,2,1,0:T(2,128)S(1)} %get-tuple-element.19), channel_id=1, source_target_pairs={{0,1},{1,0},{2,3},{3,2},{4,5},{5,4},{6,7},{7,6},{8,9},{9,8},{10,11... | collective-permute-start | bytes 98312 | tf_op jit(solution)/shard_map/ppermute | solution.py:36
  77.1 7.5 %collective-permute-start.12 = (f32[2,8,2,256]{3,2,1,0:T(2,128)S(1)}, f32[2,8,2,256]{3,2,1,0:T(2,128)S(1)}, u32[]{:S(2)}, u32[]{:S(2)}) collective-permute-start(f32[2,8,2,256]{3,2,1,0:T(2,128)S(1)} %get-tuple-element.19), channel_id=1, source_target_pairs={{0,16},{16,32},{32,48},{48,64},{64,80},{80,96},{96,112},{112,128},... | collective-permute-start | bytes 98312 | tf_op jit(solution)/shard_map/ppermute | solution.py:27
  84.6 0.4 collective-permute-start.14
  85.0 1.8 %fusion.49 = (f32[2,8,152,2]{3,2,1,0:T(8,128)}, f32[2,8,152,2]{3,2,1,0:T(8,128)}) fusion(f32[2,8,152,256]{3,2,1,0:T(8,128)S(1)} %fusion.35), kind=kLoop, calls=%fused_computation.89 | loop fusion | bytes 77824 | tf_op jit(solution)/shard_map/slice | solution.py:28
  86.8 1.9 %copy.208 = f32[2,8,152,2]{2,1,3,0:T(8,128)S(1)} copy(f32[2,8,152,2]{3,2,1,0:T(8,128)} %get-tuple-element.17) | data formatting | bytes 38912 | tf_op jit(solution)/shard_map/slice | solution.py:28
  88.7 1.9 %copy.210 = f32[2,8,152,2]{2,1,3,0:T(8,128)S(1)} copy(f32[2,8,152,2]{3,2,1,0:T(8,128)} %get-tuple-element.18) | data formatting | bytes 38912 | tf_op jit(solution)/shard_map/slice | solution.py:30
  90.6 1.1 collective-permute-start.11
  91.7 0.4 collective-permute-start.10
  92.1 1.6 %collective-permute-start.15 = (f32[2,8,2,256]{3,2,1,0:T(2,128)}, f32[2,8,2,256]{3,2,1,0:T(2,128)}, u32[]{:S(2)}, u32[]{:S(2)}) collective-permute-start(f32[2,8,2,256]{3,2,1,0:T(2,128)} %collective-permute-done.14), channel_id=1, source_target_pairs={{0,4},{1,5},{2,6},{3,7},{4,0},{5,1},{6,2},{7,3},{8,12},{9,13},{10,... | collective-permute-start | bytes 98312 | tf_op jit(solution)/shard_map/ppermute | solution.py:36
  93.7 2.9 %fusion.36 = f32[2,7,152,256]{3,2,1,0:T(8,128)} fusion(f32[2,8,152,256]{3,2,1,0:T(8,128)S(1)} %fusion.35, f32[7,152,256]{2,1,0:T(8,128)} %copy-done.9), kind=kLoop, calls=%fused_computation.63 | loop fusion | flops 1089536 | bytes 7626752 | tf_op jit(solution)/shard_map/mul | solution.py:96
  96.6 2.0 %collective-permute-start.17 = (f32[2,8,2,256]{3,2,1,0:T(2,128)}, f32[2,8,2,256]{3,2,1,0:T(2,128)S(1)}, u32[]{:S(2)}, u32[]{:S(2)}) collective-permute-start(f32[2,8,2,256]{3,2,1,0:T(2,128)} %get-tuple-element.20), channel_id=1, source_target_pairs={{16,0},{32,16},{48,32},{64,48},{80,64},{96,80},{112,96},{128,112},... | collective-permute-start | bytes 98312 | tf_op jit(solution)/shard_map/ppermute | solution.py:30
  98.7 1.5 %copy.209 = f32[2,8,152,2]{3,2,1,0:T(8,128)} copy(f32[2,8,152,2]{2,1,3,0:T(8,128)S(1)} %collective-permute-done.10) | data formatting | bytes 38912 | tf_op jit(solution)/shard_map/ppermute | solution.py:27
  100.2 1.5 %copy.211 = f32[2,8,152,2]{3,2,1,0:T(8,128)} copy(f32[2,8,152,2]{2,1,3,0:T(8,128)S(1)} %collective-permute-done.11) | data formatting | bytes 38912 | tf_op jit(solution)/shard_map/ppermute | solution.py:30
  101.7 3.9 %collective-permute-start.16 = (f32[2,8,2,256]{3,2,1,0:T(2,128)}, f32[2,8,2,256]{3,2,1,0:T(2,128)S(1)}, u32[]{:S(2)}, u32[]{:S(2)}) collective-permute-start(f32[2,8,2,256]{3,2,1,0:T(2,128)} %collective-permute-done.15), channel_id=1, source_target_pairs={{0,8},{1,9},{2,10},{3,11},{4,12},{5,13},{6,14},{7,15},{8,0},{9,1},... | collective-permute-start | bytes 98312 | tf_op jit(solution)/shard_map/ppermute | solution.py:36
  105.6 7.5 %fusion.4 = f32[2,8,152,257]{3,2,1,0:T(8,128)} fusion(f32[2,8,152,2]{3,2,1,0:T(8,128)} %copy.211, f32[2,8,152,256]{3,2,1,0:T(8,128)S(1)} %fusion.35, f32[2,8,152,2]{3,2,1,0:T(8,128)} %copy.209, f32[8,152,257]{2,1,0:T(8,128)} %fusion.39, f32[8,152,257]{2,1,0:T(8,128)} %get-tuple-element.12, pred[8,152,257]{2,1,0:T(8,128)(4,1)S(1)} %copy-done.13), kind=kLoop, calls=%fused_computation.7 | loop fusion | flops 11875456 | bytes 7841984 | tf_op jit(solution)/shard_map/sub | solution.py:42
  113.0 0.1 rev.7
  113.2 0.2 copy.212
  113.4 2.1 %gather_fusion.1 = f32[256,2,8,2]{2,3,1,0:T(2,128)} fusion(f32[2,8,2,256]{1,2,3,0:T(2,128)S(1)} %copy.212, s32[1024]{0:T(1024)S(1)} %pad_clamp_fusion), kind=kCustom, calls=%fused_computation.1.clone | custom fusion | bytes 66560 | tf_op jit(solution)/shard_map/jit(_take)/gather | solution.py:67
  115.5 1.2 copy.213
  116.8 3.5 %fusion.18 = f32[2,8,153,256]{3,2,1,0:T(8,128)S(1)} fusion(f32[2,8,2,256]{3,2,1,0:T(2,128)S(1)} %bitcast_select_fusion, f32[2,8,152,256]{3,2,1,0:T(8,128)S(1)} %fusion.35, f32[2,8,2,256]{3,2,1,0:T(2,128)S(1)} %collective-permute-done.12, f32[8,153,256]{2,1,0:T(8,128)} %fusion.42, f32[8,153,256]{2,1,0:T(8,128)} %get-tuple-element.14, ...), kind=kLoop, calls=%fused_computation.31 | loop fusion | flops 11907072 | bytes 7882752 | tf_op jit(solution)/shard_map/sub | solution.py:42
  120.4 5.1 %fusion.31 = f32[2,8,152,256]{3,2,1,0:T(8,128)} fusion(f32[2,8,152,256]{3,2,1,0:T(8,128)S(1)} %fusion.35, f32[2,8,153,256]{3,2,1,0:T(8,128)S(1)} %fusion.18, f32[2,8,152,257]{3,2,1,0:T(8,128)S(1)} %copy-done.5, f32[2,7,152,256]{3,2,1,0:T(8,128)} %fusion.36, f32[8,152,256]{2,1,0:T(8,128)S(1)} %copy-done.4), kind=kLoop, calls=%fused_computation.54 | loop fusion | flops 4358144 | bytes 18366464 | tf_op jit(solution)/shard_map/add | solution.py:102
  125.5 3.0 %fusion.44 = f32[8,152,256]{2,1,0:T(8,128)} fusion(f32[2,8,152,256]{3,2,1,0:T(8,128)} %fusion.31, s32[8,152,256]{2,1,0:T(8,128)S(1)} %copy-done.11), kind=kLoop, calls=%fused_computation.75 | loop fusion | flops 2490368 | bytes 4980736 | tf_op jit(solution)/shard_map/mul | solution.py:105
  (51 shorter events, 0.2 us)
Async XLA Ops:
  0.6 19.0 %copy-start = (f32[2,8,152,256]{3,2,1,0:T(8,128)S(1)}, f32[2,8,152,256]{3,2,1,0:T(8,128)}, u32[]{:S(2)}) copy-start(f32[2,8,152,256]{3,2,1,0:T(8,128)} %param.8) | copy-start | bytes 7471108
  2.4 40.7 %collective-permute-start.5 = (f32[2,8,2,256]{3,2,1,0:T(2,128)S(1)}, f32[2,8,2,256]{3,2,1,0:T(2,128)}, u32[]{:S(2)}, u32[]{:S(2)}) collective-permute-start(f32[2,8,2,256]{3,2,1,0:T(2,128)S(1)} %get-tuple-element.23), channel_id=1, source_target_pairs={{0,1},{1,0},{2,3},{3,2},{4,5},{5,4},{6,7},{7,6},{8,9},{9,8},{10,11... | collective-permute-start | bytes 98312 | tf_op jit(solution)/shard_map/ppermute | solution.py:36
  4.4 63.1 %collective-permute-start.4 = (f32[2,8,2,256]{3,2,1,0:T(2,128)S(1)}, f32[2,8,2,256]{3,2,1,0:T(2,128)S(1)}, u32[]{:S(2)}, u32[]{:S(2)}) collective-permute-start(f32[2,8,2,256]{3,2,1,0:T(2,128)S(1)} %get-tuple-element.23), channel_id=1, source_target_pairs={{0,16},{16,32},{32,48},{48,64},{64,80},{80,96},{96,112},{112,128},... | collective-permute-start | bytes 98312 | tf_op jit(solution)/shard_map/ppermute | solution.py:27
  10.6 32.5 %collective-permute-start.3 = (f32[2,8,1,256]{3,2,1,0:T(1,128)S(1)}, f32[2,8,1,256]{3,2,1,0:T(1,128)S(1)}, u32[]{:S(2)}, u32[]{:S(2)}) collective-permute-start(f32[2,8,1,256]{3,2,1,0:T(1,128)S(1)} %slice.167), channel_id=1, source_target_pairs={{0,16},{16,32},{32,48},{48,64},{64,80},{80,96},{96,112},{112,128},... | collective-permute-start | bytes 49160 | tf_op jit(solution)/shard_map/ppermute | solution.py:17
  12.5 55.0 %collective-permute-start.9 = (f32[2,8,2,256]{3,2,1,0:T(2,128)}, f32[2,8,2,256]{3,2,1,0:T(2,128)S(1)}, u32[]{:S(2)}, u32[]{:S(2)}) collective-permute-start(f32[2,8,2,256]{3,2,1,0:T(2,128)} %get-tuple-element.24), channel_id=1, source_target_pairs={{16,0},{32,16},{48,32},{64,48},{80,64},{96,80},{112,96},{128,112},... | collective-permute-start | bytes 98312 | tf_op jit(solution)/shard_map/ppermute | solution.py:30
  19.5 11.5 %collective-permute-start = (f32[2,8,152,1]{2,1,3,0:T(8,128)S(1)}, f32[2,8,152,1]{2,1,3,0:T(8,128)S(1)}, u32[]{:S(2)}, u32[]{:S(2)}) collective-permute-start(f32[2,8,152,1]{2,1,3,0:T(8,128)S(1)} %copy.214), channel_id=1, source_target_pairs={{0,1},{1,2},{2,3},{3,4},{4,5},{5,6},{6,7},{7,8},{8,9},{9,10},{10,1... | collective-permute-start | bytes 29192 | tf_op jit(solution)/shard_map/ppermute | solution.py:11
  19.6 4.3 %copy-start.17 = (f32[7]{0:T(128)S(1)}, f32[7]{0:T(128)}, u32[]{:S(2)}) copy-start(f32[7]{0:T(128)} %param.13) | copy-start | bytes 88
  22.8 1.1 copy-start.2
  24.1 1.0 copy-start.9
  25.1 1.6 %copy-start.16 = (s32[256]{0:T(256)S(1)}, s32[256]{0:T(256)}, u32[]{:S(2)}) copy-start(s32[256]{0:T(256)} %param.12) | copy-start | bytes 3076
  31.0 20.4 %collective-permute-start.2 = (f32[2,8,152,2]{2,1,3,0:T(8,128)S(1)}, f32[2,8,152,2]{2,1,3,0:T(8,128)S(1)}, u32[]{:S(2)}, u32[]{:S(2)}) collective-permute-start(f32[2,8,152,2]{2,1,3,0:T(8,128)S(1)} %copy.216), channel_id=1, source_target_pairs={{1,0},{2,1},{3,2},{4,3},{5,4},{6,5},{7,6},{8,7},{9,8},{10,9},{11,1... | collective-permute-start | bytes 58376 | tf_op jit(solution)/shard_map/ppermute | solution.py:30
  37.8 3.4 %copy-start.6 = (f32[2,8,152,256]{3,2,1,0:T(8,128)S(1)}, f32[2,8,152,256]{3,2,1,0:T(8,128)}, u32[]{:S(2)}) copy-start(f32[2,8,152,256]{3,2,1,0:T(8,128)} %param.9) | copy-start | bytes 7471108
  37.8 3.4 %copy-start.7 = (f32[2,8,152,1]{3,2,1,0:T(8,128)S(1)}, f32[2,8,152,1]{3,2,1,0:T(8,128)}, u32[]{:S(2)}) copy-start(f32[2,8,152,1]{3,2,1,0:T(8,128)} %copy.201) | copy-start | bytes 29188
  41.2 15.0 %copy-start.12 = (pred[8,152,257]{2,1,0:T(8,128)(4,1)}, pred[8,152,257]{2,1,0:T(8,128)(4,1)S(1)}, u32[]{:S(2)}) copy-start(pred[8,152,257]{2,1,0:T(8,128)(4,1)S(1)} %get-tuple-element.11) | copy-start | bytes 937540
  41.2 2.6 %copy-start.8 = (f32[2,8,152,256]{3,2,1,0:T(8,128)S(1)}, f32[2,8,152,256]{3,2,1,0:T(8,128)}, u32[]{:S(2)}) copy-start(f32[2,8,152,256]{3,2,1,0:T(8,128)} %param.10) | copy-start | bytes 7471108
  43.1 6.8 %collective-permute-start.1 = (f32[2,8,152,2]{2,1,3,0:T(8,128)S(1)}, f32[2,8,152,2]{2,1,3,0:T(8,128)S(1)}, u32[]{:S(2)}, u32[]{:S(2)}) collective-permute-start(f32[2,8,152,2]{2,1,3,0:T(8,128)S(1)} %copy.215), channel_id=1, source_target_pairs={{0,1},{1,2},{2,3},{3,4},{4,5},{5,6},{6,7},{7,8},{8,9},{9,10},{10,1... | collective-permute-start | bytes 58376 | tf_op jit(solution)/shard_map/ppermute | solution.py:27
  43.1 3.7 %collective-permute-start.6 = (f32[2,8,2,256]{3,2,1,0:T(2,128)}, f32[2,8,2,256]{3,2,1,0:T(2,128)}, u32[]{:S(2)}, u32[]{:S(2)}) collective-permute-start(f32[2,8,2,256]{3,2,1,0:T(2,128)} %collective-permute-done.5), channel_id=1, source_target_pairs={{0,2},{1,3},{2,0},{3,1},{4,6},{5,7},{6,4},{7,5},{8,10},{9,11},{10,... | collective-permute-start | bytes 98312 | tf_op jit(solution)/shard_map/ppermute | solution.py:36
  46.8 6.1 %collective-permute-start.7 = (f32[2,8,2,256]{3,2,1,0:T(2,128)}, f32[2,8,2,256]{3,2,1,0:T(2,128)}, u32[]{:S(2)}, u32[]{:S(2)}) collective-permute-start(f32[2,8,2,256]{3,2,1,0:T(2,128)} %collective-permute-done.6), channel_id=1, source_target_pairs={{0,4},{1,5},{2,6},{3,7},{4,0},{5,1},{6,2},{7,3},{8,12},{9,13},{10,... | collective-permute-start | bytes 98312 | tf_op jit(solution)/shard_map/ppermute | solution.py:36
  52.9 10.8 %collective-permute-start.8 = (f32[2,8,2,256]{3,2,1,0:T(2,128)}, f32[2,8,2,256]{3,2,1,0:T(2,128)S(1)}, u32[]{:S(2)}, u32[]{:S(2)}) collective-permute-start(f32[2,8,2,256]{3,2,1,0:T(2,128)} %collective-permute-done.7), channel_id=1, source_target_pairs={{0,8},{1,9},{2,10},{3,11},{4,12},{5,13},{6,14},{7,15},{8,0},{9,1},... | collective-permute-start | bytes 98312 | tf_op jit(solution)/shard_map/ppermute | solution.py:36
  56.2 11.2 %copy-start.14 = (pred[256]{0:T(512)(128)(4,1)S(1)}, pred[256]{0:T(512)(128)(4,1)}, u32[]{:S(2)}) copy-start(pred[256]{0:T(512)(128)(4,1)} %get-tuple-element.15) | copy-start | bytes 772
  67.5 3.6 %copy-start.1 = (f32[2,8,152,256]{3,2,1,0:T(8,128)S(1)}, f32[2,8,152,256]{3,2,1,0:T(8,128)}, u32[]{:S(2)}) copy-start(f32[2,8,152,256]{3,2,1,0:T(8,128)} %param.8) | copy-start | bytes 7471108
  67.5 3.6 %copy-start.3 = (f32[8,152,256]{2,1,0:T(8,128)S(1)}, f32[8,152,256]{2,1,0:T(8,128)}, u32[]{:S(2)}) copy-start(f32[8,152,256]{2,1,0:T(8,128)} %copy-done.2) | copy-start | bytes 3735556
  67.5 3.6 %copy-start.10 = (f32[2,7,152,256]{3,2,1,0:T(8,128)S(1)}, f32[2,7,152,256]{3,2,1,0:T(8,128)}, u32[]{:S(2)}) copy-start(f32[2,7,152,256]{3,2,1,0:T(8,128)} %subtract_multiply_fusion) | copy-start | bytes 6537220
  75.7 8.8 %collective-permute-start.13 = (f32[2,8,2,256]{3,2,1,0:T(2,128)S(1)}, f32[2,8,2,256]{3,2,1,0:T(2,128)S(1)}, u32[]{:S(2)}, u32[]{:S(2)}) collective-permute-start(f32[2,8,2,256]{3,2,1,0:T(2,128)S(1)} %get-tuple-element.19), channel_id=1, source_target_pairs={{0,1},{1,0},{2,3},{3,2},{4,5},{5,4},{6,7},{7,6},{8,9},{9,8},{10,11... | collective-permute-start | bytes 98312 | tf_op jit(solution)/shard_map/ppermute | solution.py:36
  77.1 39.8 %collective-permute-start.12 = (f32[2,8,2,256]{3,2,1,0:T(2,128)S(1)}, f32[2,8,2,256]{3,2,1,0:T(2,128)S(1)}, u32[]{:S(2)}, u32[]{:S(2)}) collective-permute-start(f32[2,8,2,256]{3,2,1,0:T(2,128)S(1)} %get-tuple-element.19), channel_id=1, source_target_pairs={{0,16},{16,32},{32,48},{48,64},{64,80},{80,96},{96,112},{112,128},... | collective-permute-start | bytes 98312 | tf_op jit(solution)/shard_map/ppermute | solution.py:27
  84.6 7.6 %collective-permute-start.14 = (f32[2,8,2,256]{3,2,1,0:T(2,128)S(1)}, f32[2,8,2,256]{3,2,1,0:T(2,128)}, u32[]{:S(2)}, u32[]{:S(2)}) collective-permute-start(f32[2,8,2,256]{3,2,1,0:T(2,128)S(1)} %collective-permute-done.13), channel_id=1, source_target_pairs={{0,2},{1,3},{2,0},{3,1},{4,6},{5,7},{6,4},{7,5},{8,10},{9,11},{10,... | collective-permute-start | bytes 98312 | tf_op jit(solution)/shard_map/ppermute | solution.py:36
  90.6 9.5 %collective-permute-start.11 = (f32[2,8,152,2]{2,1,3,0:T(8,128)S(1)}, f32[2,8,152,2]{2,1,3,0:T(8,128)S(1)}, u32[]{:S(2)}, u32[]{:S(2)}) collective-permute-start(f32[2,8,152,2]{2,1,3,0:T(8,128)S(1)} %copy.210), channel_id=1, source_target_pairs={{1,0},{2,1},{3,2},{4,3},{5,4},{6,5},{7,6},{8,7},{9,8},{10,9},{11,1... | collective-permute-start | bytes 58376 | tf_op jit(solution)/shard_map/ppermute | solution.py:30
  91.7 6.9 %collective-permute-start.10 = (f32[2,8,152,2]{2,1,3,0:T(8,128)S(1)}, f32[2,8,152,2]{2,1,3,0:T(8,128)S(1)}, u32[]{:S(2)}, u32[]{:S(2)}) collective-permute-start(f32[2,8,152,2]{2,1,3,0:T(8,128)S(1)} %copy.208), channel_id=1, source_target_pairs={{0,1},{1,2},{2,3},{3,4},{4,5},{5,6},{6,7},{7,8},{8,9},{9,10},{10,1... | collective-permute-start | bytes 58376 | tf_op jit(solution)/shard_map/ppermute | solution.py:27
  92.1 9.5 %collective-permute-start.15 = (f32[2,8,2,256]{3,2,1,0:T(2,128)}, f32[2,8,2,256]{3,2,1,0:T(2,128)}, u32[]{:S(2)}, u32[]{:S(2)}) collective-permute-start(f32[2,8,2,256]{3,2,1,0:T(2,128)} %collective-permute-done.14), channel_id=1, source_target_pairs={{0,4},{1,5},{2,6},{3,7},{4,0},{5,1},{6,2},{7,3},{8,12},{9,13},{10,... | collective-permute-start | bytes 98312 | tf_op jit(solution)/shard_map/ppermute | solution.py:36
  96.6 9.0 %copy-start.13 = (pred[8,152,257]{2,1,0:T(8,128)(4,1)S(1)}, pred[8,152,257]{2,1,0:T(8,128)(4,1)}, u32[]{:S(2)}) copy-start(pred[8,152,257]{2,1,0:T(8,128)(4,1)} %copy-done.12) | copy-start | bytes 937540
  96.6 20.2 %collective-permute-start.17 = (f32[2,8,2,256]{3,2,1,0:T(2,128)}, f32[2,8,2,256]{3,2,1,0:T(2,128)S(1)}, u32[]{:S(2)}, u32[]{:S(2)}) collective-permute-start(f32[2,8,2,256]{3,2,1,0:T(2,128)} %get-tuple-element.20), channel_id=1, source_target_pairs={{16,0},{32,16},{48,32},{64,48},{80,64},{96,80},{112,96},{128,112},... | collective-permute-start | bytes 98312 | tf_op jit(solution)/shard_map/ppermute | solution.py:30
  101.7 15.1 %copy-start.15 = (pred[256]{0:T(512)(128)(4,1)S(1)}, pred[256]{0:T(512)(128)(4,1)}, u32[]{:S(2)}) copy-start(pred[256]{0:T(512)(128)(4,1)} %get-tuple-element.15) | copy-start | bytes 772
  101.7 11.4 %collective-permute-start.16 = (f32[2,8,2,256]{3,2,1,0:T(2,128)}, f32[2,8,2,256]{3,2,1,0:T(2,128)S(1)}, u32[]{:S(2)}, u32[]{:S(2)}) collective-permute-start(f32[2,8,2,256]{3,2,1,0:T(2,128)} %collective-permute-done.15), channel_id=1, source_target_pairs={{0,8},{1,9},{2,10},{3,11},{4,12},{5,13},{6,14},{7,15},{8,0},{9,1},... | collective-permute-start | bytes 98312 | tf_op jit(solution)/shard_map/ppermute | solution.py:36
  116.8 3.6 %copy-start.4 = (f32[8,152,256]{2,1,0:T(8,128)S(1)}, f32[8,152,256]{2,1,0:T(8,128)}, u32[]{:S(2)}) copy-start(f32[8,152,256]{2,1,0:T(8,128)} %copy-done.2) | copy-start | bytes 3735556
  116.8 3.6 %copy-start.5 = (f32[2,8,152,257]{3,2,1,0:T(8,128)S(1)}, f32[2,8,152,257]{3,2,1,0:T(8,128)}, u32[]{:S(2)}) copy-start(f32[2,8,152,257]{3,2,1,0:T(8,128)} %fusion.4) | copy-start | bytes 7500292
  120.4 5.1 %copy-start.11 = (s32[8,152,256]{2,1,0:T(8,128)S(1)}, s32[8,152,256]{2,1,0:T(8,128)}, u32[]{:S(2)}) copy-start(s32[8,152,256]{2,1,0:T(8,128)} %param.11) | copy-start | bytes 3735556
where the time goes:
time: 131 us; the launch traced here: 128 us
  other arithmetic  48.5 us (37%)
  starting transfers between devices  40.4 us (31%)
  local copies, waits for them, and re-layouts  36.8 us (28%)
  waiting for transfers between devices  1.72 us (1%)
    sub x4, other arithmetic, quick_flux(): flow_number * jnp.where(flow_number > 0.0, upwind, downwind)  22 us
    ppermute x8, starting transfers between devices, partner(): lax.ppermute(x, axis, [(i, i ^ 1 << apart) for i in range(lax.axis_size(a...  14.5 us
    ppermute x4, starting transfers between devices, extended(): lax.ppermute(lax.slice_in_dim(block, block.shape[dim] - width, None, axis...  13.1 us
    ppermute x4, starting transfers between devices, extended(): lax.ppermute(lax.slice_in_dim(block, 0, width, axis=dim), axis, backward)  10.9 us
    add x2, other arithmetic, on_device(): fields = fields + wet_cells * change  9.05 us
    unnamed x39, local copies, waits for them, and re-layouts  8.43 us
    slice x5, local copies, waits for them, and re-layouts, extended(): lax.slice_in_dim(block, block.shape[dim] - width, None, axis=dim)  7.96 us
    gather x4, local copies, waits for them, and re-layouts, on_device(): fold_ghost = jnp.take(mirror_rows[:, :, ::-1, :], local_index, axis=3)  6.6 us
  transfers between devices with their start and end apart: 18, of which 1 were waited for; matrix products, arithmetic and copies ran while one was open for 48% of the time, Pallas kernels for 0%

commit v1 on v0

v1 whole, which is shorter than its diff:
```python
import jax
import jax.numpy as jnp
from jax import lax
from jax.experimental import pallas as pl
from jax.experimental.pallas import tpu as pltpu
from jax.sharding import PartitionSpec as P

F32 = jnp.float32
LANES = 128
SUB = 8
PAD = 8
TRACERS = 2
VMEM_BYTES = 48 * 1024 * 1024


def lane_ids():
    return lax.broadcasted_iota(jnp.int32, (SUB, LANES), 1)


def rolled(x, by):
    by = by % LANES
    return x if by == 0 else pltpu.roll(x, by, 1)


def face_terms(flow, spread):
    g = 0.125 * flow
    up = flow > 0.0
    g3 = 3.0 * g
    g6 = 6.0 * g
    return jnp.where(up, g6, g3) + spread, jnp.where(up, g3, g6) - spread, g, up


def tile_rows(index, offset=0):
    return pl.ds(pl.multiple_of(index * SUB, SUB) + offset, SUB)


def advance_tile(r, c, south, east, north, mask, mix, out, out_pad):
    levels = mask.shape[0]
    lane = lane_ids()
    first, last, last2 = lane > 0, lane < LANES - 1, lane < LANES - 2
    rows = tile_rows(r)
    wet = [mask[0, h, rows, :].astype(F32) for h in range(2)]
    below = [[None] * 2 for _ in range(TRACERS)]
    here = [[c[t, 0, h, tile_rows(r, PAD), :] for h in range(2)] for t in range(TRACERS)]
    for k in range(levels):
        if k + 1 < levels:
            wet_up = [mask[k + 1, h, rows, :].astype(F32) for h in range(2)]
            mixing = [mix[k] * wet[h] * wet_up[h] for h in range(2)]
            above = [[c[t, k + 1, h, tile_rows(r, PAD), :] for h in range(2)] for t in range(TRACERS)]
        east_terms = [face_terms(east[0, k, h, rows, :], east[1, k, h, rows, :]) for h in range(2)]
        north_terms = [face_terms(north[0, k, h, rows, :], north[1, k, h, rows, :]) for h in range(2)]
        for t in range(TRACERS):
            c0 = here[t][0], here[t][1]
            plus1 = [rolled(x, -1) for x in c0]
            plus2 = [rolled(x, -2) for x in c0]
            minus1 = [rolled(x, 1) for x in c0]
            p1 = jnp.where(last, plus1[0], plus1[1]), jnp.where(last, plus1[1], 0.0)
            p2 = jnp.where(last2, plus2[0], plus2[1]), jnp.where(last2, plus2[1], 0.0)
            m1 = jnp.where(first, minus1[0], 0.0), jnp.where(first, minus1[1], minus1[0])
            flux = []
            for h in range(2):
                a, b, g, up = east_terms[h]
                flux.append(a * c0[h] + b * p1[h] - g * jnp.where(up, m1[h], p2[h]))
            shifted = [rolled(x, 1) for x in flux]
            west = jnp.where(first, shifted[0], 0.0), jnp.where(first, shifted[1], shifted[0])
            for h in range(2):
                change = west[h] - flux[h]
                a, b, g, up = north_terms[h]
                further = jnp.where(
                    up,
                    c[t, k, h, tile_rows(r, PAD - 1), :],
                    c[t, k, h, tile_rows(r, PAD + 2), :],
                )
                face = a * c0[h] + b * c[t, k, h, tile_rows(r, PAD + 1), :] - g * further
                south[t, k, h, tile_rows(r, PAD), :] = face
                change = change + (south[t, k, h, tile_rows(r, PAD - 1), :] - face)
                if k + 1 < levels:
                    vertical = mixing[h] * (above[t][h] - c0[h])
                    change = change + vertical
                if k > 0:
                    change = change - below[t][h]
                if k + 1 < levels:
                    below[t][h] = vertical
                out[t, k, h, tile_rows(r, out_pad), :] = c0[h] + wet[h] * change
        if k + 1 < levels:
            wet = wet_up
            here = above


def slot_group(slot_lane, tl):
    return lax.shift_right_logical(slot_lane, 3) == tl


def packed_edges(get, levels):
    lane = lane_ids()
    west = jnp.zeros((SUB, LANES), F32)
    east = jnp.zeros((SUB, LANES), F32)
    for t in range(TRACERS):
        for k in range(levels):
            tl = t * levels + k
            inside = slot_group(lane, tl)
            west = jnp.where(inside, rolled(get(t, k, 0), 8 * tl), west)
            east = jnp.where(inside, rolled(get(t, k, 1), 8 * tl + 2), east)
    return west, east


def parity(axis):
    return lax.rem(lax.axis_index(axis), 2) == 0


def start_kernel(tracers, east, north, c, side_a, side_b, rows_a, rows_b, east_last, north_top, sems):
    levels, tall = tracers.shape[1], tracers.shape[2]
    tiles = tall // SUB
    cuts = [0, 40, 80, 120, tall]
    copies = []
    for i, (lo, hi) in enumerate(zip(cuts[:-1], cuts[1:])):
        group = []
        for h in range(2):
            group.append(
                pltpu.make_async_copy(
                    tracers.at[:, :, lo:hi, h * LANES : (h + 1) * LANES],
                    c.at[:, :, h, PAD + lo : PAD + hi, :],
                    sems.at[3 * i + h],
                )
            )
        group.append(
            pltpu.make_async_copy(
                east.at[:, :, lo:hi, LANES:], east_last.at[:, :, lo:hi, :], sems.at[3 * i + 2]
            )
        )
        copies.append(group)
    top_copy = pltpu.make_async_copy(north.at[:, :, tall - SUB :, :], north_top, sems.at[12])
    for group in copies:
        for one in group:
            one.start()
    top_copy.start()
    for t in range(TRACERS):
        for k in range(levels):
            for h in range(2):
                c[t, k, h, 0:PAD, :] = jnp.zeros((PAD, LANES), F32)
                c[t, k, h, PAD + tall :, :] = jnp.zeros((PAD, LANES), F32)
    lane = lane_ids()
    even_lon = parity("lon")

    def pack(r, carry):
        rows = tile_rows(r)
        faces = []
        for k in range(levels):
            flow = rolled(east_last[0, k, rows, :], 1)
            spread = rolled(east_last[1, k, rows, :], 2)
            faces.append(jnp.where(lane == 0, flow, spread))

        def get(t, k, h):
            x = c[t, k, h, tile_rows(r, PAD), :]
            return jnp.where(lane >= LANES - 2, x, faces[k]) if h == 1 else x

        west, east_side = packed_edges(get, levels)
        side_a[rows, :] = jnp.where(even_lon, east_side, west)
        side_b[rows, :] = jnp.where(even_lon, west, east_side)
        return carry

    for i, (lo, hi) in enumerate(zip(cuts[:-1], cuts[1:])):
        for one in copies[i]:
            one.wait()
        lax.fori_loop(lo // SUB, hi // SUB, pack, 0)
    top_copy.wait()
    send_rows(c, rows_a, rows_b, levels, tall)
    for comp in range(2):
        for k in range(levels):
            one_row = north_top[comp, k, SUB - 1 : SUB, :]
            at = 2 * TRACERS * levels + comp * levels + k
            rows_a[at : at + 1, :] = one_row
            rows_b[at : at + 1, :] = one_row


def send_rows(c, rows_a, rows_b, levels, tall):
    even_lat = parity("lat")
    for depth in range(2):
        top, bottom = PAD + tall - 1 - depth, PAD + depth
        at_a = jnp.where(even_lat, top, bottom)
        at_b = jnp.where(even_lat, bottom, top)
        for t in range(TRACERS):
            for k in range(levels):
                tl = (depth * TRACERS + t) * levels + k
                for h in range(2):
                    cols = slice(h * LANES, (h + 1) * LANES)
                    rows_a[tl : tl + 1, cols] = c[t, k, h, pl.ds(at_a, 1), :]
                    rows_b[tl : tl + 1, cols] = c[t, k, h, pl.ds(at_b, 1), :]


def inner_kernel(c, east, north, mask, mix, out, packed, own, row_own, east_in, north_in, mask_in, south, sems):
    levels, tall = mask.shape[0], mask.shape[1]
    cuts = [0, 24, 64, 104, tall]
    copies = []
    for i, (lo, hi) in enumerate(zip(cuts[:-1], cuts[1:])):
        group = []
        for h in range(2):
            cols = slice(h * LANES, (h + 1) * LANES)
            for j, (src, dst) in enumerate(((east, east_in), (north, north_in))):
                group.append(
                    pltpu.make_async_copy(
                        src.at[:, :, lo:hi, cols], dst.at[:, :, h, lo:hi, :], sems.at[6 * i + 3 * h + j]
                    )
                )
            group.append(
                pltpu.make_async_copy(
                    mask.at[:, lo:hi, cols], mask_in.at[:, h, lo:hi, :], sems.at[6 * i + 3 * h + 2]
                )
            )
        copies.append(group)
    for group in copies:
        for one in group:
            one.start()
    for t in range(TRACERS):
        for k in range(levels):
            for h in range(2):
                south[t, k, h, 0:PAD, :] = jnp.zeros((PAD, LANES), F32)
                out[t, k, h, 0:PAD, :] = jnp.zeros((PAD, LANES), F32)
                out[t, k, h, PAD + tall :, :] = jnp.zeros((PAD, LANES), F32)
    lane = lane_ids()

    def body(r, carry):
        rows = tile_rows(r)
        advance_tile(r, c, south, east_in, north_in, mask_in, mix, out, PAD)
        west, last = packed_edges(lambda t, k, h: out[t, k, h, tile_rows(r, PAD), :], levels)
        packed[0, rows, :] = west
        packed[1, rows, :] = last
        kept = jnp.zeros((SUB, LANES), F32)
        for k in range(levels):
            wet0 = mask_in[k, 0, rows, :].astype(F32)
            wet1 = mask_in[k, 1, rows, :].astype(F32)
            flow1 = east_in[0, k, 1, rows, :]
            one = jnp.where(lane == 0, east_in[0, k, 0, rows, :], rolled(wet0, 1))
            one = jnp.where(lane >= 3, rolled(flow1, 5), one)
            one = jnp.where(lane >= 5, rolled(east_in[1, k, 1, rows, :], 6), one)
            one = jnp.where(lane >= 6, rolled(wet1, 8), one)
            for t in range(TRACERS):
                tl = t * levels + k
                kept = jnp.where(slot_group(lane, tl), rolled(one, 8 * tl), kept)
        own[rows, :] = kept
        return carry

    for i, (lo, hi) in enumerate(zip(cuts[:-1], cuts[1:])):
        for one in copies[i]:
            one.wait()
        lax.fori_loop(lo // SUB, hi // SUB, body, 0)
    for k in range(levels):
        for h in range(2):
            cols = slice(h * LANES, (h + 1) * LANES)
            kept_rows = (
                north_in[0, k, h, 0:1, :],
                north_in[0, k, h, tall - 2 : tall - 1, :],
                north_in[0, k, h, tall - 1 : tall, :],
                north_in[1, k, h, tall - 1 : tall, :],
                mask_in[k, h, 0:1, :].astype(F32),
                mask_in[k, h, 1:2, :].astype(F32),
                mask_in[k, h, tall - 2 : tall - 1, :].astype(F32),
                mask_in[k, h, tall - 1 : tall, :].astype(F32),
            )
            for j, one in enumerate(kept_rows):
                row_own[j * levels + k : j * levels + k + 1, cols] = one


def side_correction(west, east, mine, own):
    lane = lax.bitwise_and(lane_ids(), 7)
    a, b, g, up = face_terms(rolled(west, -2), rolled(west, -3))
    near = rolled(west, -1)
    flux = a * near + b * mine - g * jnp.where(up, west, rolled(mine, -1))
    first = jnp.maximum(0.125 * own, 0.0) * near
    col0 = rolled(own, -1) * (flux + first)
    col1 = -(rolled(own, -2) * first)
    a, b, g, up = face_terms(rolled(own, -4), rolled(own, -5))
    last = b * east - jnp.minimum(g, 0.0) * rolled(east, -1)
    before = -(jnp.minimum(0.125 * rolled(own, -3), 0.0) * east)
    col2 = -(rolled(own, -6) * before)
    col3 = rolled(own, -7) * (before - last)
    found = jnp.where(lane == 0, col0, rolled(col1, 1))
    found = jnp.where(lane >= 2, rolled(col2, 2), found)
    found = jnp.where(lane >= 3, rolled(col3, 3), found)
    return jnp.where(lane < 4, found, 0.0)


def unpacked(correction, tl, h):
    lane = lane_ids()
    if h == 0:
        return jnp.where(lane < 2, rolled(correction, -8 * tl), 0.0)
    return jnp.where(lane >= LANES - 2, rolled(correction, LANES - 4 - 8 * tl), 0.0)


def across_fold(x, index):
    picked = []
    for h in range(2):
        at = jnp.broadcast_to(index[:, h * LANES : (h + 1) * LANES], (SUB, LANES))
        low = lax.bitwise_and(at, LANES - 1)
        parts = [jnp.take_along_axis(x[j], low, axis=1) for j in range(2)]
        picked.append(jnp.where(at < LANES, parts[0], parts[1]))
    return picked


def row_corrections(state, offset, rows_a, rows_b, faces_a, faces_b, row_own, index, tall, levels, apply):
    even_lat = parity("lat")
    lat = lax.axis_index("lat")
    at_top = lat == lax.axis_size("lat") - 1
    at_bottom = lat == 0
    for t in range(TRACERS):
        part = [slice((depth * TRACERS + t) * levels, (depth * TRACERS + t + 1) * levels) for depth in range(2)]
        north, south = [], []
        for depth in range(2):
            one, other = rows_a[part[depth], :], rows_b[part[depth], :]
            upper = jnp.where(even_lat, one, other)
            lower = jnp.where(even_lat, other, one)
            lower = jnp.where(at_bottom, 0.0, lower)
            upper = [upper[:, h * LANES : (h + 1) * LANES] for h in range(2)]
            folded = across_fold(upper, index)
            north.append([jnp.where(at_top, folded[h], upper[h]) for h in range(2)])
            south.append([lower[:, h * LANES : (h + 1) * LANES] for h in range(2)])
        for h in range(2):
            cols = slice(h * LANES, (h + 1) * LANES)
            base = 2 * TRACERS * levels
            faces = []
            for comp in range(2):
                span = slice(base + comp * levels, base + (comp + 1) * levels)
                one = jnp.where(even_lat, faces_b[span, cols], faces_a[span, cols])
                faces.append(jnp.where(at_bottom, 0.0, one))
            kept = [row_own[j * levels : (j + 1) * levels, cols] for j in range(8)]
            bottom = [
                jnp.concatenate([state[t, k, h, offset + j : offset + j + 1, :] for k in range(levels)], axis=0)
                for j in range(2)
            ]
            a, b, g, up = face_terms(faces[0], faces[1])
            flux = a * south[0][h] + b * bottom[0] - g * jnp.where(up, south[1][h], bottom[1])
            first = jnp.maximum(0.125 * kept[0], 0.0) * south[0][h]
            row0 = kept[4] * (flux + first)
            row1 = -(kept[5] * first)
            a, b, g, up = face_terms(kept[2], kept[3])
            last = b * north[0][h] - jnp.minimum(g, 0.0) * north[1][h]
            before = -(jnp.minimum(0.125 * kept[1], 0.0) * north[0][h])
            row2 = -(kept[6] * before)
            row3 = kept[7] * (before - last)
            for k in range(levels):
                for at, add in ((0, row0), (1, row1), (tall - 2, row2), (tall - 1, row3)):
                    apply(t, k, h, at, add[k : k + 1, :])


def received(side_a, side_b, rows, even_lon):
    one, other = side_a[rows, :], side_b[rows, :]
    return jnp.where(even_lon, other, one), jnp.where(even_lon, one, other)


def add_rows(state, offset):
    def apply(t, k, h, at, add):
        spot = (t, k, h, slice(offset + at, offset + at + 1), slice(None))
        state[spot] = state[spot] + add

    return apply


def edge_kernel(
    got_a, got_b, sent_a, sent_b, rows_a, rows_b, own, row_own, packed, index, before, c_in,
    c, next_a, next_b, next_rows_a, next_rows_b, correction,
):
    levels, tall = before.shape[1], own.shape[0]
    tiles = tall // SUB
    even_lon = parity("lon")

    def one_tile(r):
        rows = tile_rows(r)
        west, east = received(got_a, got_b, rows, even_lon)
        _, mine = received(sent_a, sent_b, rows, jnp.logical_not(even_lon))
        return side_correction(west, east, mine, own[rows, :])

    def middle(r, carry):
        rows = tile_rows(r)
        found = one_tile(r)
        correction[rows, :] = found
        west = packed[0, rows, :] + found
        east = packed[1, rows, :] + rolled(found, -2)
        next_a[rows, :] = jnp.where(even_lon, east, west)
        next_b[rows, :] = jnp.where(even_lon, west, east)
        return carry

    lax.fori_loop(1, tiles - 1, middle, 0)
    row_corrections(before, PAD, rows_a, rows_b, rows_a, rows_b, row_own, index, tall, levels, add_rows(c, PAD))
    for r in (0, tiles - 1):
        rows = tile_rows(r)
        found = one_tile(r)
        correction[rows, :] = jnp.zeros((SUB, LANES), F32)
        for t in range(TRACERS):
            for k in range(levels):
                for h in range(2):
                    spot = (t, k, h, tile_rows(r, PAD), slice(None))
                    c[spot] = c[spot] + unpacked(found, t * levels + k, h)
        west, east = packed_edges(lambda t, k, h: c[t, k, h, tile_rows(r, PAD), :], levels)
        next_a[rows, :] = jnp.where(even_lon, east, west)
        next_b[rows, :] = jnp.where(even_lon, west, east)
    send_rows(c, next_rows_a, next_rows_b, levels, tall)


def second_kernel(c_in, correction, east_in, north_in, mask_in, mix, c, out, south):
    levels, tall = mask_in.shape[0], mask_in.shape[2]
    tiles = tall // SUB
    for t in range(TRACERS):
        for k in range(levels):
            for h in range(2):
                south[t, k, h, 0:PAD, :] = jnp.zeros((PAD, LANES), F32)

    def fix(r):
        found = correction[tile_rows(r), :]
        for t in range(TRACERS):
            for k in range(levels):
                for h in range(2):
                    spot = (t, k, h, tile_rows(r, PAD), slice(None))
                    c[spot] = c[spot] + unpacked(found, t * levels + k, h)

    def body(r, carry):
        fix(r + 1)
        advance_tile(r, c, south, east_in, north_in, mask_in, mix, out, 0)
        return carry

    lax.fori_loop(0, tiles - 1, body, 0)
    advance_tile(tiles - 1, c, south, east_in, north_in, mask_in, mix, out, 0)


def last_kernel(
    got_a, got_b, sent_a, sent_b, first_a, first_b, rows_a, rows_b, faces_a, faces_b,
    own, row_own, index, before, mask_in, c_in,
    fields, density, c, fields_out, density_out, sems,
):
    levels, tall = before.shape[1], own.shape[0]
    even_lon = parity("lon")
    slot = lax.bitwise_and(lane_ids(), 7)
    row_corrections(before, PAD, rows_a, rows_b, faces_a, faces_b, row_own, index, tall, levels, add_rows(c, 0))

    def body(r, carry):
        rows = tile_rows(r)
        west, east = received(got_a, got_b, rows, even_lon)
        earlier, _ = received(first_a, first_b, rows, even_lon)
        west = jnp.where(slot < 2, west, earlier)
        _, mine = received(sent_a, sent_b, rows, jnp.logical_not(even_lon))
        found = side_correction(west, east, mine, own[rows, :])
        for k in range(levels):
            for h in range(2):
                both = []
                for t in range(TRACERS):
                    x = c[t, k, h, rows, :] + unpacked(found, t * levels + k, h)
                    fields_out[t, k, h, rows, :] = x
                    both.append(x)
                heat, salt = both
                wet = mask_in[k, h, rows, :].astype(F32)
                density_out[k, h, rows, :] = wet * (0.8 * salt - 0.2 * heat - 0.05 * heat * heat)
        return carry

    cuts = [0, 40, 80, 120, tall]
    copies = []
    for i, (lo, hi) in enumerate(zip(cuts[:-1], cuts[1:])):
        lax.fori_loop(lo // SUB, hi // SUB, body, 0)
        for h in range(2):
            cols = slice(h * LANES, (h + 1) * LANES)
            copies.append(
                pltpu.make_async_copy(
                    fields_out.at[:, :, h, lo:hi, :], fields.at[:, :, lo:hi, cols], sems.at[4 * i + h]
                )
            )
            copies.append(
                pltpu.make_async_copy(
                    density_out.at[:, h, lo:hi, :], density.at[:, lo:hi, cols], sems.at[4 * i + 2 + h]
                )
            )
        for one in copies[-4:]:
            one.start()
    for one in copies:
        one.wait()


def vmem(*shape, dtype=F32):
    return pltpu.VMEM(shape, dtype)


ON_CHIP = pl.BlockSpec(memory_space=pltpu.VMEM)
ANYWHERE = pl.BlockSpec(memory_space=pl.ANY)
SCALARS = pl.BlockSpec(memory_space=pltpu.SMEM)


def call(kernel, ins, out_shape, out_specs, scratch, cost, aliases=None):
    return pl.pallas_call(
        kernel,
        out_shape=out_shape,
        in_specs=ins,
        out_specs=out_specs,
        scratch_shapes=scratch,
        input_output_aliases=aliases or {},
        cost_estimate=pl.CostEstimate(flops=cost[0], bytes_accessed=cost[1], transcendentals=0),
        compiler_params=pltpu.CompilerParams(vmem_limit_bytes=VMEM_BYTES),
    )


def pairings(lats, lons):
    place = lambda a, o: (a % lats) * lons + o % lons
    by = {"lon_a": [], "lon_b": [], "lat_a": [], "lat_b": []}
    for a in range(lats):
        for o in range(lons):
            me = place(a, o)
            by["lon_a"].append((me, place(a, o ^ 1)))
            by["lon_b"].append((me, place(a, o + 1 if o % 2 else o - 1)))
            by["lat_a"].append((me, place(a ^ 1, o)))
            if a == lats - 1:
                other = place(a, lons - 1 - o)
            elif a == 0:
                other = place(a, o ^ 1)
            else:
                other = place(a + 1 if a % 2 else a - 1, o)
            by["lat_b"].append((me, other))
    return by


def on_device(pairs, tracers, east_faces, north_faces, land_mask, fold_partner, vert_mix):
    _, levels, tall, wide = tracers.shape
    assert wide == 2 * LANES and TRACERS * levels * 8 == LANES and tall % SUB == 0
    index = (fold_partner & (wide - 1)).reshape(1, wide)
    both = ("lat", "lon")
    swap = lambda x, name: lax.ppermute(x, both, pairs[name])
    state = vmem(TRACERS, levels, 2, tall + 2 * PAD, LANES)
    side, rows3, rows2 = vmem(tall, LANES), vmem(6 * levels, wide), vmem(4 * levels, wide)
    faces = vmem(2, levels, 2, tall, LANES)
    mask_shape = vmem(levels, 2, tall, LANES, dtype=jnp.int32)
    grid_bytes = tracers.size * 4

    c0, side_a, side_b, rows_a, rows_b = call(
        start_kernel,
        [ANYWHERE] * 3,
        [state, side, side, rows3, rows3],
        [ON_CHIP] * 5,
        [vmem(2, levels, tall, LANES), vmem(2, levels, SUB, wide), pltpu.SemaphoreType.DMA((13,))],
        (1000000, 2 * grid_bytes),
    )(tracers, east_faces, north_faces)
    got_a, got_b = swap(side_a, "lon_a"), swap(side_b, "lon_b")
    got_rows_a, got_rows_b = swap(rows_a, "lat_a"), swap(rows_b, "lat_b")
    c1, packed, own, row_own, east_in, north_in, mask_in = call(
        inner_kernel,
        [ON_CHIP, ANYWHERE, ANYWHERE, ANYWHERE, SCALARS],
        [state, vmem(2, tall, LANES), side, vmem(8 * levels, wide), faces, faces, mask_shape],
        [ON_CHIP] * 7,
        [vmem(TRACERS, levels, 2, tall + PAD, LANES), pltpu.SemaphoreType.DMA((24,))],
        (40000000, 4 * grid_bytes),
    )(c0, east_faces, north_faces, land_mask, vert_mix)
    c1, next_a, next_b, next_rows_a, next_rows_b, correction = call(
        edge_kernel,
        [ON_CHIP] * 12,
        [state, side, side, rows2, rows2, side],
        [ON_CHIP] * 6,
        [],
        (1000000, 1000000),
        {11: 0},
    )(got_a, got_b, side_a, side_b, got_rows_a, got_rows_b, own, row_own, packed, index, c0, c1)
    new_a, new_b = swap(next_a, "lon_a"), swap(next_b, "lon_b")
    new_rows_a, new_rows_b = swap(next_rows_a, "lat_a"), swap(next_rows_b, "lat_b")
    c1, c2 = call(
        second_kernel,
        [ON_CHIP] * 5 + [SCALARS],
        [state, vmem(TRACERS, levels, 2, tall, LANES)],
        [ON_CHIP] * 2,
        [vmem(TRACERS, levels, 2, tall + PAD, LANES)],
        (40000000, 4 * grid_bytes),
        {0: 0},
    )(c1, correction, east_in, north_in, mask_in, vert_mix)
    fields, density, _ = call(
        last_kernel,
        [ON_CHIP] * 16,
        [
            jax.ShapeDtypeStruct(tracers.shape, F32),
            jax.ShapeDtypeStruct(land_mask.shape, F32),
            vmem(TRACERS, levels, 2, tall, LANES),
        ],
        [ANYWHERE, ANYWHERE, ON_CHIP],
        [
            vmem(TRACERS, levels, 2, tall, LANES),
            vmem(levels, 2, tall, LANES),
            pltpu.SemaphoreType.DMA((16,)),
        ],
        (4000000, 2 * grid_bytes),
        {15: 2},
    )(
        new_a, new_b, next_a, next_b, got_a, got_b, new_rows_a, new_rows_b, got_rows_a, got_rows_b,
        own, row_own, index, c1, mask_in, c2,
    )
    return fields, density


def solution(mesh):
    in_specs = (
        P(None, None, "lat", "lon"),
        P(None, None, "lat", "lon"),
        P(None, None, "lat", "lon"),
        P(None, "lat", "lon"),
        P("lon"),
        P(),
    )
    out_specs = (P(None, None, "lat", "lon"), P(None, "lat", "lon"))
    pairs = pairings(mesh.shape["lat"], mesh.shape["lon"])

    def body(*args):
        return on_device(pairs, *args)

    return jax.shard_map(body, mesh=mesh, in_specs=in_specs, out_specs=out_specs, check_vma=False)
```

time: 131 us -> 67.2 us (0.51); the launches traced: 128 us -> 66.9 us
  other arithmetic: 48.5 us -> 0.01 us
  Pallas kernels: 0 us -> 45 us
  local copies, waits for them, and re-layouts: 36.8 us -> 6.26 us
  starting transfers between devices: 40.4 us -> 14.9 us
  waiting for transfers between devices: 1.72 us -> 0.02 us
    pallas_call x0 -> x5, Pallas kernels: none -> 45 us  [the longest x1 14.3 us: on_device(): call(inner_kernel, [ON_CHIP, ANYWHERE, ANYWHERE, ANYWHERE, SCALARS], [sta...]
    ppermute x18 -> x8, starting transfers between devices: 40.4 us -> 14.9 us  [on_device(): swap = lambda x, name: lax.ppermute(x, both, pairs[name])]
    sub x4 -> x0, other arithmetic: 22 us -> none  [quick_flux(): flow_number * jnp.where(flow_number > 0.0, upwind, downwind)]
    slice x8 -> x0, local copies, waits for them, and re-layouts: 13.5 us -> none  [the longest x5 7.96 us: extended(): lax.slice_in_dim(block, block.shape[dim] - width, None, axis=dim)]
    mul x6 -> x0, other arithmetic: 10.7 us -> none  [the longest x2 4.44 us: on_device(): vertical = vert_open * (fields[:, 1:] - fields[:, :-1])]
    add x2 -> x0, other arithmetic: 9.05 us -> none  [on_device(): fields = fields + wet_cells * change]
    ppermute x5 -> x0, local copies, waits for them, and re-layouts: 7.51 us -> none  [the longest x2 3.02 us: extended(): lax.ppermute(lax.slice_in_dim(block, block.shape[dim] - width, None, axis...]
    gather x4 -> x0, local copies, waits for them, and re-layouts: 6.6 us -> none  [on_device(): fold_ghost = jnp.take(mirror_rows[:, :, ::-1, :], local_index, axis=3)]
  transfers between devices with their start and end apart: 18 -> 8, of which waited for: 1 -> 0; matrix products, arithmetic and copies ran while one was open for 48% -> 0% of each run, Pallas kernels for 0% -> 38%
where the time goes in v1:
time: 67.2 us; the launch traced here: 66.9 us
  Pallas kernels  45 us (67%)
  starting transfers between devices  14.9 us (22%)
  local copies, waits for them, and re-layouts  6.26 us (9%)
  between operations  0.76 us (1%)
    ppermute x8, starting transfers between devices, on_device(): swap = lambda x, name: lax.ppermute(x, both, pairs[name])  14.9 us
    pallas_call x1, Pallas kernels, on_device(): call(inner_kernel, [ON_CHIP, ANYWHERE, ANYWHERE, ANYWHERE, SCALARS], [sta...  14.3 us
    pallas_call x1, Pallas kernels, on_device(): call(second_kernel, [ON_CHIP] * 5 + [SCALARS], [state, vmem(TRACERS, leve...  11.2 us
    pallas_call x1, Pallas kernels, on_device(): call(last_kernel, [ON_CHIP] * 16, [jax.ShapeDtypeStruct(tracers.shape, F3...  7.76 us
    pallas_call x1, Pallas kernels, on_device(): call(edge_kernel, [ON_CHIP] * 12, [state, side, side, rows2, rows2, side]...  7.26 us
    unnamed x18, local copies, waits for them, and re-layouts  6.26 us
    pallas_call x1, Pallas kernels, on_device(): call(start_kernel, [ANYWHERE] * 3, [state, side, side, rows3, rows3], [ON...  4.49 us
  transfers between devices with their start and end apart: 8, of which 0 were waited for; matrix products, arithmetic and copies ran while one was open for 0% of the time, Pallas kernels for 38%

profile of v1, /device:TPU:1, one launch (start us, length us, event | category | flops | bytes accessed | tf_op | source)
XLA Modules:
  0.0 66.9 jit_solution(7680234171902166884)
XLA Ops:
  0.6 0.0 copy-start.4
  0.6 1.7 %copy-done.4 = f32[2,8,152,256]{3,2,1,0:T(8,128)S(1)} copy-done((f32[2,8,152,256]{3,2,1,0:T(8,128)S(1)}, f32[2,8,152,256]{3,2,1,0:T(8,128)}, u32[]{:S(2)}) %copy-start.4) | copy-done | bytes 2490392
  2.3 0.0 copy-start.8
  2.3 4.5 %shard_map.77 = (f32[2,8,2,168,128]{4,3,2,1,0:T(8,128)S(1)}, f32[152,128]{1,0:T(8,128)S(1)}, f32[152,128]{1,0:T(8,128)S(1)}, f32[48,256]{1,0:T(8,128)S(1)}, f32[48,256]{1,0:T(8,128)S(1)}) custom-call(f32[2,8,152,256]{3,2,1,0:T(8,128)S(1)} %copy-done.4, f32[2,8,152,256]{3,2,1,0:T(8,128)} %east.3, f32[2,8,152,256]{3,2,1,0:T(8,128)} %north.3), custom_call_target="tpu_custom_call" | custom-call | flops 1000000 | bytes 4980736 | tf_op jit(solution)/shard_map/pallas_call | solution.py:528
  6.8 0.0 copy-start.1
  6.8 1.5 %copy-done.1 = f32[2,8,2,168,128]{4,3,2,1,0:T(8,128)} copy-done((f32[2,8,2,168,128]{4,3,2,1,0:T(8,128)}, f32[2,8,2,168,128]{4,3,2,1,0:T(8,128)S(1)}, u32[]{:S(2)}) %copy-start.1) | copy-done | bytes 2752536
  8.4 3.2 %collective-permute-start.2 = (f32[48,256]{1,0:T(8,128)S(1)}, f32[48,256]{1,0:T(8,128)S(1)}, u32[]{:S(2)}, u32[]{:S(2)}) collective-permute-start(f32[48,256]{1,0:T(8,128)S(1)} %get-tuple-element.26), channel_id=1, source_target_pairs={{0,16},{1,17},{2,18},{3,19},{4,20},{5,21},{6,22},{7,23},{8,24},{9,... | collective-permute-start | bytes 147464 | tf_op jit(solution)/shard_map/ppermute | solution.py:521
  11.6 0.9 %collective-permute-start.3 = (f32[48,256]{1,0:T(8,128)S(1)}, f32[48,256]{1,0:T(8,128)S(1)}, u32[]{:S(2)}, u32[]{:S(2)}) collective-permute-start(f32[48,256]{1,0:T(8,128)S(1)} %get-tuple-element.27), channel_id=1, source_target_pairs={{0,1},{1,0},{2,3},{3,2},{4,5},{5,4},{6,7},{7,6},{8,9},{9,8},{10,11... | collective-permute-start | bytes 147464 | tf_op jit(solution)/shard_map/ppermute | solution.py:521
  12.5 0.3 collective-permute-start
  12.8 6.4 %collective-permute-start.1 = (f32[152,128]{1,0:T(8,128)S(1)}, f32[152,128]{1,0:T(8,128)S(1)}, u32[]{:S(2)}, u32[]{:S(2)}) collective-permute-start(f32[152,128]{1,0:T(8,128)S(1)} %get-tuple-element.25.sent_b), channel_id=1, source_target_pairs={{0,15},{1,2},{2,1},{3,4},{4,3},{5,6},{6,5},{7,8},{8,7},{9,10},{10,... | collective-permute-start | bytes 233480 | tf_op jit(solution)/shard_map/ppermute | solution.py:521
  19.3 0.0 copy-done.8
  19.3 14.3 %shard_map.78 = (f32[2,8,2,168,128]{4,3,2,1,0:T(8,128)S(1)}, f32[2,152,128]{2,1,0:T(8,128)S(1)}, f32[152,128]{1,0:T(8,128)S(1)}, f32[64,256]{1,0:T(8,128)S(1)}, ...) custom-call(f32[2,8,2,168,128]{4,3,2,1,0:T(8,128)} %copy-done.1, ...), custom_call_target="tpu_custom_call" | custom-call | flops 40000000 | bytes 9961472 | tf_op jit(solution)/shard_map/pallas_call | solution.py:538
  33.6 0.0 copy-start.5
  33.6 1.4 %copy-done.5 = f32[2,8,2,152,128]{4,3,2,1,0:T(8,128)} copy-done((f32[2,8,2,152,128]{4,3,2,1,0:T(8,128)}, f32[2,8,2,152,128]{4,3,2,1,0:T(8,128)S(1)}, u32[]{:S(2)}) %copy-start.5) | copy-done | bytes 2490392
  35.1 0.0 copy-start.2
  35.1 0.0 copy-start.6
  35.1 0.0 collective-permute-done.2.rows_a.faces_a
  35.1 0.0 collective-permute-done.3.rows_b.faces_b
  35.1 0.0 collective-permute-done.got_a.first_a
  35.1 0.0 collective-permute-done.1.got_b.first_b
  35.1 0.0 copy-start.7
  35.1 7.3 %shard_map.79 = (f32[2,8,2,168,128]{4,3,2,1,0:T(8,128)S(1)}, f32[152,128]{1,0:T(8,128)S(1)}, f32[152,128]{1,0:T(8,128)S(1)}, f32[32,256]{1,0:T(8,128)S(1)}, f32[...) custom-call(f32[152,128]{1,0:T(8,128)S(1)} %collective-permute-done.got_a.first_a, ...), custom_call_target="tpu_custom_call", output_to_operand_aliasing={{0}: (11, {})} | custom-call | flops 1000000 | bytes 1000000 | tf_op jit(solution)/shard_map/pallas_call | solution.py:546
  42.4 0.0 copy-done.2
  42.4 0.0 copy-done.6
  42.4 0.1 collective-permute-start.4
  42.5 1.9 %collective-permute-start.5 = (f32[152,128]{1,0:T(8,128)S(1)}, f32[152,128]{1,0:T(8,128)S(1)}, u32[]{:S(2)}, u32[]{:S(2)}) collective-permute-start(f32[152,128]{1,0:T(8,128)S(1)} %get-tuple-element.34.sent_b), channel_id=1, source_target_pairs={{0,15},{1,2},{2,1},{3,4},{4,3},{5,6},{6,5},{7,8},{8,7},{9,10},{10,... | collective-permute-start | bytes 233480 | tf_op jit(solution)/shard_map/ppermute | solution.py:521
  44.4 0.0 collective-permute-start.6
  44.4 2.0 %collective-permute-start.7 = (f32[32,256]{1,0:T(8,128)S(1)}, f32[32,256]{1,0:T(8,128)S(1)}, u32[]{:S(2)}, u32[]{:S(2)}) collective-permute-start(f32[32,256]{1,0:T(8,128)S(1)} %get-tuple-element.36), channel_id=1, source_target_pairs={{0,1},{1,0},{2,3},{3,2},{4,5},{5,4},{6,7},{7,6},{8,9},{9,8},{10,11... | collective-permute-start | bytes 98312 | tf_op jit(solution)/shard_map/ppermute | solution.py:521
  46.4 0.0 copy-done.7
  46.4 0.0 copy-start.3
  46.4 11.2 %shard_map.80 = (f32[2,8,2,168,128]{4,3,2,1,0:T(8,128)S(1)}, f32[2,8,2,152,128]{4,3,2,1,0:T(8,128)S(1)}) custom-call(f32[2,8,2,168,128]{4,3,2,1,0:T(8,128)S(1)} %get-tuple-element.37.c_in, f32[152,128]{1,0:T(8,128)S(1)} %get-tuple-element.38.correction, f32[2,8,2,152,128]{4,3,2,1,0:T(8,128)} %copy-done.5, ...), custom_call_target="tpu_custom_call", output_to_operand_aliasing={{0}: (0, {})} | custom-call | flops 40000000 | bytes 9961472 | tf_op jit(solution)/shard_map/pallas_call | solution.py:557
  57.6 0.0 copy-start
  57.6 1.5 %copy-done = f32[2,8,2,168,128]{4,3,2,1,0:T(8,128)} copy-done((f32[2,8,2,168,128]{4,3,2,1,0:T(8,128)}, f32[2,8,2,168,128]{4,3,2,1,0:T(8,128)S(1)}, u32[]{:S(2)}) %copy-start) | copy-done | bytes 2752536
  59.1 0.0 collective-permute-done.6.rows_a
  59.1 0.0 collective-permute-done.7.rows_b
  59.1 0.0 collective-permute-done.4.got_a
  59.1 0.0 collective-permute-done.5.got_b
  59.1 0.0 copy-done.3
  59.2 7.8 %shard_map.81 = (f32[2,8,152,256]{3,2,1,0:T(8,128)}, f32[8,152,256]{2,1,0:T(8,128)}, f32[2,8,2,152,128]{4,3,2,1,0:T(8,128)S(1)}) custom-call(f32[152,128]{1,0:T(8,128)S(1)} %collective-permute-done.4.got_a, f32[152,128]{1,0:T(8,128)S(1)} %collective-permute-done.5.got_b, f32[152,128]{1,0:T(8,128)S(1)} %get-tuple-element.33.sent_a, ...), custom_call_target="tpu_custom_call", output_to_operand_aliasing={{2}: (15, {})} | custom-call | flops 4000000 | bytes 4980736 | tf_op jit(solution)/shard_map/pallas_call | solution.py:566
  (1 shorter events, 0.0 us)
Async XLA Ops:
  0.6 1.7 %copy-start.4 = (f32[2,8,152,256]{3,2,1,0:T(8,128)S(1)}, f32[2,8,152,256]{3,2,1,0:T(8,128)}, u32[]{:S(2)}) copy-start(f32[2,8,152,256]{3,2,1,0:T(8,128)} %tracers.1) | copy-start | bytes 7471108
  2.3 17.0 %copy-start.8 = (s32[256]{0:T(256)S(1)}, s32[256]{0:T(256)}, u32[]{:S(2)}) copy-start(s32[256]{0:T(256)} %param.10) | copy-start | bytes 3076
  6.8 1.6 %copy-start.1 = (f32[2,8,2,168,128]{4,3,2,1,0:T(8,128)}, f32[2,8,2,168,128]{4,3,2,1,0:T(8,128)S(1)}, u32[]{:S(2)}) copy-start(f32[2,8,2,168,128]{4,3,2,1,0:T(8,128)S(1)} %get-tuple-element.28.c.before) | copy-start | bytes 8257540
  8.4 26.7 %collective-permute-start.2 = (f32[48,256]{1,0:T(8,128)S(1)}, f32[48,256]{1,0:T(8,128)S(1)}, u32[]{:S(2)}, u32[]{:S(2)}) collective-permute-start(f32[48,256]{1,0:T(8,128)S(1)} %get-tuple-element.26), channel_id=1, source_target_pairs={{0,16},{1,17},{2,18},{3,19},{4,20},{5,21},{6,22},{7,23},{8,24},{9,... | collective-permute-start | bytes 147464 | tf_op jit(solution)/shard_map/ppermute | solution.py:521
  11.6 23.5 %collective-permute-start.3 = (f32[48,256]{1,0:T(8,128)S(1)}, f32[48,256]{1,0:T(8,128)S(1)}, u32[]{:S(2)}, u32[]{:S(2)}) collective-permute-start(f32[48,256]{1,0:T(8,128)S(1)} %get-tuple-element.27), channel_id=1, source_target_pairs={{0,1},{1,0},{2,3},{3,2},{4,5},{5,4},{6,7},{7,6},{8,9},{9,8},{10,11... | collective-permute-start | bytes 147464 | tf_op jit(solution)/shard_map/ppermute | solution.py:521
  12.5 22.6 %collective-permute-start = (f32[152,128]{1,0:T(8,128)S(1)}, f32[152,128]{1,0:T(8,128)S(1)}, u32[]{:S(2)}, u32[]{:S(2)}) collective-permute-start(f32[152,128]{1,0:T(8,128)S(1)} %get-tuple-element.24.sent_a), channel_id=1, source_target_pairs={{0,1},{1,0},{2,3},{3,2},{4,5},{5,4},{6,7},{7,6},{8,9},{9,8},{10,11... | collective-permute-start | bytes 233480 | tf_op jit(solution)/shard_map/ppermute | solution.py:521
  12.8 22.3 %collective-permute-start.1 = (f32[152,128]{1,0:T(8,128)S(1)}, f32[152,128]{1,0:T(8,128)S(1)}, u32[]{:S(2)}, u32[]{:S(2)}) collective-permute-start(f32[152,128]{1,0:T(8,128)S(1)} %get-tuple-element.25.sent_b), channel_id=1, source_target_pairs={{0,15},{1,2},{2,1},{3,4},{4,3},{5,6},{6,5},{7,8},{8,7},{9,10},{10,... | collective-permute-start | bytes 233480 | tf_op jit(solution)/shard_map/ppermute | solution.py:521
  33.6 1.5 %copy-start.5 = (f32[2,8,2,152,128]{4,3,2,1,0:T(8,128)}, f32[2,8,2,152,128]{4,3,2,1,0:T(8,128)S(1)}, u32[]{:S(2)}) copy-start(f32[2,8,2,152,128]{4,3,2,1,0:T(8,128)S(1)} %get-tuple-element.39.east_in) | copy-start | bytes 7471108
  35.1 7.3 %copy-start.2 = (s32[8,2,152,128]{3,2,1,0:T(8,128)}, s32[8,2,152,128]{3,2,1,0:T(8,128)S(1)}, u32[]{:S(2)}) copy-start(s32[8,2,152,128]{3,2,1,0:T(8,128)S(1)} %get-tuple-element.41.mask_in) | copy-start | bytes 3735556
  35.1 7.3 %copy-start.6 = (f32[2,8,2,152,128]{4,3,2,1,0:T(8,128)}, f32[2,8,2,152,128]{4,3,2,1,0:T(8,128)S(1)}, u32[]{:S(2)}) copy-start(f32[2,8,2,152,128]{4,3,2,1,0:T(8,128)S(1)} %get-tuple-element.40.north_in) | copy-start | bytes 7471108
  35.1 11.3 %copy-start.7 = (f32[7]{0:T(128)S(1)}, f32[7]{0:T(128)}, u32[]{:S(2)}) copy-start(f32[7]{0:T(128)} %mix.3) | copy-start | bytes 88
  42.4 16.7 %collective-permute-start.4 = (f32[152,128]{1,0:T(8,128)S(1)}, f32[152,128]{1,0:T(8,128)S(1)}, u32[]{:S(2)}, u32[]{:S(2)}) collective-permute-start(f32[152,128]{1,0:T(8,128)S(1)} %get-tuple-element.33.sent_a), channel_id=1, source_target_pairs={{0,1},{1,0},{2,3},{3,2},{4,5},{5,4},{6,7},{7,6},{8,9},{9,8},{10,11... | collective-permute-start | bytes 233480 | tf_op jit(solution)/shard_map/ppermute | solution.py:521
  42.5 16.6 %collective-permute-start.5 = (f32[152,128]{1,0:T(8,128)S(1)}, f32[152,128]{1,0:T(8,128)S(1)}, u32[]{:S(2)}, u32[]{:S(2)}) collective-permute-start(f32[152,128]{1,0:T(8,128)S(1)} %get-tuple-element.34.sent_b), channel_id=1, source_target_pairs={{0,15},{1,2},{2,1},{3,4},{4,3},{5,6},{6,5},{7,8},{8,7},{9,10},{10,... | collective-permute-start | bytes 233480 | tf_op jit(solution)/shard_map/ppermute | solution.py:521
  44.4 14.7 %collective-permute-start.6 = (f32[32,256]{1,0:T(8,128)S(1)}, f32[32,256]{1,0:T(8,128)S(1)}, u32[]{:S(2)}, u32[]{:S(2)}) collective-permute-start(f32[32,256]{1,0:T(8,128)S(1)} %get-tuple-element.35), channel_id=1, source_target_pairs={{0,16},{1,17},{2,18},{3,19},{4,20},{5,21},{6,22},{7,23},{8,24},{9,... | collective-permute-start | bytes 98312 | tf_op jit(solution)/shard_map/ppermute | solution.py:521
  44.4 14.7 %collective-permute-start.7 = (f32[32,256]{1,0:T(8,128)S(1)}, f32[32,256]{1,0:T(8,128)S(1)}, u32[]{:S(2)}, u32[]{:S(2)}) collective-permute-start(f32[32,256]{1,0:T(8,128)S(1)} %get-tuple-element.36), channel_id=1, source_target_pairs={{0,1},{1,0},{2,3},{3,2},{4,5},{5,4},{6,7},{7,6},{8,9},{9,8},{10,11... | collective-permute-start | bytes 98312 | tf_op jit(solution)/shard_map/ppermute | solution.py:521
  46.4 12.8 %copy-start.3 = (s32[8,2,152,128]{3,2,1,0:T(8,128)S(1)}, s32[8,2,152,128]{3,2,1,0:T(8,128)}, u32[]{:S(2)}) copy-start(s32[8,2,152,128]{3,2,1,0:T(8,128)} %copy-done.2) | copy-start | bytes 3735556
  57.6 1.6 %copy-start = (f32[2,8,2,168,128]{4,3,2,1,0:T(8,128)}, f32[2,8,2,168,128]{4,3,2,1,0:T(8,128)S(1)}, u32[]{:S(2)}) copy-start(f32[2,8,2,168,128]{4,3,2,1,0:T(8,128)S(1)} %get-tuple-element.42.before) | copy-start | bytes 8257540

commit v2 on v1

v2 whole, which is shorter than its diff:
```python
import jax
import jax.numpy as jnp
from jax import lax
from jax.experimental import pallas as pl
from jax.experimental.pallas import tpu as pltpu
from jax.sharding import PartitionSpec as P

F32 = jnp.float32
LANES = 128
SUB = 8
PAD = 8
TRACERS = 2
VMEM_BYTES = 12 * 1024 * 1024


def lane_ids():
    return lax.broadcasted_iota(jnp.int32, (SUB, LANES), 1)


def rolled(x, by):
    by = by % LANES
    return x if by == 0 else pltpu.roll(x, by, 1)


def face_terms(flow, spread):
    g = 0.125 * flow
    up = flow > 0.0
    g3 = 3.0 * g
    g6 = 6.0 * g
    return jnp.where(up, g6, g3) + spread, jnp.where(up, g3, g6) - spread, g, up


def tile_rows(index, offset=0):
    return pl.ds(pl.multiple_of(index * SUB, SUB) + offset, SUB)


def set_terms(r, east, north, mask, mix, terms, wet, mixing):
    levels = wet.shape[0]
    rows = tile_rows(r)
    for h in range(2):
        cells = [mask[k, h, rows, :].astype(F32) for k in range(levels)]
        for k in range(levels):
            wet[k, h, rows, :] = cells[k]
            if k + 1 < levels:
                mixing[k, h, rows, :] = mix[k] * cells[k] * cells[k + 1]
            for way, faces in enumerate((east, north)):
                a, b, g, _ = face_terms(faces[0, k, h, rows, :], faces[1, k, h, rows, :])
                for j, one in enumerate((a, b, g)):
                    terms[way, j, k, h, rows, :] = one


def advance_tile(r, c, south, terms, wet, mixing, out, out_pad):
    levels = wet.shape[0]
    lane = lane_ids()
    first, last, last2 = lane > 0, lane < LANES - 1, lane < LANES - 2
    rows = tile_rows(r)

    def cells(t, k, h, by=0):
        return c[t, k, h, tile_rows(r, PAD + by), :]

    for k in range(levels):
        for h in range(2):
            a, b, g = (terms[1, j, k, h, rows, :] for j in range(3))
            up = g > 0.0
            for t in range(TRACERS):
                further = jnp.where(up, cells(t, k, h, -1), cells(t, k, h, 2))
                face = a * cells(t, k, h) + b * cells(t, k, h, 1) - g * further
                south[t, k, h, tile_rows(r, PAD), :] = face
    below = [[None] * 2 for _ in range(TRACERS)]
    for k in range(levels):
        for t in range(TRACERS):
            c0 = [cells(t, k, h) for h in range(2)]
            plus1 = [rolled(x, -1) for x in c0]
            plus2 = [rolled(x, -2) for x in c0]
            minus1 = [rolled(x, 1) for x in c0]
            p1 = jnp.where(last, plus1[0], plus1[1]), jnp.where(last, plus1[1], 0.0)
            p2 = jnp.where(last2, plus2[0], plus2[1]), jnp.where(last2, plus2[1], 0.0)
            m1 = jnp.where(first, minus1[0], 0.0), jnp.where(first, minus1[1], minus1[0])
            flux = []
            for h in range(2):
                a, b, g = (terms[0, j, k, h, rows, :] for j in range(3))
                flux.append(a * c0[h] + b * p1[h] - g * jnp.where(g > 0.0, m1[h], p2[h]))
            shifted = [rolled(x, 1) for x in flux]
            west = jnp.where(first, shifted[0], 0.0), jnp.where(first, shifted[1], shifted[0])
            for h in range(2):
                change = west[h] - flux[h]
                change = change + (south[t, k, h, tile_rows(r, PAD - 1), :] - south[t, k, h, tile_rows(r, PAD), :])
                if k + 1 < levels:
                    vertical = mixing[k, h, rows, :] * (cells(t, k + 1, h) - c0[h])
                    change = change + vertical
                if k > 0:
                    change = change - below[t][h]
                if k + 1 < levels:
                    below[t][h] = vertical
                out[t, k, h, tile_rows(r, out_pad), :] = c0[h] + wet[k, h, rows, :] * change


def group(tl):
    lane = lane_ids()
    return lax.bitwise_and(lax.shift_right_logical(lane + 2, 3), LANES // SUB - 1) == tl


def slots():
    return lax.bitwise_and(lane_ids() + 2, 7) - 2


def packed_edges(get, levels, extra=None):
    lane = lane_ids()
    packed = jnp.zeros((SUB, LANES), F32)
    for t in range(TRACERS):
        for k in range(levels):
            tl = t * levels + k
            one = jnp.where(lane >= LANES - 2, get(t, k, 1), get(t, k, 0))
            if extra is not None:
                one = jnp.where(jnp.logical_and(lane >= 2, lane < 4), extra[k], one)
            packed = jnp.where(group(tl), rolled(one, 8 * tl), packed)
    return packed


def parity(axis):
    return lax.rem(lax.axis_index(axis), 2) == 0


def start_kernel(tracers, east, north, c, side, rows_a, rows_b, east_last, north_top, sems):
    levels, tall = tracers.shape[1], tracers.shape[2]
    cuts = [0, 40, 80, 120, tall]
    copies = []
    for i, (lo, hi) in enumerate(zip(cuts[:-1], cuts[1:])):
        group_of = []
        for h in range(2):
            group_of.append(
                pltpu.make_async_copy(
                    tracers.at[:, :, lo:hi, h * LANES : (h + 1) * LANES],
                    c.at[:, :, h, PAD + lo : PAD + hi, :],
                    sems.at[3 * i + h],
                )
            )
        group_of.append(
            pltpu.make_async_copy(
                east.at[:, :, lo:hi, LANES:], east_last.at[:, :, lo:hi, :], sems.at[3 * i + 2]
            )
        )
        copies.append(group_of)
    top_copy = pltpu.make_async_copy(north.at[:, :, tall - SUB :, :], north_top, sems.at[12])
    for group_of in copies:
        for one in group_of:
            one.start()
    top_copy.start()
    for t in range(TRACERS):
        for k in range(levels):
            for h in range(2):
                c[t, k, h, 0:PAD, :] = jnp.zeros((PAD, LANES), F32)
                c[t, k, h, PAD + tall :, :] = jnp.zeros((PAD, LANES), F32)
    lane = lane_ids()

    def pack(r, carry):
        rows = tile_rows(r)
        faces = []
        for k in range(levels):
            faces.append(
                jnp.where(lane == 2, rolled(east_last[0, k, rows, :], 3), rolled(east_last[1, k, rows, :], 4))
            )
        side[rows, :] = packed_edges(lambda t, k, h: c[t, k, h, tile_rows(r, PAD), :], levels, faces)
        return carry

    for i, (lo, hi) in enumerate(zip(cuts[:-1], cuts[1:])):
        for one in copies[i]:
            one.wait()
        lax.fori_loop(lo // SUB, hi // SUB, pack, 0)
    top_copy.wait()
    send_rows(c, rows_a, rows_b, levels, tall)
    for comp in range(2):
        for k in range(levels):
            one_row = north_top[comp, k, SUB - 1 : SUB, :]
            at = 2 * TRACERS * levels + comp * levels + k
            rows_a[at : at + 1, :] = one_row
            rows_b[at : at + 1, :] = one_row


def send_rows(c, rows_a, rows_b, levels, tall):
    even_lat = parity("lat")
    for depth in range(2):
        top, bottom = PAD + tall - 1 - depth, PAD + depth
        at_a = jnp.where(even_lat, top, bottom)
        at_b = jnp.where(even_lat, bottom, top)
        for t in range(TRACERS):
            for k in range(levels):
                tl = (depth * TRACERS + t) * levels + k
                for h in range(2):
                    cols = slice(h * LANES, (h + 1) * LANES)
                    rows_a[tl : tl + 1, cols] = c[t, k, h, pl.ds(at_a, 1), :]
                    rows_b[tl : tl + 1, cols] = c[t, k, h, pl.ds(at_b, 1), :]


def inner_kernel(c, east, north, mask, mix, out, packed, own, row_own, terms, wet, mixing, east_in, north_in, mask_in, south, sems):
    levels, tall = mask.shape[0], mask.shape[1]
    cuts = [0, 24, 64, 104, tall]
    copies = []
    for i, (lo, hi) in enumerate(zip(cuts[:-1], cuts[1:])):
        group_of = []
        for h in range(2):
            cols = slice(h * LANES, (h + 1) * LANES)
            for j, (src, dst) in enumerate(((east, east_in), (north, north_in))):
                group_of.append(
                    pltpu.make_async_copy(
                        src.at[:, :, lo:hi, cols], dst.at[:, :, h, lo:hi, :], sems.at[6 * i + 3 * h + j]
                    )
                )
            group_of.append(
                pltpu.make_async_copy(
                    mask.at[:, lo:hi, cols], mask_in.at[:, h, lo:hi, :], sems.at[6 * i + 3 * h + 2]
                )
            )
        copies.append(group_of)
    for group_of in copies:
        for one in group_of:
            one.start()
    for t in range(TRACERS):
        for k in range(levels):
            for h in range(2):
                south[t, k, h, 0:PAD, :] = jnp.zeros((PAD, LANES), F32)
                out[t, k, h, 0:PAD, :] = jnp.zeros((PAD, LANES), F32)
                out[t, k, h, PAD + tall :, :] = jnp.zeros((PAD, LANES), F32)
    lane = lane_ids()

    def body(r, carry):
        rows = tile_rows(r)
        set_terms(r, east_in, north_in, mask_in, mix, terms, wet, mixing)
        advance_tile(r, c, south, terms, wet, mixing, out, PAD)
        packed[rows, :] = packed_edges(lambda t, k, h: out[t, k, h, tile_rows(r, PAD), :], levels)
        kept = jnp.zeros((SUB, LANES), F32)
        edge = lane >= LANES - 2
        for k in range(levels):
            one = jnp.where(edge, wet[k, 1, rows, :], wet[k, 0, rows, :])
            flow = jnp.where(edge, east_in[0, k, 1, rows, :], east_in[0, k, 0, rows, :])
            some = jnp.where(lane == 5, rolled(east_in[1, k, 1, rows, :], 6), rolled(flow, 4))
            one = jnp.where(jnp.logical_and(lane >= 2, lane < 6), some, one)
            kept = jnp.where(group(k), rolled(one, 8 * k), kept)
        own[rows, :] = jnp.where(
            jnp.logical_or(lane < LANES // 2 - 2, edge), kept, rolled(kept, LANES // 2)
        )
        return carry

    for i, (lo, hi) in enumerate(zip(cuts[:-1], cuts[1:])):
        for one in copies[i]:
            one.wait()
        lax.fori_loop(lo // SUB, hi // SUB, body, 0)
    for k in range(levels):
        for h in range(2):
            cols = slice(h * LANES, (h + 1) * LANES)
            kept_rows = (
                north_in[0, k, h, 0:1, :],
                north_in[0, k, h, tall - 2 : tall - 1, :],
                north_in[0, k, h, tall - 1 : tall, :],
                north_in[1, k, h, tall - 1 : tall, :],
                wet[k, h, 0:1, :],
                wet[k, h, 1:2, :],
                wet[k, h, tall - 2 : tall - 1, :],
                wet[k, h, tall - 1 : tall, :],
            )
            for j, one in enumerate(kept_rows):
                row_own[j * levels + k : j * levels + k + 1, cols] = one


def side_correction(west, east, faces, mine, own):
    slot = slots()
    a, b, g, up = face_terms(rolled(faces, -2), rolled(faces, -3))
    near = rolled(west, 1)
    flux = a * near + b * mine - g * jnp.where(up, rolled(west, 2), rolled(mine, -1))
    flow = 0.125 * rolled(own, -4)
    first = jnp.maximum(flow, 0.0) * near
    _, b, _, _ = face_terms(rolled(own, -4), rolled(own, -6))
    beyond = jnp.minimum(flow, 0.0) * rolled(east, -2)
    last = rolled(beyond, 1) + b * rolled(east, -1)
    found = jnp.where(slot == 0, flux + first, -rolled(first, 1))
    found = jnp.where(slot < 0, beyond - jnp.where(slot == -1, last, 0.0), found)
    return jnp.where(slot < 2, own * found, 0.0)


def add_sides(get, correction, tl):
    lane = lane_ids()
    here = rolled(correction, -8 * tl)
    return get(0) + jnp.where(lane < 2, here, 0.0), get(1) + jnp.where(lane >= LANES - 2, here, 0.0)


def across_fold(x, index):
    picked = []
    for h in range(2):
        at = jnp.broadcast_to(index[:, h * LANES : (h + 1) * LANES], (SUB, LANES))
        low = lax.bitwise_and(at, LANES - 1)
        parts = [jnp.take_along_axis(x[j], low, axis=1) for j in range(2)]
        picked.append(jnp.where(at < LANES, parts[0], parts[1]))
    return picked


def row_corrections(state, offset, rows_a, rows_b, faces_a, faces_b, row_own, index, tall, levels, apply):
    even_lat = parity("lat")
    lat = lax.axis_index("lat")
    at_top = lat == lax.axis_size("lat") - 1
    at_bottom = lat == 0
    for t in range(TRACERS):
        part = [slice((depth * TRACERS + t) * levels, (depth * TRACERS + t + 1) * levels) for depth in range(2)]
        north, south = [], []
        for depth in range(2):
            one, other = rows_a[part[depth], :], rows_b[part[depth], :]
            upper = jnp.where(even_lat, one, other)
            lower = jnp.where(even_lat, other, one)
            lower = jnp.where(at_bottom, 0.0, lower)
            upper = [upper[:, h * LANES : (h + 1) * LANES] for h in range(2)]
            folded = across_fold(upper, index)
            north.append([jnp.where(at_top, folded[h], upper[h]) for h in range(2)])
            south.append([lower[:, h * LANES : (h + 1) * LANES] for h in range(2)])
        for h in range(2):
            cols = slice(h * LANES, (h + 1) * LANES)
            base = 2 * TRACERS * levels
            faces = []
            for comp in range(2):
                span = slice(base + comp * levels, base + (comp + 1) * levels)
                one = jnp.where(even_lat, faces_b[span, cols], faces_a[span, cols])
                faces.append(jnp.where(at_bottom, 0.0, one))
            kept = [row_own[j * levels : (j + 1) * levels, cols] for j in range(8)]
            bottom = [
                jnp.concatenate([state[t, k, h, offset + j : offset + j + 1, :] for k in range(levels)], axis=0)
                for j in range(2)
            ]
            a, b, g, up = face_terms(faces[0], faces[1])
            flux = a * south[0][h] + b * bottom[0] - g * jnp.where(up, south[1][h], bottom[1])
            first = jnp.maximum(0.125 * kept[0], 0.0) * south[0][h]
            row0 = kept[4] * (flux + first)
            row1 = -(kept[5] * first)
            a, b, g, up = face_terms(kept[2], kept[3])
            last = b * north[0][h] - jnp.minimum(g, 0.0) * north[1][h]
            before = -(jnp.minimum(0.125 * kept[1], 0.0) * north[0][h])
            row2 = -(kept[6] * before)
            row3 = kept[7] * (before - last)
            for k in range(levels):
                for at, add in ((0, row0), (1, row1), (tall - 2, row2), (tall - 1, row3)):
                    apply(t, k, h, at, add[k : k + 1, :])


def received(side_a, side_b, rows, even_lon):
    one, other = side_a[rows, :], side_b[rows, :]
    return jnp.where(even_lon, other, one), jnp.where(even_lon, one, other)


def add_rows(state, offset):
    def apply(t, k, h, at, add):
        spot = (t, k, h, slice(offset + at, offset + at + 1), slice(None))
        state[spot] = state[spot] + add

    return apply


def edge_kernel(
    got_a, got_b, sent, rows_a, rows_b, own, row_own, packed, index, before, c_in,
    c, next_side, next_rows_a, next_rows_b, correction,
):
    levels, tall = before.shape[1], own.shape[0]
    tiles = tall // SUB
    even_lon = parity("lon")

    def one_tile(r):
        rows = tile_rows(r)
        west, east = received(got_a, got_b, rows, even_lon)
        return side_correction(west, east, west, sent[rows, :], own[rows, :])

    def middle(r, carry):
        rows = tile_rows(r)
        found = one_tile(r)
        correction[rows, :] = found
        next_side[rows, :] = packed[rows, :] + found
        return carry

    lax.fori_loop(1, tiles - 1, middle, 0)
    row_corrections(before, PAD, rows_a, rows_b, rows_a, rows_b, row_own, index, tall, levels, add_rows(c, PAD))
    for r in (0, tiles - 1):
        rows = tile_rows(r)
        found = one_tile(r)
        correction[rows, :] = jnp.zeros((SUB, LANES), F32)
        fix_tile(c, r, found, levels)
        next_side[rows, :] = packed_edges(lambda t, k, h: c[t, k, h, tile_rows(r, PAD), :], levels)
    send_rows(c, next_rows_a, next_rows_b, levels, tall)


def fix_tile(c, r, found, levels):
    for t in range(TRACERS):
        for k in range(levels):
            new = add_sides(lambda h: c[t, k, h, tile_rows(r, PAD), :], found, t * levels + k)
            for h in range(2):
                c[t, k, h, tile_rows(r, PAD), :] = new[h]


def second_kernel(c_in, correction, terms, wet, mixing, c, out, south):
    levels, tall = wet.shape[0], wet.shape[2]
    tiles = tall // SUB
    for t in range(TRACERS):
        for k in range(levels):
            for h in range(2):
                south[t, k, h, 0:PAD, :] = jnp.zeros((PAD, LANES), F32)

    def body(r, carry):
        fix_tile(c, r + 1, correction[tile_rows(r + 1), :], levels)
        advance_tile(r, c, south, terms, wet, mixing, out, 0)
        return carry

    lax.fori_loop(0, tiles - 1, body, 0)
    advance_tile(tiles - 1, c, south, terms, wet, mixing, out, 0)


def last_kernel(
    got_a, got_b, sent, first_a, first_b, rows_a, rows_b, faces_a, faces_b, own, row_own, index, before, wet, c_in,
    fields, density, c, fields_out, density_out, sems,
):
    levels, tall = before.shape[1], own.shape[0]
    even_lon = parity("lon")
    row_corrections(before, PAD, rows_a, rows_b, faces_a, faces_b, row_own, index, tall, levels, add_rows(c, 0))

    def body(r, carry):
        rows = tile_rows(r)
        west, east = received(got_a, got_b, rows, even_lon)
        faces, _ = received(first_a, first_b, rows, even_lon)
        found = side_correction(west, east, faces, sent[rows, :], own[rows, :])
        for k in range(levels):
            new = [add_sides(lambda h: c[t, k, h, rows, :], found, t * levels + k) for t in range(TRACERS)]
            for h in range(2):
                for t in range(TRACERS):
                    fields_out[t, k, h, rows, :] = new[t][h]
                heat, salt = new[0][h], new[1][h]
                density_out[k, h, rows, :] = wet[k, h, rows, :] * (0.8 * salt - 0.2 * heat - 0.05 * heat * heat)
        return carry

    cuts = [0, 40, 80, 120, tall]
    copies = []
    for i, (lo, hi) in enumerate(zip(cuts[:-1], cuts[1:])):
        lax.fori_loop(lo // SUB, hi // SUB, body, 0)
        for h in range(2):
            cols = slice(h * LANES, (h + 1) * LANES)
            copies.append(
                pltpu.make_async_copy(
                    fields_out.at[:, :, h, lo:hi, :], fields.at[:, :, lo:hi, cols], sems.at[4 * i + h]
                )
            )
            copies.append(
                pltpu.make_async_copy(
                    density_out.at[:, h, lo:hi, :], density.at[:, lo:hi, cols], sems.at[4 * i + 2 + h]
                )
            )
        for one in copies[-4:]:
            one.start()
    for one in copies:
        one.wait()


def vmem(*shape, dtype=F32):
    return pltpu.VMEM(shape, dtype)


ON_CHIP = pl.BlockSpec(memory_space=pltpu.VMEM)
ANYWHERE = pl.BlockSpec(memory_space=pltpu.HBM)
SCALARS = pl.BlockSpec(memory_space=pltpu.SMEM)


def call(kernel, ins, out_shape, out_specs, scratch, cost, aliases=None):
    return pl.pallas_call(
        kernel,
        out_shape=out_shape,
        in_specs=ins,
        out_specs=out_specs,
        scratch_shapes=scratch,
        input_output_aliases=aliases or {},
        cost_estimate=pl.CostEstimate(flops=cost[0], bytes_accessed=cost[1], transcendentals=0),
        compiler_params=pltpu.CompilerParams(vmem_limit_bytes=VMEM_BYTES),
    )


def pairings(lats, lons):
    place = lambda a, o: (a % lats) * lons + o % lons
    by = {"lon_a": [], "lon_b": [], "lat_a": [], "lat_b": []}
    for a in range(lats):
        for o in range(lons):
            me = place(a, o)
            by["lon_a"].append((me, place(a, o ^ 1)))
            by["lon_b"].append((me, place(a, o + 1 if o % 2 else o - 1)))
            by["lat_a"].append((me, place(a ^ 1, o)))
            if a == lats - 1:
                other = place(a, lons - 1 - o)
            elif a == 0:
                other = place(a, o ^ 1)
            else:
                other = place(a + 1 if a % 2 else a - 1, o)
            by["lat_b"].append((me, other))
    return by


def on_device(pairs, tracers, east_faces, north_faces, land_mask, fold_partner, vert_mix):
    _, levels, tall, wide = tracers.shape
    assert wide == 2 * LANES and TRACERS * levels * 8 == LANES and tall % SUB == 0
    index = (fold_partner & (wide - 1)).reshape(1, wide)
    both = ("lat", "lon")
    swap = lambda x, name: lax.ppermute(x, both, pairs[name])
    tracers, east_faces, north_faces, land_mask = (
        pltpu.with_memory_space_constraint(x, pltpu.HBM) for x in (tracers, east_faces, north_faces, land_mask)
    )
    state = vmem(TRACERS, levels, 2, tall + 2 * PAD, LANES)
    side, rows3, rows2 = vmem(tall, LANES), vmem(6 * levels, wide), vmem(4 * levels, wide)
    faces = vmem(2, levels, 2, tall, LANES)
    level = vmem(levels, 2, tall, LANES)
    grid_bytes = tracers.size * 4

    c0, sent, rows_a, rows_b = call(
        start_kernel,
        [ANYWHERE] * 3,
        [state, side, rows3, rows3],
        [ON_CHIP] * 4,
        [vmem(2, levels, tall, LANES), vmem(2, levels, SUB, wide), pltpu.SemaphoreType.DMA((13,))],
        (1000000, 2 * grid_bytes),
    )(tracers, east_faces, north_faces)
    got_a, got_b = swap(sent, "lon_a"), swap(sent, "lon_b")
    got_rows_a, got_rows_b = swap(rows_a, "lat_a"), swap(rows_b, "lat_b")
    c1, packed, own, row_own, terms, wet, mixing = call(
        inner_kernel,
        [ON_CHIP, ANYWHERE, ANYWHERE, ANYWHERE, SCALARS],
        [state, side, side, vmem(8 * levels, wide), vmem(2, 3, levels, 2, tall, LANES), level,
         vmem(levels - 1, 2, tall, LANES)],
        [ON_CHIP] * 7,
        [faces, faces, vmem(levels, 2, tall, LANES, dtype=jnp.int32),
         vmem(TRACERS, levels, 2, tall + PAD, LANES), pltpu.SemaphoreType.DMA((24,))],
        (40000000, 4 * grid_bytes),
    )(c0, east_faces, north_faces, land_mask, vert_mix)
    c1, next_side, next_rows_a, next_rows_b, correction = call(
        edge_kernel,
        [ON_CHIP] * 11,
        [state, side, rows2, rows2, side],
        [ON_CHIP] * 5,
        [],
        (1000000, 1000000),
        {10: 0},
    )(got_a, got_b, sent, got_rows_a, got_rows_b, own, row_own, packed, index, c0, c1)
    new_a, new_b = swap(next_side, "lon_a"), swap(next_side, "lon_b")
    new_rows_a, new_rows_b = swap(next_rows_a, "lat_a"), swap(next_rows_b, "lat_b")
    c1, c2 = call(
        second_kernel,
        [ON_CHIP] * 5,
        [state, vmem(TRACERS, levels, 2, tall, LANES)],
        [ON_CHIP] * 2,
        [vmem(TRACERS, levels, 2, tall + PAD, LANES)],
        (40000000, 4 * grid_bytes),
        {0: 0},
    )(c1, correction, terms, wet, mixing)
    fields, density, _ = call(
        last_kernel,
        [ON_CHIP] * 15,
        [
            jax.ShapeDtypeStruct(tracers.shape, F32),
            jax.ShapeDtypeStruct(land_mask.shape, F32),
            vmem(TRACERS, levels, 2, tall, LANES),
        ],
        [ANYWHERE, ANYWHERE, ON_CHIP],
        [vmem(TRACERS, levels, 2, tall, LANES), level, pltpu.SemaphoreType.DMA((16,))],
        (4000000, 2 * grid_bytes),
        {14: 2},
    )(
        new_a, new_b, next_side, got_a, got_b, new_rows_a, new_rows_b, got_rows_a, got_rows_b,
        own, row_own, index, c1, wet, c2,
    )
    return fields, density


def solution(mesh):
    in_specs = (
        P(None, None, "lat", "lon"),
        P(None, None, "lat", "lon"),
        P(None, None, "lat", "lon"),
        P(None, "lat", "lon"),
        P("lon"),
        P(),
    )
    out_specs = (P(None, None, "lat", "lon"), P(None, "lat", "lon"))
    pairs = pairings(mesh.shape["lat"], mesh.shape["lon"])

    def body(*args):
        return on_device(pairs, *args)

    return jax.shard_map(body, mesh=mesh, in_specs=in_specs, out_specs=out_specs, check_vma=False)
```

time: 67.2 us -> 45.8 us (0.68)
  Pallas kernels: 45 us -> 29.4 us
  local copies, waits for them, and re-layouts: 6.26 us -> 0.01 us
    pallas_call x4, Pallas kernels: 30.7 us -> 19.9 us  [the longest x1 6.92 us: on_device(): call(second_kernel, [ON_CHIP] * 5, [state, vmem(TRACERS, levels, 2, tall,...]
    unnamed x18 -> x4, local copies, waits for them, and re-layouts: 6.26 us -> 0.01 us
    pallas_call x1, Pallas kernels: 14.3 us -> 9.47 us  [on_device(): call(inner_kernel, [ON_CHIP, ANYWHERE, ANYWHERE, ANYWHERE, SCALARS], [sta...]
  transfers between devices with their start and end apart: 8 -> 8, of which waited for: 0 -> 0; matrix products, arithmetic and copies ran while one was open for 0% -> 0% of each run, Pallas kernels for 38% -> 36%
where the time goes in v2:
time: 45.8 us; the launch traced here: 45.7 us
  Pallas kernels  29.4 us (64%)
  starting transfers between devices  15.5 us (34%)
  between operations  0.73 us (2%)
    ppermute x8, starting transfers between devices, on_device(): swap = lambda x, name: lax.ppermute(x, both, pairs[name])  15.5 us
    pallas_call x1, Pallas kernels, on_device(): call(inner_kernel, [ON_CHIP, ANYWHERE, ANYWHERE, ANYWHERE, SCALARS], [sta...  9.47 us
    pallas_call x1, Pallas kernels, on_device(): call(second_kernel, [ON_CHIP] * 5, [state, vmem(TRACERS, levels, 2, tall,...  6.92 us
    pallas_call x1, Pallas kernels, on_device(): call(last_kernel, [ON_CHIP] * 15, [jax.ShapeDtypeStruct(tracers.shape, F3...  5.73 us
    pallas_call x1, Pallas kernels, on_device(): call(start_kernel, [ANYWHERE] * 3, [state, side, rows3, rows3], [ON_CHIP]...  4.43 us
    pallas_call x1, Pallas kernels, on_device(): call(edge_kernel, [ON_CHIP] * 11, [state, side, rows2, rows2, side], [ON_...  2.85 us
  transfers between devices with their start and end apart: 8, of which 0 were waited for; matrix products, arithmetic and copies ran while one was open for 0% of the time, Pallas kernels for 36%

profile of v2, /device:TPU:1, one launch (start us, length us, event | category | flops | bytes accessed | tf_op | source)
XLA Modules:
  0.0 45.7 jit_solution(2445704845207261454)
XLA Ops:
  0.6 0.0 copy-start.1
  0.6 0.0 copy-start
  0.6 4.4 %shard_map.77 = (f32[2,8,2,168,128]{4,3,2,1,0:T(8,128)S(1)}, f32[152,128]{1,0:T(8,128)S(1)}, f32[48,256]{1,0:T(8,128)S(1)}, f32[48,256]{1,0:T(8,128)S(1)}) custom-call(f32[2,8,152,256]{3,2,1,0:T(8,128)} %tracers.1, f32[2,8,152,256]{3,2,1,0:T(8,128)} %east.3, f32[2,8,152,256]{3,2,1,0:T(8,128)} %north.3), custom_call_target="tpu_custom_call" | custom-call | flops 1000000 | bytes 4980736 | tf_op jit(solution)/shard_map/pallas_call | solution.py:510
  5.1 7.4 %collective-permute-start.1 = (f32[152,128]{1,0:T(8,128)S(1)}, f32[152,128]{1,0:T(8,128)S(1)}, u32[]{:S(2)}, u32[]{:S(2)}) collective-permute-start(f32[152,128]{1,0:T(8,128)S(1)} %get-tuple-element.22.sent), channel_id=1, source_target_pairs={{0,15},{1,2},{2,1},{3,4},{4,3},{5,6},{6,5},{7,8},{8,7},{9,10},{10,... | collective-permute-start | bytes 233480 | tf_op jit(solution)/shard_map/ppermute | solution.py:500
  12.5 0.0 collective-permute-start
  12.5 1.0 %collective-permute-start.2 = (f32[48,256]{1,0:T(8,128)S(1)}, f32[48,256]{1,0:T(8,128)S(1)}, u32[]{:S(2)}, u32[]{:S(2)}) collective-permute-start(f32[48,256]{1,0:T(8,128)S(1)} %get-tuple-element.23), channel_id=1, source_target_pairs={{0,16},{1,17},{2,18},{3,19},{4,20},{5,21},{6,22},{7,23},{8,24},{9,... | collective-permute-start | bytes 147464 | tf_op jit(solution)/shard_map/ppermute | solution.py:500
  13.5 2.3 %collective-permute-start.3 = (f32[48,256]{1,0:T(8,128)S(1)}, f32[48,256]{1,0:T(8,128)S(1)}, u32[]{:S(2)}, u32[]{:S(2)}) collective-permute-start(f32[48,256]{1,0:T(8,128)S(1)} %get-tuple-element.24), channel_id=1, source_target_pairs={{0,1},{1,0},{2,3},{3,2},{4,5},{5,4},{6,7},{7,6},{8,9},{9,8},{10,11... | collective-permute-start | bytes 147464 | tf_op jit(solution)/shard_map/ppermute | solution.py:500
  15.8 0.0 copy-done.1
  15.8 0.0 copy-done
  15.8 9.5 %shard_map.78 = (f32[2,8,2,168,128]{4,3,2,1,0:T(8,128)S(1)}, f32[152,128]{1,0:T(8,128)S(1)}, f32[152,128]{1,0:T(8,128)S(1)}, f32[64,256]{1,0:T(8,128)S(1)}, f32[...) custom-call(f32[2,8,2,168,128]{4,3,2,1,0:T(8,128)S(1)} %get-tuple-element.25.c.bef, ...), custom_call_target="tpu_custom_call" | custom-call | flops 40000000 | bytes 9961472 | tf_op jit(solution)/shard_map/pallas_call | solution.py:520
  25.3 0.0 collective-permute-done.2.rows_a.faces_a
  25.3 0.0 collective-permute-done.3.rows_b.faces_b
  25.3 0.0 collective-permute-done.1.got_b.first_b
  25.3 0.0 collective-permute-done.got_a.first_a
  25.3 2.9 %shard_map.79 = (f32[2,8,2,168,128]{4,3,2,1,0:T(8,128)S(1)}, f32[152,128]{1,0:T(8,128)S(1)}, f32[32,256]{1,0:T(8,128)S(1)}, f32[32,256]{1,0:T(8,128)S(1)}, f32[152,128]{1,0:T(8,128)S(1)}) custom-call(f32[152,128]{1,0:T(8,128)S(1)} %collective-permute-done.got_a.first_a, ...), custom_call_target="tpu_custom_call", output_to_operand_aliasing={{0}: (10, {})} | custom-call | flops 1000000 | bytes 1000000 | tf_op jit(solution)/shard_map/pallas_call | solution.py:530
  28.2 1.7 %collective-permute-start.5 = (f32[152,128]{1,0:T(8,128)S(1)}, f32[152,128]{1,0:T(8,128)S(1)}, u32[]{:S(2)}, u32[]{:S(2)}) collective-permute-start(f32[152,128]{1,0:T(8,128)S(1)} %get-tuple-element.30.sent), channel_id=1, source_target_pairs={{0,15},{1,2},{2,1},{3,4},{4,3},{5,6},{6,5},{7,8},{8,7},{9,10},{10,... | collective-permute-start | bytes 233480 | tf_op jit(solution)/shard_map/ppermute | solution.py:500
  29.9 0.0 collective-permute-start.4
  29.9 0.0 collective-permute-start.6
  29.9 3.1 %collective-permute-start.7 = (f32[32,256]{1,0:T(8,128)S(1)}, f32[32,256]{1,0:T(8,128)S(1)}, u32[]{:S(2)}, u32[]{:S(2)}) collective-permute-start(f32[32,256]{1,0:T(8,128)S(1)} %get-tuple-element.32), channel_id=1, source_target_pairs={{0,1},{1,0},{2,3},{3,2},{4,5},{5,4},{6,7},{7,6},{8,9},{9,8},{10,11... | collective-permute-start | bytes 98312 | tf_op jit(solution)/shard_map/ppermute | solution.py:500
  33.0 6.9 %shard_map.80 = (f32[2,8,2,168,128]{4,3,2,1,0:T(8,128)S(1)}, f32[2,8,2,152,128]{4,3,2,1,0:T(8,128)S(1)}) custom-call(f32[2,8,2,168,128]{4,3,2,1,0:T(8,128)S(1)} %get-tuple-element.33.c_in, f32[152,128]{1,0:T(8,128)S(1)} %get-tuple-element.34.correction, f32[2,3,8,2,152,128]{5,4,3,2,1,0:T(8,128)S(1)} %get-tuple-element.35.terms, ...), custom_call_target="tpu_custom_call", output_to_operand_aliasing={{0}: (0, {})} | custom-call | flops 40000000 | bytes 9961472 | tf_op jit(solution)/shard_map/pallas_call | solution.py:541
  39.9 0.0 collective-permute-done.6.rows_a
  39.9 0.0 collective-permute-done.7.rows_b
  39.9 0.0 collective-permute-done.5.got_b
  39.9 0.0 collective-permute-done.4.got_a
  40.0 5.7 %shard_map.81 = (f32[2,8,152,256]{3,2,1,0:T(8,128)}, f32[8,152,256]{2,1,0:T(8,128)}, f32[2,8,2,152,128]{4,3,2,1,0:T(8,128)S(1)}) custom-call(f32[152,128]{1,0:T(8,128)S(1)} %collective-permute-done.4.got_a, f32[152,128]{1,0:T(8,128)S(1)} %collective-permute-done.5.got_b, f32[152,128]{1,0:T(8,128)S(1)} %get-tuple-element.30.sent, ...), custom_call_target="tpu_custom_call", output_to_operand_aliasing={{2}: (14, {})} | custom-call | flops 4000000 | bytes 4980736 | tf_op jit(solution)/shard_map/pallas_call | solution.py:550
  (1 shorter events, 0.0 us)
Async XLA Ops:
  0.6 15.2 %copy-start.1 = (s32[256]{0:T(256)S(1)}, s32[256]{0:T(256)}, u32[]{:S(2)}) copy-start(s32[256]{0:T(256)} %param.10) | copy-start | bytes 3076
  0.6 15.2 %copy-start = (f32[7]{0:T(128)S(1)}, f32[7]{0:T(128)}, u32[]{:S(2)}) copy-start(f32[7]{0:T(128)} %mix.1) | copy-start | bytes 88
  5.1 20.2 %collective-permute-start.1 = (f32[152,128]{1,0:T(8,128)S(1)}, f32[152,128]{1,0:T(8,128)S(1)}, u32[]{:S(2)}, u32[]{:S(2)}) collective-permute-start(f32[152,128]{1,0:T(8,128)S(1)} %get-tuple-element.22.sent), channel_id=1, source_target_pairs={{0,15},{1,2},{2,1},{3,4},{4,3},{5,6},{6,5},{7,8},{8,7},{9,10},{10,... | collective-permute-start | bytes 233480 | tf_op jit(solution)/shard_map/ppermute | solution.py:500
  12.5 12.8 %collective-permute-start = (f32[152,128]{1,0:T(8,128)S(1)}, f32[152,128]{1,0:T(8,128)S(1)}, u32[]{:S(2)}, u32[]{:S(2)}) collective-permute-start(f32[152,128]{1,0:T(8,128)S(1)} %get-tuple-element.22.sent), channel_id=1, source_target_pairs={{0,1},{1,0},{2,3},{3,2},{4,5},{5,4},{6,7},{7,6},{8,9},{9,8},{10,11... | collective-permute-start | bytes 233480 | tf_op jit(solution)/shard_map/ppermute | solution.py:500
  12.5 12.8 %collective-permute-start.2 = (f32[48,256]{1,0:T(8,128)S(1)}, f32[48,256]{1,0:T(8,128)S(1)}, u32[]{:S(2)}, u32[]{:S(2)}) collective-permute-start(f32[48,256]{1,0:T(8,128)S(1)} %get-tuple-element.23), channel_id=1, source_target_pairs={{0,16},{1,17},{2,18},{3,19},{4,20},{5,21},{6,22},{7,23},{8,24},{9,... | collective-permute-start | bytes 147464 | tf_op jit(solution)/shard_map/ppermute | solution.py:500
  13.5 11.8 %collective-permute-start.3 = (f32[48,256]{1,0:T(8,128)S(1)}, f32[48,256]{1,0:T(8,128)S(1)}, u32[]{:S(2)}, u32[]{:S(2)}) collective-permute-start(f32[48,256]{1,0:T(8,128)S(1)} %get-tuple-element.24), channel_id=1, source_target_pairs={{0,1},{1,0},{2,3},{3,2},{4,5},{5,4},{6,7},{7,6},{8,9},{9,8},{10,11... | collective-permute-start | bytes 147464 | tf_op jit(solution)/shard_map/ppermute | solution.py:500
  28.2 11.8 %collective-permute-start.5 = (f32[152,128]{1,0:T(8,128)S(1)}, f32[152,128]{1,0:T(8,128)S(1)}, u32[]{:S(2)}, u32[]{:S(2)}) collective-permute-start(f32[152,128]{1,0:T(8,128)S(1)} %get-tuple-element.30.sent), channel_id=1, source_target_pairs={{0,15},{1,2},{2,1},{3,4},{4,3},{5,6},{6,5},{7,8},{8,7},{9,10},{10,... | collective-permute-start | bytes 233480 | tf_op jit(solution)/shard_map/ppermute | solution.py:500
  29.9 10.1 %collective-permute-start.4 = (f32[152,128]{1,0:T(8,128)S(1)}, f32[152,128]{1,0:T(8,128)S(1)}, u32[]{:S(2)}, u32[]{:S(2)}) collective-permute-start(f32[152,128]{1,0:T(8,128)S(1)} %get-tuple-element.30.sent), channel_id=1, source_target_pairs={{0,1},{1,0},{2,3},{3,2},{4,5},{5,4},{6,7},{7,6},{8,9},{9,8},{10,11... | collective-permute-start | bytes 233480 | tf_op jit(solution)/shard_map/ppermute | solution.py:500
  29.9 10.1 %collective-permute-start.6 = (f32[32,256]{1,0:T(8,128)S(1)}, f32[32,256]{1,0:T(8,128)S(1)}, u32[]{:S(2)}, u32[]{:S(2)}) collective-permute-start(f32[32,256]{1,0:T(8,128)S(1)} %get-tuple-element.31), channel_id=1, source_target_pairs={{0,16},{1,17},{2,18},{3,19},{4,20},{5,21},{6,22},{7,23},{8,24},{9,... | collective-permute-start | bytes 98312 | tf_op jit(solution)/shard_map/ppermute | solution.py:500
  29.9 10.1 %collective-permute-start.7 = (f32[32,256]{1,0:T(8,128)S(1)}, f32[32,256]{1,0:T(8,128)S(1)}, u32[]{:S(2)}, u32[]{:S(2)}) collective-permute-start(f32[32,256]{1,0:T(8,128)S(1)} %get-tuple-element.32), channel_id=1, source_target_pairs={{0,1},{1,0},{2,3},{3,2},{4,5},{5,4},{6,7},{7,6},{8,9},{9,8},{10,11... | collective-permute-start | bytes 98312 | tf_op jit(solution)/shard_map/ppermute | solution.py:500

commit v3 on v2

--- a/solution.py
+++ b/solution.py
@@ -10,7 +10,7 @@
 SUB = 8
 PAD = 8
 TRACERS = 2
-VMEM_BYTES = 12 * 1024 * 1024
+VMEM_BYTES = 14 * 1024 * 1024
 
 
 def lane_ids():
@@ -31,6 +31,8 @@
 
 
 def tile_rows(index, offset=0):
+    if isinstance(index, int):
+        return pl.ds(index * SUB + offset, SUB)
     return pl.ds(pl.multiple_of(index * SUB, SUB) + offset, SUB)
 
 
@@ -95,6 +97,97 @@
                 out[t, k, h, tile_rows(r, out_pad), :] = c0[h] + wet[k, h, rows, :] * change
 
 
+class Step:
+    def __init__(self, c, east_next, east_far, along, south, terms, wet, mixing, out, out_pad):
+        self.c, self.east_next, self.east_far, self.along, self.south = c, east_next, east_far, along, south
+        self.terms, self.wet, self.mixing, self.out, self.out_pad = terms, wet, mixing, out, out_pad
+        self.levels = wet.shape[0]
+        self.below = {}
+
+    def cells(self, t, k, h, i, ahead, by=0):
+        return self.c[t, k, h, tile_rows(i, PAD + ahead * SUB + by), :]
+
+    def neighbours(self, i, ahead, k, t):
+        lane = lane_ids()
+        first, last, last2 = lane > 0, lane < LANES - 1, lane < LANES - 2
+        rows = tile_rows(i, ahead * SUB)
+        c0 = [self.cells(t, k, h, i, ahead) for h in range(2)]
+        plus1 = [rolled(x, -1) for x in c0]
+        plus2 = [rolled(x, -2) for x in c0]
+        minus1 = [rolled(x, 1) for x in c0]
+        p1 = jnp.where(last, plus1[0], plus1[1]), jnp.where(last, plus1[1], 0.0)
+        p2 = jnp.where(last2, plus2[0], plus2[1]), jnp.where(last2, plus2[1], 0.0)
+        m1 = jnp.where(first, minus1[0], 0.0), jnp.where(first, minus1[1], minus1[0])
+        for h in range(2):
+            self.east_next[t, k, h, rows, :] = p1[h]
+            self.east_far[t, k, h, rows, :] = jnp.where(self.terms[0, 2, k, h, rows, :] > 0.0, m1[h], p2[h])
+
+    def fluxes(self, i, ahead, k, t):
+        first = lane_ids() > 0
+        rows = tile_rows(i, ahead * SUB)
+        flux = []
+        for h in range(2):
+            a, b, g = (self.terms[0, j, k, h, rows, :] for j in range(3))
+            flux.append(
+                a * self.cells(t, k, h, i, ahead)
+                + b * self.east_next[t, k, h, rows, :]
+                - g * self.east_far[t, k, h, rows, :]
+            )
+        shifted = [rolled(x, 1) for x in flux]
+        west = jnp.where(first, shifted[0], 0.0), jnp.where(first, shifted[1], shifted[0])
+        for h in range(2):
+            self.along[t, k, h, rows, :] = west[h] - flux[h]
+            a, b, g = (self.terms[1, j, k, h, rows, :] for j in range(3))
+            further = jnp.where(g > 0.0, self.cells(t, k, h, i, ahead, -1), self.cells(t, k, h, i, ahead, 2))
+            self.south[t, k, h, tile_rows(i, PAD + ahead * SUB), :] = (
+                a * self.cells(t, k, h, i, ahead) + b * self.cells(t, k, h, i, ahead, 1) - g * further
+            )
+
+    def finish(self, i, ahead, k, t):
+        rows = tile_rows(i, ahead * SUB)
+        for h in range(2):
+            c0 = self.cells(t, k, h, i, ahead)
+            change = self.along[t, k, h, rows, :] + (
+                self.south[t, k, h, tile_rows(i, PAD + ahead * SUB - 1), :]
+                - self.south[t, k, h, tile_rows(i, PAD + ahead * SUB), :]
+            )
+            if k > 0:
+                change = change - self.below[t, h]
+            if k + 1 < self.levels:
+                self.below[t, h] = self.mixing[k, h, rows, :] * (self.cells(t, k + 1, h, i, ahead) - c0)
+                change = change + self.below[t, h]
+            place = tile_rows(i, self.out_pad + ahead * SUB)
+            self.out[t, k, h, place, :] = c0 + self.wet[k, h, rows, :] * change
+
+    def turn(self, i, tiles, before=None, after=None):
+        inside = lambda ahead: 0 <= i + ahead < tiles
+        packs = after(i, -3) if after is not None and inside(-3) else None
+        for k in range(self.levels):
+            for t in range(TRACERS):
+                if inside(-2):
+                    self.finish(i, -2, k, t)
+                if inside(-1):
+                    self.fluxes(i, -1, k, t)
+                if inside(0):
+                    self.neighbours(i, 0, k, t)
+                if before is not None and inside(1):
+                    before(i, 1, k, t)
+            if packs is not None:
+                packs(k)
+
+
+WINDOW = 5
+
+
+def windows(i, refs, more):
+    start = pl.multiple_of((i - 3) * SUB, SUB)
+    seen = []
+    for ref, rows in zip(refs, more):
+        before = (slice(None),) * (len(ref.shape) - 2)
+        seen.append(ref.at[before + (pl.ds(start, WINDOW * SUB + rows), slice(None))])
+    return seen
+
+
 def group(tl):
     lane = lane_ids()
     return lax.bitwise_and(lax.shift_right_logical(lane + 2, 3), LANES // SUB - 1) == tl
@@ -121,7 +214,7 @@
     return lax.rem(lax.axis_index(axis), 2) == 0
 
 
-def start_kernel(tracers, east, north, c, side, rows_a, rows_b, east_last, north_top, sems):
+def start_kernel(tracers, east, north, c, side, side_again, rows_a, rows_b, east_last, north_top, sems):
     levels, tall = tracers.shape[1], tracers.shape[2]
     cuts = [0, 40, 80, 120, tall]
     copies = []
@@ -161,12 +254,13 @@
                 jnp.where(lane == 2, rolled(east_last[0, k, rows, :], 3), rolled(east_last[1, k, rows, :], 4))
             )
         side[rows, :] = packed_edges(lambda t, k, h: c[t, k, h, tile_rows(r, PAD), :], levels, faces)
+        side_again[rows, :] = side[rows, :]
         return carry
 
     for i, (lo, hi) in enumerate(zip(cuts[:-1], cuts[1:])):
         for one in copies[i]:
             one.wait()
-        lax.fori_loop(lo // SUB, hi // SUB, pack, 0)
+        lax.fori_loop(lo // SUB, hi // SUB, pack, 0, unroll=True)
     top_copy.wait()
     send_rows(c, rows_a, rows_b, levels, tall)
     for comp in range(2):
@@ -192,11 +286,9 @@
                     rows_b[tl : tl + 1, cols] = c[t, k, h, pl.ds(at_b, 1), :]
 
 
-def inner_kernel(c, east, north, mask, mix, out, packed, own, row_own, terms, wet, mixing, east_in, north_in, mask_in, south, sems):
-    levels, tall = mask.shape[0], mask.shape[1]
-    cuts = [0, 24, 64, 104, tall]
+def inner_copies(pieces, east, north, mask, east_in, north_in, mask_in, sems):
     copies = []
-    for i, (lo, hi) in enumerate(zip(cuts[:-1], cuts[1:])):
+    for i, (lo, hi) in enumerate(pieces):
         group_of = []
         for h in range(2):
             cols = slice(h * LANES, (h + 1) * LANES)
@@ -212,47 +304,127 @@
                 )
             )
         copies.append(group_of)
+    return copies
+
+
+def clear(ref, rows):
+    for t in range(TRACERS):
+        for k in range(ref.shape[1]):
+            for h in range(2):
+                ref[t, k, h, rows, :] = jnp.zeros((PAD, LANES), F32)
+
+
+def inner_tile(r, c, mix, out, packed, own, terms, wet, mixing, south, east_in, north_in, mask_in):
+    levels = wet.shape[0]
+    lane = lane_ids()
+    rows = tile_rows(r)
+    set_terms(r, east_in, north_in, mask_in, mix, terms, wet, mixing)
+    advance_tile(r, c, south, terms, wet, mixing, out, PAD)
+    packed[rows, :] = packed_edges(lambda t, k, h: out[t, k, h, tile_rows(r, PAD), :], levels)
+    kept = jnp.zeros((SUB, LANES), F32)
+    edge = lane >= LANES - 2
+    for k in range(levels):
+        one = jnp.where(edge, wet[k, 1, rows, :], wet[k, 0, rows, :])
+        g = jnp.where(edge, terms[0, 2, k, 1, rows, :], terms[0, 2, k, 0, rows, :])
+        some = jnp.where(lane == 5, rolled(terms[0, 1, k, 1, rows, :], 6), rolled(g, 4))
+        one = jnp.where(jnp.logical_and(lane >= 2, lane < 6), some, one)
+        kept = jnp.where(group(k), rolled(one, 8 * k), kept)
+    own[rows, :] = jnp.where(jnp.logical_or(lane < LANES // 2 - 2, edge), kept, rolled(kept, LANES // 2))
+
+
+FIRST_PIECES = ((0, 24), (24, 64))
+REST_PIECES = ((64, 88), (88, 120), (120, 152))
+
+
+def share(parts):
+    place = lax.axis_index("lon") // 2
+    amount = jnp.int32(0)
+    for i, part in enumerate(parts):
+        amount = jnp.where(place == i, part, amount)
+    return amount
+
+
+EARLY_TILES = (8, 5, 3, 2)
+EARLY_TURNS = (10, 6, 3, 1)
+
+
+def early_kernel(
+    c, east, north, mask, mix, side_in, rows_in,
+    out, packed, own, terms, wet, mixing, south, side, rows_b, east_in, north_in, mask_in, sems,
+):
+    count = share(EARLY_TILES)
+
+    @pl.when(count > 0)
+    def _():
+        clear(south, slice(0, PAD))
+        run_pieces(
+            FIRST_PIECES, c, east, north, mask, mix, out, packed, own, terms, wet, mixing, south,
+            east_in, north_in, mask_in, sems, count,
+        )
+
+
+def run_pieces(
+    pieces, c, east, north, mask, mix, out, packed, own, terms, wet, mixing, south, east_in, north_in, mask_in, sems,
+    count,
+):
+    copies = inner_copies(pieces, east, north, mask, east_in, north_in, mask_in, sems)
+
+    def body(r, carry):
+        inner_tile(r, c, mix, out, packed, own, terms, wet, mixing, south, east_in, north_in, mask_in)
+        return carry
+
     for group_of in copies:
         for one in group_of:
             one.start()
-    for t in range(TRACERS):
-        for k in range(levels):
-            for h in range(2):
-                south[t, k, h, 0:PAD, :] = jnp.zeros((PAD, LANES), F32)
-                out[t, k, h, 0:PAD, :] = jnp.zeros((PAD, LANES), F32)
-                out[t, k, h, PAD + tall :, :] = jnp.zeros((PAD, LANES), F32)
-    lane = lane_ids()
+    for (lo, hi), group_of in zip(pieces, copies):
+        for one in group_of:
+            one.wait()
+        lax.fori_loop(lo // SUB, jnp.minimum(hi // SUB, count), body, 0)
+
+
+def inner_kernel(
+    c, east, north, mask, mix, out_in, packed_in, own_in, terms_in, wet_in, mixing_in, south_in,
+    out, packed, own, terms, wet, mixing, south, row_own, east_in, north_in, mask_in, sems,
+):
+    levels, tall = wet.shape[0], wet.shape[2]
+    done = share(EARLY_TILES)
+    clear(out, slice(0, PAD))
+    clear(out, slice(PAD + tall, PAD + tall + PAD))
+
+    @pl.when(done == 0)
+    def _():
+        clear(south, slice(0, PAD))
+
+    pieces = FIRST_PIECES + REST_PIECES
+    copies = inner_copies(pieces, east, north, mask, east_in, north_in, mask_in, sems)
 
     def body(r, carry):
-        rows = tile_rows(r)
-        set_terms(r, east_in, north_in, mask_in, mix, terms, wet, mixing)
-        advance_tile(r, c, south, terms, wet, mixing, out, PAD)
-        packed[rows, :] = packed_edges(lambda t, k, h: out[t, k, h, tile_rows(r, PAD), :], levels)
-        kept = jnp.zeros((SUB, LANES), F32)
-        edge = lane >= LANES - 2
-        for k in range(levels):
-            one = jnp.where(edge, wet[k, 1, rows, :], wet[k, 0, rows, :])
-            flow = jnp.where(edge, east_in[0, k, 1, rows, :], east_in[0, k, 0, rows, :])
-            some = jnp.where(lane == 5, rolled(east_in[1, k, 1, rows, :], 6), rolled(flow, 4))
-            one = jnp.where(jnp.logical_and(lane >= 2, lane < 6), some, one)
-            kept = jnp.where(group(k), rolled(one, 8 * k), kept)
-        own[rows, :] = jnp.where(
-            jnp.logical_or(lane < LANES // 2 - 2, edge), kept, rolled(kept, LANES // 2)
-        )
+        inner_tile(r, c, mix, out, packed, own, terms, wet, mixing, south, east_in, north_in, mask_in)
         return carry
 
-    for i, (lo, hi) in enumerate(zip(cuts[:-1], cuts[1:])):
-        for one in copies[i]:
-            one.wait()
-        lax.fori_loop(lo // SUB, hi // SUB, body, 0)
+    for (lo, hi), group_of in zip(pieces, copies):
+
+        @pl.when(done < hi // SUB)
+        def _(group_of=group_of):
+            for one in group_of:
+                one.start()
+
+    for (lo, hi), group_of in zip(pieces, copies):
+
+        @pl.when(done < hi // SUB)
+        def _(lo=lo, hi=hi, group_of=group_of):
+            for one in group_of:
+                one.wait()
+            lax.fori_loop(jnp.maximum(lo // SUB, done), hi // SUB, body, 0)
+
     for k in range(levels):
         for h in range(2):
             cols = slice(h * LANES, (h + 1) * LANES)
             kept_rows = (
-                north_in[0, k, h, 0:1, :],
-                north_in[0, k, h, tall - 2 : tall - 1, :],
-                north_in[0, k, h, tall - 1 : tall, :],
-                north_in[1, k, h, tall - 1 : tall, :],
+                terms[1, 2, k, h, 0:1, :],
+                terms[1, 2, k, h, tall - 2 : tall - 1, :],
+                terms[1, 2, k, h, tall - 1 : tall, :],
+                terms[1, 1, k, h, tall - 1 : tall, :],
                 wet[k, h, 0:1, :],
                 wet[k, h, 1:2, :],
                 wet[k, h, tall - 2 : tall - 1, :],
@@ -267,11 +439,10 @@
     a, b, g, up = face_terms(rolled(faces, -2), rolled(faces, -3))
     near = rolled(west, 1)
     flux = a * near + b * mine - g * jnp.where(up, rolled(west, 2), rolled(mine, -1))
-    flow = 0.125 * rolled(own, -4)
-    first = jnp.maximum(flow, 0.0) * near
-    _, b, _, _ = face_terms(rolled(own, -4), rolled(own, -6))
-    beyond = jnp.minimum(flow, 0.0) * rolled(east, -2)
-    last = rolled(beyond, 1) + b * rolled(east, -1)
+    mine_g = rolled(own, -4)
+    first = jnp.maximum(mine_g, 0.0) * near
+    beyond = jnp.minimum(mine_g, 0.0) * rolled(east, -2)
+    last = rolled(beyond, 1) + rolled(own, -6) * rolled(east, -1)
     found = jnp.where(slot == 0, flux + first, -rolled(first, 1))
     found = jnp.where(slot < 0, beyond - jnp.where(slot == -1, last, 0.0), found)
     return jnp.where(slot < 2, own * found, 0.0)
@@ -287,6 +458,7 @@
     picked = []
     for h in range(2):
         at = jnp.broadcast_to(index[:, h * LANES : (h + 1) * LANES], (SUB, LANES))
+        at = lax.bitwise_and(at, 2 * LANES - 1)
         low = lax.bitwise_and(at, LANES - 1)
         parts = [jnp.take_along_axis(x[j], low, axis=1) for j in range(2)]
         picked.append(jnp.where(at < LANES, parts[0], parts[1]))
@@ -325,12 +497,11 @@
             ]
             a, b, g, up = face_terms(faces[0], faces[1])
             flux = a * south[0][h] + b * bottom[0] - g * jnp.where(up, south[1][h], bottom[1])
-            first = jnp.maximum(0.125 * kept[0], 0.0) * south[0][h]
+            first = jnp.maximum(kept[0], 0.0) * south[0][h]
             row0 = kept[4] * (flux + first)
             row1 = -(kept[5] * first)
-            a, b, g, up = face_terms(kept[2], kept[3])
-            last = b * north[0][h] - jnp.minimum(g, 0.0) * north[1][h]
-            before = -(jnp.minimum(0.125 * kept[1], 0.0) * north[0][h])
+            last = kept[3] * north[0][h] - jnp.minimum(kept[2], 0.0) * north[1][h]
+            before = -(jnp.minimum(kept[1], 0.0) * north[0][h])
             row2 = -(kept[6] * before)
             row3 = kept[7] * (before - last)
             for k in range(levels):
@@ -353,7 +524,7 @@
 
 def edge_kernel(
     got_a, got_b, sent, rows_a, rows_b, own, row_own, packed, index, before, c_in,
-    c, next_side, next_rows_a, next_rows_b, correction,
+    c, next_side, next_side_again, next_rows_a, next_rows_b, correction,
 ):
     levels, tall = before.shape[1], own.shape[0]
     tiles = tall // SUB
@@ -369,16 +540,19 @@
         found = one_tile(r)
         correction[rows, :] = found
         next_side[rows, :] = packed[rows, :] + found
+        next_side_again[rows, :] = packed[rows, :] + found
         return carry
 
-    lax.fori_loop(1, tiles - 1, middle, 0)
+    lax.fori_loop(1, tiles - 1, middle, 0, unroll=True)
     row_corrections(before, PAD, rows_a, rows_b, rows_a, rows_b, row_own, index, tall, levels, add_rows(c, PAD))
     for r in (0, tiles - 1):
         rows = tile_rows(r)
         found = one_tile(r)
         correction[rows, :] = jnp.zeros((SUB, LANES), F32)
         fix_tile(c, r, found, levels)
-        next_side[rows, :] = packed_edges(lambda t, k, h: c[t, k, h, tile_rows(r, PAD), :], levels)
+        sides = packed_edges(lambda t, k, h: c[t, k, h, tile_rows(r, PAD), :], levels)
+        next_side[rows, :] = sides
+        next_side_again[rows, :] = sides
     send_rows(c, next_rows_a, next_rows_b, levels, tall)
 
 
@@ -390,21 +564,76 @@
                 c[t, k, h, tile_rows(r, PAD), :] = new[h]
 
 
-def second_kernel(c_in, correction, terms, wet, mixing, c, out, south):
+def second_turns(c, correction, terms, wet, mixing, out, south, east_next, east_far, along):
     levels, tall = wet.shape[0], wet.shape[2]
     tiles = tall // SUB
-    for t in range(TRACERS):
-        for k in range(levels):
+    whole = (c, east_next, east_far, along, south, terms, wet, mixing, out, correction)
+    more = (2 * PAD, 0, 0, 0, PAD, 0, 0, 0, 0, 0)
+
+    def turn(i, count, refs):
+        c, east_next, east_far, along, south, terms, wet, mixing, out, correction = refs
+        step = Step(c, east_next, east_far, along, south, terms, wet, mixing, out, 0)
+
+        def ready(i, ahead, k, t):
+            rows = tile_rows(i, PAD + ahead * SUB)
+            found = correction[tile_rows(i, ahead * SUB), :]
+            new = add_sides(lambda h: c[t, k, h, rows, :], found, t * levels + k)
             for h in range(2):
-                south[t, k, h, 0:PAD, :] = jnp.zeros((PAD, LANES), F32)
-
-    def body(r, carry):
-        fix_tile(c, r + 1, correction[tile_rows(r + 1), :], levels)
-        advance_tile(r, c, south, terms, wet, mixing, out, 0)
-        return carry
-
-    lax.fori_loop(0, tiles - 1, body, 0)
-    advance_tile(tiles - 1, c, south, terms, wet, mixing, out, 0)
+                c[t, k, h, rows, :] = new[h]
+
+        step.turn(i, count, ready)
+
+    def begin():
+        for t in range(TRACERS):
+            for k in range(levels):
+                for h in range(2):
+                    south[t, k, h, 0:PAD, :] = jnp.zeros((PAD, LANES), F32)
+        for i in range(-1, FIRST_TURN):
+            turn(i, tiles, whole)
+
+    def middle(lo, hi):
+        def body(i, carry):
+            turn(3, WINDOW, windows(i, whole, more))
+            return carry
+
+        lax.fori_loop(lo, hi, body, 0)
+
+    def end():
+        for i in range(tiles - 1, tiles + 2):
+            turn(i, tiles, whole)
+
+    return begin, middle, end
+
+
+FIRST_TURN = 3
+
+
+def second_early_kernel(
+    c_in, side_in, side_again_in, rows_a_in, rows_b_in, correction, terms, wet, mixing,
+    c, side, side_again, rows_a, rows_b, out, south, east_next, east_far, along,
+):
+    count = share(EARLY_TURNS)
+    begin, middle, _ = second_turns(c, correction, terms, wet, mixing, out, south, east_next, east_far, along)
+
+    @pl.when(count > 0)
+    def _():
+        begin()
+        middle(FIRST_TURN, FIRST_TURN + count)
+
+
+def second_kernel(
+    c_in, out_in, south_in, east_next_in, east_far_in, along_in, correction, terms, wet, mixing,
+    c, out, south, east_next, east_far, along,
+):
+    count = share(EARLY_TURNS)
+    begin, middle, end = second_turns(c, correction, terms, wet, mixing, out, south, east_next, east_far, along)
+
+    @pl.when(count == 0)
+    def _():
+        begin()
+
+    middle(FIRST_TURN + count, wet.shape[2] // SUB - 1)
+    end()
 
 
 def last_kernel(
@@ -432,7 +661,7 @@
     cuts = [0, 40, 80, 120, tall]
     copies = []
     for i, (lo, hi) in enumerate(zip(cuts[:-1], cuts[1:])):
-        lax.fori_loop(lo // SUB, hi // SUB, body, 0)
+        lax.fori_loop(lo // SUB, hi // SUB, body, 0, unroll=True)
         for h in range(2):
             cols = slice(h * LANES, (h + 1) * LANES)
             copies.append(
@@ -495,7 +724,7 @@
 def on_device(pairs, tracers, east_faces, north_faces, land_mask, fold_partner, vert_mix):
     _, levels, tall, wide = tracers.shape
     assert wide == 2 * LANES and TRACERS * levels * 8 == LANES and tall % SUB == 0
-    index = (fold_partner & (wide - 1)).reshape(1, wide)
+    index = fold_partner.reshape(1, wide)
     both = ("lat", "lon")
     swap = lambda x, name: lax.ppermute(x, both, pairs[name])
     tracers, east_faces, north_faces, land_mask = (
@@ -505,48 +734,72 @@
     side, rows3, rows2 = vmem(tall, LANES), vmem(6 * levels, wide), vmem(4 * levels, wide)
     faces = vmem(2, levels, 2, tall, LANES)
     level = vmem(levels, 2, tall, LANES)
+    grid = vmem(TRACERS, levels, 2, tall, LANES)
     grid_bytes = tracers.size * 4
 
-    c0, sent, rows_a, rows_b = call(
+    c0, sent, sent_again, rows_a, rows_b = call(
         start_kernel,
         [ANYWHERE] * 3,
-        [state, side, rows3, rows3],
-        [ON_CHIP] * 4,
+        [state, side, side, rows3, rows3],
+        [ON_CHIP] * 5,
         [vmem(2, levels, tall, LANES), vmem(2, levels, SUB, wide), pltpu.SemaphoreType.DMA((13,))],
         (1000000, 2 * grid_bytes),
     )(tracers, east_faces, north_faces)
-    got_a, got_b = swap(sent, "lon_a"), swap(sent, "lon_b")
-    got_rows_a, got_rows_b = swap(rows_a, "lat_a"), swap(rows_b, "lat_b")
-    c1, packed, own, row_own, terms, wet, mixing = call(
+    got_a, got_rows_a = swap(sent, "lon_a"), swap(rows_a, "lat_a")
+    assert REST_PIECES[-1][1] == tall
+    shared = [state, side, side, vmem(2, 3, levels, 2, tall, LANES), level, vmem(levels - 1, 2, tall, LANES),
+              vmem(TRACERS, levels, 2, tall + PAD, LANES)]
+    early_rows = FIRST_PIECES[-1][1]
+    *state_so_far, sent_again, rows_b = call(
+        early_kernel,
+        [ON_CHIP, ANYWHERE, ANYWHERE, ANYWHERE, SCALARS, ON_CHIP, ON_CHIP],
+        shared + [side, rows3],
+        [ON_CHIP] * 9,
+        [vmem(2, levels, 2, early_rows, LANES)] * 2
+        + [vmem(levels, 2, early_rows, LANES, dtype=jnp.int32), pltpu.SemaphoreType.DMA((12,))],
+        (10000000, grid_bytes),
+        {5: 7, 6: 8},
+    )(c0, east_faces, north_faces, land_mask, vert_mix, sent_again, rows_b)
+    got_b, got_rows_b = swap(sent_again, "lon_b"), swap(rows_b, "lat_b")
+    c1, packed, own, terms, wet, mixing, _, row_own = call(
         inner_kernel,
-        [ON_CHIP, ANYWHERE, ANYWHERE, ANYWHERE, SCALARS],
-        [state, side, side, vmem(8 * levels, wide), vmem(2, 3, levels, 2, tall, LANES), level,
-         vmem(levels - 1, 2, tall, LANES)],
-        [ON_CHIP] * 7,
-        [faces, faces, vmem(levels, 2, tall, LANES, dtype=jnp.int32),
-         vmem(TRACERS, levels, 2, tall + PAD, LANES), pltpu.SemaphoreType.DMA((24,))],
+        [ON_CHIP, ANYWHERE, ANYWHERE, ANYWHERE, SCALARS] + [ON_CHIP] * 7,
+        shared + [vmem(8 * levels, wide)],
+        [ON_CHIP] * 8,
+        [faces, faces, vmem(levels, 2, tall, LANES, dtype=jnp.int32), pltpu.SemaphoreType.DMA((30,))],
         (40000000, 4 * grid_bytes),
-    )(c0, east_faces, north_faces, land_mask, vert_mix)
-    c1, next_side, next_rows_a, next_rows_b, correction = call(
+        {5 + j: j for j in range(7)},
+    )(c0, east_faces, north_faces, land_mask, vert_mix, *state_so_far)
+    c1, next_side, next_again, next_rows_a, next_rows_b, correction = call(
         edge_kernel,
         [ON_CHIP] * 11,
-        [state, side, rows2, rows2, side],
-        [ON_CHIP] * 5,
+        [state, side, side, rows2, rows2, side],
+        [ON_CHIP] * 6,
         [],
         (1000000, 1000000),
         {10: 0},
     )(got_a, got_b, sent, got_rows_a, got_rows_b, own, row_own, packed, index, c0, c1)
-    new_a, new_b = swap(next_side, "lon_a"), swap(next_side, "lon_b")
+    kept = [grid, vmem(TRACERS, levels, 2, tall + PAD, LANES), grid, grid, grid]
+    c1, sent_side, sent_side_again, next_rows_a, next_rows_b, *kept_so_far = call(
+        second_early_kernel,
+        [ON_CHIP] * 9,
+        [state, side, side, rows2, rows2] + kept,
+        [ON_CHIP] * 10,
+        [],
+        (10000000, grid_bytes),
+        {j: j for j in range(5)},
+    )(c1, next_side, next_again, next_rows_a, next_rows_b, correction, terms, wet, mixing)
+    new_a, new_b = swap(sent_side, "lon_a"), swap(sent_side_again, "lon_b")
     new_rows_a, new_rows_b = swap(next_rows_a, "lat_a"), swap(next_rows_b, "lat_b")
-    c1, c2 = call(
+    c1, c2, *_ = call(
         second_kernel,
-        [ON_CHIP] * 5,
-        [state, vmem(TRACERS, levels, 2, tall, LANES)],
-        [ON_CHIP] * 2,
-        [vmem(TRACERS, levels, 2, tall + PAD, LANES)],
+        [ON_CHIP] * 10,
+        [state] + kept,
+        [ON_CHIP] * 6,
+        [],
         (40000000, 4 * grid_bytes),
-        {0: 0},
-    )(c1, correction, terms, wet, mixing)
+        {j: j for j in range(6)},
+    )(c1, *kept_so_far, correction, terms, wet, mixing)
     fields, density, _ = call(
         last_kernel,
         [ON_CHIP] * 15,
@@ -560,7 +813,7 @@
         (4000000, 2 * grid_bytes),
         {14: 2},
     )(
-        new_a, new_b, next_side, got_a, got_b, new_rows_a, new_rows_b, got_rows_a, got_rows_b,
+        new_a, new_b, sent_side, got_a, got_b, new_rows_a, new_rows_b, got_rows_a, got_rows_b,
         own, row_own, index, c1, wet, c2,
     )
     return fields, density

time: 45.8 us -> 38 us (0.83)
  Pallas kernels: 29.4 us -> 23.8 us
  starting transfers between devices: 15.5 us -> 11.6 us
  waiting for transfers between devices: 0.02 us -> 1.77 us
    ppermute x8, starting transfers between devices: 15.5 us -> 11.6 us  [on_device(): swap = lambda x, name: lax.ppermute(x, both, pairs[name])]
    pallas_call x1, Pallas kernels: 5.73 us -> 2.48 us  [on_device(): call(last_kernel, [ON_CHIP] * 15, [jax.ShapeDtypeStruct(tracers.shape, F3...]
    pallas_call x4 -> x6, Pallas kernels: 23.7 us -> 21.3 us  [the longest x1 6.64 us: on_device(): call(inner_kernel, [ON_CHIP, ANYWHERE, ANYWHERE, ANYWHERE, SCALARS] + [ON...]
    ppermute x8, waiting for transfers between devices: 0.02 us -> 1.77 us  [on_device(): swap = lambda x, name: lax.ppermute(x, both, pairs[name])]
  transfers between devices with their start and end apart: 8 -> 8, of which waited for: 0 -> 1; matrix products, arithmetic and copies ran while one was open for 0% -> 0% of each run, Pallas kernels for 36% -> 23%
where the time goes in v3:
time: 38 us; the launch traced here: 37.9 us
  Pallas kernels  23.8 us (63%)
  starting transfers between devices  11.6 us (31%)
  waiting for transfers between devices  1.77 us (5%)
  between operations  0.74 us (2%)
    ppermute x8, starting transfers between devices, on_device(): swap = lambda x, name: lax.ppermute(x, both, pairs[name])  11.6 us
    pallas_call x1, Pallas kernels, on_device(): call(inner_kernel, [ON_CHIP, ANYWHERE, ANYWHERE, ANYWHERE, SCALARS] + [ON...  6.64 us
    pallas_call x1, Pallas kernels, on_device(): call(early_kernel, [ON_CHIP, ANYWHERE, ANYWHERE, ANYWHERE, SCALARS, ON_CH...  5.18 us
    pallas_call x1, Pallas kernels, on_device(): call(second_early_kernel, [ON_CHIP] * 9, [state, side, side, rows2, rows2...  3.73 us
    pallas_call x1, Pallas kernels, on_device(): call(start_kernel, [ANYWHERE] * 3, [state, side, side, rows3, rows3], [ON...  2.58 us
    pallas_call x1, Pallas kernels, on_device(): call(last_kernel, [ON_CHIP] * 15, [jax.ShapeDtypeStruct(tracers.shape, F3...  2.48 us
    pallas_call x1, Pallas kernels, on_device(): call(second_kernel, [ON_CHIP] * 10, [state] + kept, [ON_CHIP] * 6, [], (4...  1.96 us
    ppermute x8, waiting for transfers between devices, on_device(): swap = lambda x, name: lax.ppermute(x, both, pairs[name])  1.77 us
  transfers between devices with their start and end apart: 8, of which 1 were waited for; matrix products, arithmetic and copies ran while one was open for 0% of the time, Pallas kernels for 23%

profile of v3, /device:TPU:1, one launch (start us, length us, event | category | flops | bytes accessed | tf_op | source)
XLA Modules:
  0.0 37.9 jit_solution(11711154758451712316)
XLA Ops:
  0.6 0.0 copy-start.1
  0.6 2.6 %shard_map.77 = (f32[2,8,2,168,128]{4,3,2,1,0:T(8,128)S(1)}, f32[152,128]{1,0:T(8,128)S(1)}, f32[152,128]{1,0:T(8,128)S(1)}, f32[48,256]{1,0:T(8,128)S(1)}, f32[48,256]{1,0:T(8,128)S(1)}) custom-call(f32[2,8,152,256]{3,2,1,0:T(8,128)} %tracers.1, f32[2,8,152,256]{3,2,1,0:T(8,128)} %east.5, f32[2,8,152,256]{3,2,1,0:T(8,128)} %north.5), custom_call_target="tpu_custom_call" | custom-call | flops 1000000 | bytes 4980736 | tf_op jit(solution)/shard_map/pallas_call | solution.py:740
  3.2 0.0 copy-done.1
  3.2 5.2 %shard_map.78 = (f32[2,8,2,168,128]{4,3,2,1,0:T(8,128)S(1)}, f32[152,128]{1,0:T(8,128)S(1)}, f32[152,128]{1,0:T(8,128)S(1)}, f32[2,3,8,2,152,128]{5,4,3,2,1,0:T(...) custom-call(f32[2,8,2,168,128]{4,3,2,1,0:T(8,128)S(1)} %get-tuple-el, ...), custom_call_target="tpu_custom_call", output_to_operand_aliasing={{7}: (5, {}), {8}: (6, {})} | custom-call | flops 10000000 | bytes 2490368 | tf_op jit(solution)/shard_map/pallas_call | solution.py:753
  8.4 2.9 %collective-permute-start.1 = (f32[152,128]{1,0:T(8,128)S(1)}, f32[152,128]{1,0:T(8,128)S(1)}, u32[]{:S(2)}, u32[]{:S(2)}) collective-permute-start(f32[152,128]{1,0:T(8,128)S(1)} %get-tuple-element.47), channel_id=1, source_target_pairs={{0,15},{1,2},{2,1},{3,4},{4,3},{5,6},{6,5},{7,8},{8,7},{9,10},{10,... | collective-permute-start | bytes 233480 | tf_op jit(solution)/shard_map/ppermute | solution.py:729
  11.3 0.0 collective-permute-start
  11.3 3.5 %collective-permute-start.3 = (f32[48,256]{1,0:T(8,128)S(1)}, f32[48,256]{1,0:T(8,128)S(1)}, u32[]{:S(2)}, u32[]{:S(2)}) collective-permute-start(f32[48,256]{1,0:T(8,128)S(1)} %get-tuple-element.49), channel_id=1, source_target_pairs={{0,1},{1,0},{2,3},{3,2},{4,5},{5,4},{6,7},{7,6},{8,9},{9,8},{10,11... | collective-permute-start | bytes 147464 | tf_op jit(solution)/shard_map/ppermute | solution.py:729
  14.8 0.0 collective-permute-start.2
  14.8 0.0 copy-start
  14.8 6.6 %shard_map.79 = (f32[2,8,2,168,128]{4,3,2,1,0:T(8,128)S(1)}, f32[152,128]{1,0:T(8,128)S(1)}, f32[152,128]{1,0:T(8,128)S(1)}, f32[2,3,8,2,152,128]{5,4,3,2,1,0:T(...) custom-call(f32[2,8,2,168,128]{4,3,2,1,0:T(8,128)S(1)} %get-tuple-el, ...), custom_call_target="tpu_custom_call", output_to_operand_aliasing={{0}: (5, {}), {1}: (6, {}), {2}: (7, {}), {3}: (8, {}), {4}... | custom-call | flops 40000000 | bytes 9961472 | tf_op jit(solution)/shard_map/pallas_call | solution.py:764
  21.5 0.0 collective-permute-done.3.rows_b.faces_b
  21.5 0.0 collective-permute-done.2.rows_a.faces_a
  21.5 0.0 collective-permute-done.1.got_b.first_b
  21.5 0.0 collective-permute-done.got_a.first_a
  21.5 0.0 copy-done
  21.5 1.2 %shard_map.80 = (f32[2,8,2,168,128]{4,3,2,1,0:T(8,128)S(1)}, f32[152,128]{1,0:T(8,128)S(1)}, f32[152,128]{1,0:T(8,128)S(1)}, f32[32,256]{1,0:T(8,128)S(1)}, f32[...) custom-call(f32[152,128]{1,0:T(8,128)S(1)} %collective-permute-done.got_a.first_a, ...), custom_call_target="tpu_custom_call", output_to_operand_aliasing={{0}: (10, {})} | custom-call | flops 1000000 | bytes 1000000 | tf_op jit(solution)/shard_map/pallas_call | solution.py:773
  22.8 3.7 %shard_map.81 = (f32[2,8,2,168,128]{4,3,2,1,0:T(8,128)S(1)}, f32[152,128]{1,0:T(8,128)S(1)}, f32[152,128]{1,0:T(8,128)S(1)}, f32[32,256]{1,0:T(8,128)S(1)}, f32[...) custom-call(f32[2,8,2,168,128]{4,3,2,1,0:T(8,128)S(1)} %get-tuple-el, ...), custom_call_target="tpu_custom_call", output_to_operand_aliasing={{0}: (0, {}), {1}: (1, {}), {2}: (2, {}), {3}: (3, {}), {4}... | custom-call | flops 10000000 | bytes 2490368 | tf_op jit(solution)/shard_map/pallas_call | solution.py:783
  26.5 1.0 %collective-permute-start.4 = (f32[152,128]{1,0:T(8,128)S(1)}, f32[152,128]{1,0:T(8,128)S(1)}, u32[]{:S(2)}, u32[]{:S(2)}) collective-permute-start(f32[152,128]{1,0:T(8,128)S(1)} %get-tuple-element.70.sent), channel_id=1, source_target_pairs={{0,1},{1,0},{2,3},{3,2},{4,5},{5,4},{6,7},{7,6},{8,9},{9,8},{10,11... | collective-permute-start | bytes 233480 | tf_op jit(solution)/shard_map/ppermute | solution.py:729
  27.5 1.9 %collective-permute-start.5 = (f32[152,128]{1,0:T(8,128)S(1)}, f32[152,128]{1,0:T(8,128)S(1)}, u32[]{:S(2)}, u32[]{:S(2)}) collective-permute-start(f32[152,128]{1,0:T(8,128)S(1)} %get-tuple-element.71), channel_id=1, source_target_pairs={{0,15},{1,2},{2,1},{3,4},{4,3},{5,6},{6,5},{7,8},{8,7},{9,10},{10,... | collective-permute-start | bytes 233480 | tf_op jit(solution)/shard_map/ppermute | solution.py:729
  29.5 1.1 %collective-permute-start.6 = (f32[32,256]{1,0:T(8,128)S(1)}, f32[32,256]{1,0:T(8,128)S(1)}, u32[]{:S(2)}, u32[]{:S(2)}) collective-permute-start(f32[32,256]{1,0:T(8,128)S(1)} %get-tuple-element.72), channel_id=1, source_target_pairs={{0,16},{1,17},{2,18},{3,19},{4,20},{5,21},{6,22},{7,23},{8,24},{9,... | collective-permute-start | bytes 98312 | tf_op jit(solution)/shard_map/ppermute | solution.py:729
  30.6 1.1 %collective-permute-start.7 = (f32[32,256]{1,0:T(8,128)S(1)}, f32[32,256]{1,0:T(8,128)S(1)}, u32[]{:S(2)}, u32[]{:S(2)}) collective-permute-start(f32[32,256]{1,0:T(8,128)S(1)} %get-tuple-element.73), channel_id=1, source_target_pairs={{0,1},{1,0},{2,3},{3,2},{4,5},{5,4},{6,7},{7,6},{8,9},{9,8},{10,11... | collective-permute-start | bytes 98312 | tf_op jit(solution)/shard_map/ppermute | solution.py:729
  31.7 2.0 %shard_map.82 = (f32[2,8,2,168,128]{4,3,2,1,0:T(8,128)S(1)}, f32[2,8,2,152,128]{4,3,2,1,0:T(8,128)S(1)}, f32[2,8,2,160,128]{4,3,2,1,0:T(8,128)S(1)}, f32[2,8,2,1...) custom-call(f32[2,8,2,168,128]{4,3,2,1,0:T(8,128)S(1)} %get-tuple-el, ...), custom_call_target="tpu_custom_call", output_to_operand_aliasing={{0}: (0, {}), {1}: (1, {}), {2}: (2, {}), {3}: (3, {}), {4}... | custom-call | flops 40000000 | bytes 9961472 | tf_op jit(solution)/shard_map/pallas_call | solution.py:794
  33.7 0.0 collective-permute-done.6.rows_a
  33.7 1.8 %collective-permute-done.7.rows_b = f32[32,256]{1,0:T(8,128)S(1)} collective-permute-done((f32[32,256]{1,0:T(8,128)S(1)}, f32[32,256]{1,0:T(8,128)S(1)}, u32[]{:S(2)}, u32[]{:S(2)}) %collective-permute-start.7) | collective-permute-done | bytes 32800 | tf_op jit(solution)/shard_map/ppermute | solution.py:729
  35.4 0.0 collective-permute-done.4.got_a
  35.4 0.0 collective-permute-done.5.got_b
  35.4 2.5 %shard_map.83 = (f32[2,8,152,256]{3,2,1,0:T(8,128)}, f32[8,152,256]{2,1,0:T(8,128)}, f32[2,8,2,152,128]{4,3,2,1,0:T(8,128)S(1)}) custom-call(f32[152,128]{1,0:T(8,128)S(1)} %collective-permute-done.4.got_a, f32[152,128]{1,0:T(8,128)S(1)} %collective-permute-done.5.got_b, f32[152,128]{1,0:T(8,128)S(1)} %get-tuple-element.70.sent, ...), custom_call_target="tpu_custom_call", output_to_operand_aliasing={{2}: (14, {})} | custom-call | flops 4000000 | bytes 4980736 | tf_op jit(solution)/shard_map/pallas_call | solution.py:803
Async XLA Ops:
  0.6 2.6 %copy-start.1 = (f32[7]{0:T(128)S(1)}, f32[7]{0:T(128)}, u32[]{:S(2)}) copy-start(f32[7]{0:T(128)} %mix.3) | copy-start | bytes 88
  8.4 13.1 %collective-permute-start.1 = (f32[152,128]{1,0:T(8,128)S(1)}, f32[152,128]{1,0:T(8,128)S(1)}, u32[]{:S(2)}, u32[]{:S(2)}) collective-permute-start(f32[152,128]{1,0:T(8,128)S(1)} %get-tuple-element.47), channel_id=1, source_target_pairs={{0,15},{1,2},{2,1},{3,4},{4,3},{5,6},{6,5},{7,8},{8,7},{9,10},{10,... | collective-permute-start | bytes 233480 | tf_op jit(solution)/shard_map/ppermute | solution.py:729
  11.3 10.2 %collective-permute-start = (f32[152,128]{1,0:T(8,128)S(1)}, f32[152,128]{1,0:T(8,128)S(1)}, u32[]{:S(2)}, u32[]{:S(2)}) collective-permute-start(f32[152,128]{1,0:T(8,128)S(1)} %get-tuple-element.43.sent), channel_id=1, source_target_pairs={{0,1},{1,0},{2,3},{3,2},{4,5},{5,4},{6,7},{7,6},{8,9},{9,8},{10,11... | collective-permute-start | bytes 233480 | tf_op jit(solution)/shard_map/ppermute | solution.py:729
  11.3 10.1 %collective-permute-start.3 = (f32[48,256]{1,0:T(8,128)S(1)}, f32[48,256]{1,0:T(8,128)S(1)}, u32[]{:S(2)}, u32[]{:S(2)}) collective-permute-start(f32[48,256]{1,0:T(8,128)S(1)} %get-tuple-element.49), channel_id=1, source_target_pairs={{0,1},{1,0},{2,3},{3,2},{4,5},{5,4},{6,7},{7,6},{8,9},{9,8},{10,11... | collective-permute-start | bytes 147464 | tf_op jit(solution)/shard_map/ppermute | solution.py:729
  14.8 6.7 %collective-permute-start.2 = (f32[48,256]{1,0:T(8,128)S(1)}, f32[48,256]{1,0:T(8,128)S(1)}, u32[]{:S(2)}, u32[]{:S(2)}) collective-permute-start(f32[48,256]{1,0:T(8,128)S(1)} %get-tuple-element.48), channel_id=1, source_target_pairs={{0,16},{1,17},{2,18},{3,19},{4,20},{5,21},{6,22},{7,23},{8,24},{9,... | collective-permute-start | bytes 147464 | tf_op jit(solution)/shard_map/ppermute | solution.py:729
  14.8 6.7 %copy-start = (s32[256]{0:T(256)S(1)}, s32[256]{0:T(256)}, u32[]{:S(2)}) copy-start(s32[256]{0:T(256)} %param.10) | copy-start | bytes 3076
  26.5 8.9 %collective-permute-start.4 = (f32[152,128]{1,0:T(8,128)S(1)}, f32[152,128]{1,0:T(8,128)S(1)}, u32[]{:S(2)}, u32[]{:S(2)}) collective-permute-start(f32[152,128]{1,0:T(8,128)S(1)} %get-tuple-element.70.sent), channel_id=1, source_target_pairs={{0,1},{1,0},{2,3},{3,2},{4,5},{5,4},{6,7},{7,6},{8,9},{9,8},{10,11... | collective-permute-start | bytes 233480 | tf_op jit(solution)/shard_map/ppermute | solution.py:729
  27.5 7.9 %collective-permute-start.5 = (f32[152,128]{1,0:T(8,128)S(1)}, f32[152,128]{1,0:T(8,128)S(1)}, u32[]{:S(2)}, u32[]{:S(2)}) collective-permute-start(f32[152,128]{1,0:T(8,128)S(1)} %get-tuple-element.71), channel_id=1, source_target_pairs={{0,15},{1,2},{2,1},{3,4},{4,3},{5,6},{6,5},{7,8},{8,7},{9,10},{10,... | collective-permute-start | bytes 233480 | tf_op jit(solution)/shard_map/ppermute | solution.py:729
  29.5 4.2 %collective-permute-start.6 = (f32[32,256]{1,0:T(8,128)S(1)}, f32[32,256]{1,0:T(8,128)S(1)}, u32[]{:S(2)}, u32[]{:S(2)}) collective-permute-start(f32[32,256]{1,0:T(8,128)S(1)} %get-tuple-element.72), channel_id=1, source_target_pairs={{0,16},{1,17},{2,18},{3,19},{4,20},{5,21},{6,22},{7,23},{8,24},{9,... | collective-permute-start | bytes 98312 | tf_op jit(solution)/shard_map/ppermute | solution.py:729
  30.6 4.9 %collective-permute-start.7 = (f32[32,256]{1,0:T(8,128)S(1)}, f32[32,256]{1,0:T(8,128)S(1)}, u32[]{:S(2)}, u32[]{:S(2)}) collective-permute-start(f32[32,256]{1,0:T(8,128)S(1)} %get-tuple-element.73), channel_id=1, source_target_pairs={{0,1},{1,0},{2,3},{3,2},{4,5},{5,4},{6,7},{7,6},{8,9},{9,8},{10,11... | collective-permute-start | bytes 98312 | tf_op jit(solution)/shard_map/ppermute | solution.py:729

commit v4 on v3

--- a/solution.py
+++ b/solution.py
@@ -40,15 +40,23 @@
     levels = wet.shape[0]
     rows = tile_rows(r)
     for h in range(2):
-        cells = [mask[k, h, rows, :].astype(F32) for k in range(levels)]
+        cells = [mask(k, h, rows).astype(F32) for k in range(levels)]
         for k in range(levels):
             wet[k, h, rows, :] = cells[k]
             if k + 1 < levels:
                 mixing[k, h, rows, :] = mix[k] * cells[k] * cells[k + 1]
             for way, faces in enumerate((east, north)):
-                a, b, g, _ = face_terms(faces[0, k, h, rows, :], faces[1, k, h, rows, :])
+                a, b, g, _ = face_terms(faces(0, k, h, rows), faces(1, k, h, rows))
                 for j, one in enumerate((a, b, g)):
                     terms[way, j, k, h, rows, :] = one
+
+
+def halved(ref):
+    return lambda *at: ref[at + (slice(None),)]
+
+
+def whole(ref):
+    return lambda *at: ref[at[:-2] + (at[-1], slice(at[-2] * LANES, (at[-2] + 1) * LANES))]
 
 
 def advance_tile(r, c, south, terms, wet, mixing, out, out_pad):
@@ -370,7 +378,8 @@
     copies = inner_copies(pieces, east, north, mask, east_in, north_in, mask_in, sems)
 
     def body(r, carry):
-        inner_tile(r, c, mix, out, packed, own, terms, wet, mixing, south, east_in, north_in, mask_in)
+        faces = halved(east_in), halved(north_in), halved(mask_in)
+        inner_tile(r, c, mix, out, packed, own, terms, wet, mixing, south, *faces)
         return carry
 
     for group_of in copies:
@@ -384,7 +393,7 @@
 
 def inner_kernel(
     c, east, north, mask, mix, out_in, packed_in, own_in, terms_in, wet_in, mixing_in, south_in,
-    out, packed, own, terms, wet, mixing, south, row_own, east_in, north_in, mask_in, sems,
+    out, packed, own, terms, wet, mixing, south, row_own,
 ):
     levels, tall = wet.shape[0], wet.shape[2]
     done = share(EARLY_TILES)
@@ -395,28 +404,12 @@
     def _():
         clear(south, slice(0, PAD))
 
-    pieces = FIRST_PIECES + REST_PIECES
-    copies = inner_copies(pieces, east, north, mask, east_in, north_in, mask_in, sems)
-
     def body(r, carry):
-        inner_tile(r, c, mix, out, packed, own, terms, wet, mixing, south, east_in, north_in, mask_in)
+        faces = whole(east), whole(north), whole(mask)
+        inner_tile(r, c, mix, out, packed, own, terms, wet, mixing, south, *faces)
         return carry
 
-    for (lo, hi), group_of in zip(pieces, copies):
-
-        @pl.when(done < hi // SUB)
-        def _(group_of=group_of):
-            for one in group_of:
-                one.start()
-
-    for (lo, hi), group_of in zip(pieces, copies):
-
-        @pl.when(done < hi // SUB)
-        def _(lo=lo, hi=hi, group_of=group_of):
-            for one in group_of:
-                one.wait()
-            lax.fori_loop(jnp.maximum(lo // SUB, done), hi // SUB, body, 0)
-
+    lax.fori_loop(done, tall // SUB, body, 0)
     for k in range(levels):
         for h in range(2):
             cols = slice(h * LANES, (h + 1) * LANES)
@@ -727,6 +720,7 @@
     index = fold_partner.reshape(1, wide)
     both = ("lat", "lon")
     swap = lambda x, name: lax.ppermute(x, both, pairs[name])
+    near = [pltpu.with_memory_space_constraint(x, pltpu.VMEM) for x in (east_faces, north_faces, land_mask)]
     tracers, east_faces, north_faces, land_mask = (
         pltpu.with_memory_space_constraint(x, pltpu.HBM) for x in (tracers, east_faces, north_faces, land_mask)
     )
@@ -763,13 +757,13 @@
     got_b, got_rows_b = swap(sent_again, "lon_b"), swap(rows_b, "lat_b")
     c1, packed, own, terms, wet, mixing, _, row_own = call(
         inner_kernel,
-        [ON_CHIP, ANYWHERE, ANYWHERE, ANYWHERE, SCALARS] + [ON_CHIP] * 7,
+        [ON_CHIP] * 4 + [SCALARS] + [ON_CHIP] * 7,
         shared + [vmem(8 * levels, wide)],
         [ON_CHIP] * 8,
-        [faces, faces, vmem(levels, 2, tall, LANES, dtype=jnp.int32), pltpu.SemaphoreType.DMA((30,))],
+        [],
         (40000000, 4 * grid_bytes),
         {5 + j: j for j in range(7)},
-    )(c0, east_faces, north_faces, land_mask, vert_mix, *state_so_far)
+    )(c0, *near, vert_mix, *state_so_far)
     c1, next_side, next_again, next_rows_a, next_rows_b, correction = call(
         edge_kernel,
         [ON_CHIP] * 11,

time: 38 us -> 36.7 us (0.966)
  Pallas kernels: 23.8 us -> 22.5 us
    pallas_call x1, Pallas kernels: 6.64 us -> 4.99 us  [on_device(): call(inner_kernel, [ON_CHIP] * 4 + [SCALARS] + [ON_CHIP] * 7, shared + [v...]
  transfers between devices with their start and end apart: 8 -> 8, of which waited for: 1 -> 1; matrix products, arithmetic and copies ran while one was open for 0% -> 0% of each run, Pallas kernels for 23% -> 19%
where the time goes in v4:
time: 36.7 us; the launch traced here: 36.6 us
  Pallas kernels  22.5 us (61%)
  starting transfers between devices  11.6 us (32%)
  waiting for transfers between devices  1.74 us (5%)
  between operations  0.77 us (2%)
    ppermute x8, starting transfers between devices, on_device(): swap = lambda x, name: lax.ppermute(x, both, pairs[name])  11.6 us
    pallas_call x1, Pallas kernels, on_device(): call(early_kernel, [ON_CHIP, ANYWHERE, ANYWHERE, ANYWHERE, SCALARS, ON_CH...  5.48 us
    pallas_call x1, Pallas kernels, on_device(): call(inner_kernel, [ON_CHIP] * 4 + [SCALARS] + [ON_CHIP] * 7, shared + [v...  4.99 us
    pallas_call x1, Pallas kernels, on_device(): call(second_early_kernel, [ON_CHIP] * 9, [state, side, side, rows2, rows2...  3.78 us
    pallas_call x1, Pallas kernels, on_device(): call(start_kernel, [ANYWHERE] * 3, [state, side, side, rows3, rows3], [ON...  2.58 us
    pallas_call x1, Pallas kernels, on_device(): call(last_kernel, [ON_CHIP] * 15, [jax.ShapeDtypeStruct(tracers.shape, F3...  2.44 us
    pallas_call x1, Pallas kernels, on_device(): call(second_kernel, [ON_CHIP] * 10, [state] + kept, [ON_CHIP] * 6, [], (4...  1.99 us
    ppermute x8, waiting for transfers between devices, on_device(): swap = lambda x, name: lax.ppermute(x, both, pairs[name])  1.74 us
  transfers between devices with their start and end apart: 8, of which 1 were waited for; matrix products, arithmetic and copies ran while one was open for 0% of the time, Pallas kernels for 19%

profile of v4, /device:TPU:1, one launch (start us, length us, event | category | flops | bytes accessed | tf_op | source)
XLA Modules:
  0.0 36.6 jit_solution(6277941261331938933)
XLA Ops:
  0.6 0.0 copy-start.4
  0.6 2.6 %shard_map.77 = (f32[2,8,2,168,128]{4,3,2,1,0:T(8,128)S(1)}, f32[152,128]{1,0:T(8,128)S(1)}, f32[152,128]{1,0:T(8,128)S(1)}, f32[48,256]{1,0:T(8,128)S(1)}, f32[48,256]{1,0:T(8,128)S(1)}) custom-call(f32[2,8,152,256]{3,2,1,0:T(8,128)} %tracers.1, f32[2,8,152,256]{3,2,1,0:T(8,128)} %east.5, f32[2,8,152,256]{3,2,1,0:T(8,128)} %north.5), custom_call_target="tpu_custom_call" | custom-call | flops 1000000 | bytes 4980736 | tf_op jit(solution)/shard_map/pallas_call | solution.py:734
  3.2 0.0 copy-done.4
  3.2 0.0 copy-start
  3.3 0.0 copy-start.1
  3.3 0.0 copy-start.2
  3.3 5.5 %shard_map.78 = (f32[2,8,2,168,128]{4,3,2,1,0:T(8,128)S(1)}, f32[152,128]{1,0:T(8,128)S(1)}, f32[152,128]{1,0:T(8,128)S(1)}, f32[2,3,8,2,152,128]{5,4,3,2,1,0:T(...) custom-call(f32[2,8,2,168,128]{4,3,2,1,0:T(8,128)S(1)} %get-tuple-el, ...), custom_call_target="tpu_custom_call", output_to_operand_aliasing={{7}: (5, {}), {8}: (6, {})} | custom-call | flops 10000000 | bytes 2490368 | tf_op jit(solution)/shard_map/pallas_call | solution.py:747
  8.8 2.6 %collective-permute-start.1 = (f32[152,128]{1,0:T(8,128)S(1)}, f32[152,128]{1,0:T(8,128)S(1)}, u32[]{:S(2)}, u32[]{:S(2)}) collective-permute-start(f32[152,128]{1,0:T(8,128)S(1)} %get-tuple-element.47), channel_id=1, source_target_pairs={{0,15},{1,2},{2,1},{3,4},{4,3},{5,6},{6,5},{7,8},{8,7},{9,10},{10,... | collective-permute-start | bytes 233480 | tf_op jit(solution)/shard_map/ppermute | solution.py:722
  11.4 0.0 collective-permute-start
  11.4 3.8 %collective-permute-start.3 = (f32[48,256]{1,0:T(8,128)S(1)}, f32[48,256]{1,0:T(8,128)S(1)}, u32[]{:S(2)}, u32[]{:S(2)}) collective-permute-start(f32[48,256]{1,0:T(8,128)S(1)} %get-tuple-element.49), channel_id=1, source_target_pairs={{0,1},{1,0},{2,3},{3,2},{4,5},{5,4},{6,7},{7,6},{8,9},{9,8},{10,11... | collective-permute-start | bytes 147464 | tf_op jit(solution)/shard_map/ppermute | solution.py:722
  15.2 0.0 collective-permute-start.2
  15.2 0.0 copy-done
  15.2 0.0 copy-done.1
  15.2 0.0 copy-done.2
  15.2 0.0 copy-start.3
  15.2 5.0 %shard_map.79 = (f32[2,8,2,168,128]{4,3,2,1,0:T(8,128)S(1)}, f32[152,128]{1,0:T(8,128)S(1)}, f32[152,128]{1,0:T(8,128)S(1)}, f32[2,3,8,2,152,128]{5,4,3,2,1,0:T(...) custom-call(f32[2,8,2,168,128]{4,3,2,1,0:T(8,128)S(1)} %get-tuple-el, ...), custom_call_target="tpu_custom_call", output_to_operand_aliasing={{0}: (5, {}), {1}: (6, {}), {2}: (7, {}), {3}: (8, {}), {4}... | custom-call | flops 40000000 | bytes 9961472 | tf_op jit(solution)/shard_map/pallas_call | solution.py:758
  20.2 0.0 collective-permute-done.3.rows_b.faces_b
  20.2 0.0 collective-permute-done.2.rows_a.faces_a
  20.2 0.0 collective-permute-done.1.got_b.first_b
  20.2 0.0 collective-permute-done.got_a.first_a
  20.2 0.0 copy-done.3
  20.2 1.2 %shard_map.80 = (f32[2,8,2,168,128]{4,3,2,1,0:T(8,128)S(1)}, f32[152,128]{1,0:T(8,128)S(1)}, f32[152,128]{1,0:T(8,128)S(1)}, f32[32,256]{1,0:T(8,128)S(1)}, f32[...) custom-call(f32[152,128]{1,0:T(8,128)S(1)} %collective-permute-done.got_a.first_a, ...), custom_call_target="tpu_custom_call", output_to_operand_aliasing={{0}: (10, {})} | custom-call | flops 1000000 | bytes 1000000 | tf_op jit(solution)/shard_map/pallas_call | solution.py:767
  21.5 3.8 %shard_map.81 = (f32[2,8,2,168,128]{4,3,2,1,0:T(8,128)S(1)}, f32[152,128]{1,0:T(8,128)S(1)}, f32[152,128]{1,0:T(8,128)S(1)}, f32[32,256]{1,0:T(8,128)S(1)}, f32[...) custom-call(f32[2,8,2,168,128]{4,3,2,1,0:T(8,128)S(1)} %get-tuple-el, ...), custom_call_target="tpu_custom_call", output_to_operand_aliasing={{0}: (0, {}), {1}: (1, {}), {2}: (2, {}), {3}: (3, {}), {4}... | custom-call | flops 10000000 | bytes 2490368 | tf_op jit(solution)/shard_map/pallas_call | solution.py:777
  25.3 0.7 %collective-permute-start.4 = (f32[152,128]{1,0:T(8,128)S(1)}, f32[152,128]{1,0:T(8,128)S(1)}, u32[]{:S(2)}, u32[]{:S(2)}) collective-permute-start(f32[152,128]{1,0:T(8,128)S(1)} %get-tuple-element.70.sent), channel_id=1, source_target_pairs={{0,1},{1,0},{2,3},{3,2},{4,5},{5,4},{6,7},{7,6},{8,9},{9,8},{10,11... | collective-permute-start | bytes 233480 | tf_op jit(solution)/shard_map/ppermute | solution.py:722
  26.0 2.2 %collective-permute-start.5 = (f32[152,128]{1,0:T(8,128)S(1)}, f32[152,128]{1,0:T(8,128)S(1)}, u32[]{:S(2)}, u32[]{:S(2)}) collective-permute-start(f32[152,128]{1,0:T(8,128)S(1)} %get-tuple-element.71), channel_id=1, source_target_pairs={{0,15},{1,2},{2,1},{3,4},{4,3},{5,6},{6,5},{7,8},{8,7},{9,10},{10,... | collective-permute-start | bytes 233480 | tf_op jit(solution)/shard_map/ppermute | solution.py:722
  28.2 1.1 %collective-permute-start.6 = (f32[32,256]{1,0:T(8,128)S(1)}, f32[32,256]{1,0:T(8,128)S(1)}, u32[]{:S(2)}, u32[]{:S(2)}) collective-permute-start(f32[32,256]{1,0:T(8,128)S(1)} %get-tuple-element.72), channel_id=1, source_target_pairs={{0,16},{1,17},{2,18},{3,19},{4,20},{5,21},{6,22},{7,23},{8,24},{9,... | collective-permute-start | bytes 98312 | tf_op jit(solution)/shard_map/ppermute | solution.py:722
  29.3 1.1 %collective-permute-start.7 = (f32[32,256]{1,0:T(8,128)S(1)}, f32[32,256]{1,0:T(8,128)S(1)}, u32[]{:S(2)}, u32[]{:S(2)}) collective-permute-start(f32[32,256]{1,0:T(8,128)S(1)} %get-tuple-element.73), channel_id=1, source_target_pairs={{0,1},{1,0},{2,3},{3,2},{4,5},{5,4},{6,7},{7,6},{8,9},{9,8},{10,11... | collective-permute-start | bytes 98312 | tf_op jit(solution)/shard_map/ppermute | solution.py:722
  30.4 2.0 %shard_map.82 = (f32[2,8,2,168,128]{4,3,2,1,0:T(8,128)S(1)}, f32[2,8,2,152,128]{4,3,2,1,0:T(8,128)S(1)}, f32[2,8,2,160,128]{4,3,2,1,0:T(8,128)S(1)}, f32[2,8,2,1...) custom-call(f32[2,8,2,168,128]{4,3,2,1,0:T(8,128)S(1)} %get-tuple-el, ...), custom_call_target="tpu_custom_call", output_to_operand_aliasing={{0}: (0, {}), {1}: (1, {}), {2}: (2, {}), {3}: (3, {}), {4}... | custom-call | flops 40000000 | bytes 9961472 | tf_op jit(solution)/shard_map/pallas_call | solution.py:788
  32.4 0.0 collective-permute-done.6.rows_a
  32.4 1.7 %collective-permute-done.7.rows_b = f32[32,256]{1,0:T(8,128)S(1)} collective-permute-done((f32[32,256]{1,0:T(8,128)S(1)}, f32[32,256]{1,0:T(8,128)S(1)}, u32[]{:S(2)}, u32[]{:S(2)}) %collective-permute-start.7) | collective-permute-done | bytes 32800 | tf_op jit(solution)/shard_map/ppermute | solution.py:722
  34.1 0.0 collective-permute-done.4.got_a
  34.2 0.0 collective-permute-done.5.got_b
  34.2 2.4 %shard_map.83 = (f32[2,8,152,256]{3,2,1,0:T(8,128)}, f32[8,152,256]{2,1,0:T(8,128)}, f32[2,8,2,152,128]{4,3,2,1,0:T(8,128)S(1)}) custom-call(f32[152,128]{1,0:T(8,128)S(1)} %collective-permute-done.4.got_a, f32[152,128]{1,0:T(8,128)S(1)} %collective-permute-done.5.got_b, f32[152,128]{1,0:T(8,128)S(1)} %get-tuple-element.70.sent, ...), custom_call_target="tpu_custom_call", output_to_operand_aliasing={{2}: (14, {})} | custom-call | flops 4000000 | bytes 4980736 | tf_op jit(solution)/shard_map/pallas_call | solution.py:797
Async XLA Ops:
  0.6 2.6 %copy-start.4 = (f32[7]{0:T(128)S(1)}, f32[7]{0:T(128)}, u32[]{:S(2)}) copy-start(f32[7]{0:T(128)} %mix.3) | copy-start | bytes 88
  3.2 11.9 %copy-start = (f32[2,8,152,256]{3,2,1,0:T(8,128)S(1)}, f32[2,8,152,256]{3,2,1,0:T(8,128)}, u32[]{:S(2)}) copy-start(f32[2,8,152,256]{3,2,1,0:T(8,128)} %east.5) | copy-start | bytes 7471108
  3.3 11.9 %copy-start.1 = (f32[2,8,152,256]{3,2,1,0:T(8,128)S(1)}, f32[2,8,152,256]{3,2,1,0:T(8,128)}, u32[]{:S(2)}) copy-start(f32[2,8,152,256]{3,2,1,0:T(8,128)} %north.5) | copy-start | bytes 7471108
  3.3 11.9 %copy-start.2 = (s32[8,152,256]{2,1,0:T(8,128)S(1)}, s32[8,152,256]{2,1,0:T(8,128)}, u32[]{:S(2)}) copy-start(s32[8,152,256]{2,1,0:T(8,128)} %mask.3) | copy-start | bytes 3735556
  8.8 11.4 %collective-permute-start.1 = (f32[152,128]{1,0:T(8,128)S(1)}, f32[152,128]{1,0:T(8,128)S(1)}, u32[]{:S(2)}, u32[]{:S(2)}) collective-permute-start(f32[152,128]{1,0:T(8,128)S(1)} %get-tuple-element.47), channel_id=1, source_target_pairs={{0,15},{1,2},{2,1},{3,4},{4,3},{5,6},{6,5},{7,8},{8,7},{9,10},{10,... | collective-permute-start | bytes 233480 | tf_op jit(solution)/shard_map/ppermute | solution.py:722
  11.4 8.8 %collective-permute-start = (f32[152,128]{1,0:T(8,128)S(1)}, f32[152,128]{1,0:T(8,128)S(1)}, u32[]{:S(2)}, u32[]{:S(2)}) collective-permute-start(f32[152,128]{1,0:T(8,128)S(1)} %get-tuple-element.43.sent), channel_id=1, source_target_pairs={{0,1},{1,0},{2,3},{3,2},{4,5},{5,4},{6,7},{7,6},{8,9},{9,8},{10,11... | collective-permute-start | bytes 233480 | tf_op jit(solution)/shard_map/ppermute | solution.py:722
  11.4 8.8 %collective-permute-start.3 = (f32[48,256]{1,0:T(8,128)S(1)}, f32[48,256]{1,0:T(8,128)S(1)}, u32[]{:S(2)}, u32[]{:S(2)}) collective-permute-start(f32[48,256]{1,0:T(8,128)S(1)} %get-tuple-element.49), channel_id=1, source_target_pairs={{0,1},{1,0},{2,3},{3,2},{4,5},{5,4},{6,7},{7,6},{8,9},{9,8},{10,11... | collective-permute-start | bytes 147464 | tf_op jit(solution)/shard_map/ppermute | solution.py:722
  15.2 5.0 %collective-permute-start.2 = (f32[48,256]{1,0:T(8,128)S(1)}, f32[48,256]{1,0:T(8,128)S(1)}, u32[]{:S(2)}, u32[]{:S(2)}) collective-permute-start(f32[48,256]{1,0:T(8,128)S(1)} %get-tuple-element.48), channel_id=1, source_target_pairs={{0,16},{1,17},{2,18},{3,19},{4,20},{5,21},{6,22},{7,23},{8,24},{9,... | collective-permute-start | bytes 147464 | tf_op jit(solution)/shard_map/ppermute | solution.py:722
  15.2 5.0 %copy-start.3 = (s32[256]{0:T(256)S(1)}, s32[256]{0:T(256)}, u32[]{:S(2)}) copy-start(s32[256]{0:T(256)} %param.10) | copy-start | bytes 3076
  25.3 8.9 %collective-permute-start.4 = (f32[152,128]{1,0:T(8,128)S(1)}, f32[152,128]{1,0:T(8,128)S(1)}, u32[]{:S(2)}, u32[]{:S(2)}) collective-permute-start(f32[152,128]{1,0:T(8,128)S(1)} %get-tuple-element.70.sent), channel_id=1, source_target_pairs={{0,1},{1,0},{2,3},{3,2},{4,5},{5,4},{6,7},{7,6},{8,9},{9,8},{10,11... | collective-permute-start | bytes 233480 | tf_op jit(solution)/shard_map/ppermute | solution.py:722
  26.0 8.2 %collective-permute-start.5 = (f32[152,128]{1,0:T(8,128)S(1)}, f32[152,128]{1,0:T(8,128)S(1)}, u32[]{:S(2)}, u32[]{:S(2)}) collective-permute-start(f32[152,128]{1,0:T(8,128)S(1)} %get-tuple-element.71), channel_id=1, source_target_pairs={{0,15},{1,2},{2,1},{3,4},{4,3},{5,6},{6,5},{7,8},{8,7},{9,10},{10,... | collective-permute-start | bytes 233480 | tf_op jit(solution)/shard_map/ppermute | solution.py:722
  28.2 4.2 %collective-permute-start.6 = (f32[32,256]{1,0:T(8,128)S(1)}, f32[32,256]{1,0:T(8,128)S(1)}, u32[]{:S(2)}, u32[]{:S(2)}) collective-permute-start(f32[32,256]{1,0:T(8,128)S(1)} %get-tuple-element.72), channel_id=1, source_target_pairs={{0,16},{1,17},{2,18},{3,19},{4,20},{5,21},{6,22},{7,23},{8,24},{9,... | collective-permute-start | bytes 98312 | tf_op jit(solution)/shard_map/ppermute | solution.py:722
  29.3 4.9 %collective-permute-start.7 = (f32[32,256]{1,0:T(8,128)S(1)}, f32[32,256]{1,0:T(8,128)S(1)}, u32[]{:S(2)}, u32[]{:S(2)}) collective-permute-start(f32[32,256]{1,0:T(8,128)S(1)} %get-tuple-element.73), channel_id=1, source_target_pairs={{0,1},{1,0},{2,3},{3,2},{4,5},{5,4},{6,7},{7,6},{8,9},{9,8},{10,11... | collective-permute-start | bytes 98312 | tf_op jit(solution)/shard_map/ppermute | solution.py:722

commit v5 on v4

--- a/solution.py
+++ b/solution.py
@@ -224,7 +224,7 @@
 
 def start_kernel(tracers, east, north, c, side, side_again, rows_a, rows_b, east_last, north_top, sems):
     levels, tall = tracers.shape[1], tracers.shape[2]
-    cuts = [0, 40, 80, 120, tall]
+    cuts = [0, 48, 96, tall]
     copies = []
     for i, (lo, hi) in enumerate(zip(cuts[:-1], cuts[1:])):
         group_of = []
@@ -242,7 +242,7 @@
             )
         )
         copies.append(group_of)
-    top_copy = pltpu.make_async_copy(north.at[:, :, tall - SUB :, :], north_top, sems.at[12])
+    top_copy = pltpu.make_async_copy(north.at[:, :, tall - SUB :, :], north_top, sems.at[9])
     for group_of in copies:
         for one in group_of:
             one.start()
@@ -651,7 +651,7 @@
                 density_out[k, h, rows, :] = wet[k, h, rows, :] * (0.8 * salt - 0.2 * heat - 0.05 * heat * heat)
         return carry
 
-    cuts = [0, 40, 80, 120, tall]
+    cuts = [0, 40, 96, tall]
     copies = []
     for i, (lo, hi) in enumerate(zip(cuts[:-1], cuts[1:])):
         lax.fori_loop(lo // SUB, hi // SUB, body, 0, unroll=True)
@@ -736,7 +736,7 @@
         [ANYWHERE] * 3,
         [state, side, side, rows3, rows3],
         [ON_CHIP] * 5,
-        [vmem(2, levels, tall, LANES), vmem(2, levels, SUB, wide), pltpu.SemaphoreType.DMA((13,))],
+        [vmem(2, levels, tall, LANES), vmem(2, levels, SUB, wide), pltpu.SemaphoreType.DMA((10,))],
         (1000000, 2 * grid_bytes),
     )(tracers, east_faces, north_faces)
     got_a, got_rows_a = swap(sent, "lon_a"), swap(rows_a, "lat_a")
@@ -803,7 +803,7 @@
             vmem(TRACERS, levels, 2, tall, LANES),
         ],
         [ANYWHERE, ANYWHERE, ON_CHIP],
-        [vmem(TRACERS, levels, 2, tall, LANES), level, pltpu.SemaphoreType.DMA((16,))],
+        [vmem(TRACERS, levels, 2, tall, LANES), level, pltpu.SemaphoreType.DMA((12,))],
         (4000000, 2 * grid_bytes),
         {14: 2},
     )(

time: 36.7 us -> 36.8 us (level)
  no operation moved by 1% of the time
where the time goes in v5:
time: 36.8 us; the launch traced here: 36.7 us
  Pallas kernels  22.6 us (61%)
  starting transfers between devices  11.6 us (32%)
  waiting for transfers between devices  1.74 us (5%)
  between operations  0.77 us (2%)
    ppermute x8, starting transfers between devices, on_device(): swap = lambda x, name: lax.ppermute(x, both, pairs[name])  11.6 us
    pallas_call x1, Pallas kernels, on_device(): call(early_kernel, [ON_CHIP, ANYWHERE, ANYWHERE, ANYWHERE, SCALARS, ON_CH...  5.48 us
    pallas_call x1, Pallas kernels, on_device(): call(inner_kernel, [ON_CHIP] * 4 + [SCALARS] + [ON_CHIP] * 7, shared + [v...  4.99 us
    pallas_call x1, Pallas kernels, on_device(): call(second_early_kernel, [ON_CHIP] * 9, [state, side, side, rows2, rows2...  3.78 us
    pallas_call x1, Pallas kernels, on_device(): call(start_kernel, [ANYWHERE] * 3, [state, side, side, rows3, rows3], [ON...  2.73 us
    pallas_call x1, Pallas kernels, on_device(): call(last_kernel, [ON_CHIP] * 15, [jax.ShapeDtypeStruct(tracers.shape, F3...  2.44 us
    pallas_call x1, Pallas kernels, on_device(): call(second_kernel, [ON_CHIP] * 10, [state] + kept, [ON_CHIP] * 6, [], (4...  1.99 us
    ppermute x8, waiting for transfers between devices, on_device(): swap = lambda x, name: lax.ppermute(x, both, pairs[name])  1.74 us
  transfers between devices with their start and end apart: 8, of which 1 were waited for; matrix products, arithmetic and copies ran while one was open for 0% of the time, Pallas kernels for 19%

profile of v5, /device:TPU:1, one launch (start us, length us, event | category | flops | bytes accessed | tf_op | source)
XLA Modules:
  0.0 36.7 jit_solution(15720781612788718596)
XLA Ops:
  0.6 0.0 copy-start.4
  0.6 2.7 %shard_map.77 = (f32[2,8,2,168,128]{4,3,2,1,0:T(8,128)S(1)}, f32[152,128]{1,0:T(8,128)S(1)}, f32[152,128]{1,0:T(8,128)S(1)}, f32[48,256]{1,0:T(8,128)S(1)}, f32[48,256]{1,0:T(8,128)S(1)}) custom-call(f32[2,8,152,256]{3,2,1,0:T(8,128)} %tracers.1, f32[2,8,152,256]{3,2,1,0:T(8,128)} %east.5, f32[2,8,152,256]{3,2,1,0:T(8,128)} %north.5), custom_call_target="tpu_custom_call" | custom-call | flops 1000000 | bytes 4980736 | tf_op jit(solution)/shard_map/pallas_call | solution.py:734
  3.4 0.0 copy-done.4
  3.4 0.0 copy-start
  3.4 0.0 copy-start.1
  3.4 0.0 copy-start.2
  3.4 5.5 %shard_map.78 = (f32[2,8,2,168,128]{4,3,2,1,0:T(8,128)S(1)}, f32[152,128]{1,0:T(8,128)S(1)}, f32[152,128]{1,0:T(8,128)S(1)}, f32[2,3,8,2,152,128]{5,4,3,2,1,0:T(...) custom-call(f32[2,8,2,168,128]{4,3,2,1,0:T(8,128)S(1)} %get-tuple-el, ...), custom_call_target="tpu_custom_call", output_to_operand_aliasing={{7}: (5, {}), {8}: (6, {})} | custom-call | flops 10000000 | bytes 2490368 | tf_op jit(solution)/shard_map/pallas_call | solution.py:747
  8.9 2.6 %collective-permute-start.1 = (f32[152,128]{1,0:T(8,128)S(1)}, f32[152,128]{1,0:T(8,128)S(1)}, u32[]{:S(2)}, u32[]{:S(2)}) collective-permute-start(f32[152,128]{1,0:T(8,128)S(1)} %get-tuple-element.47), channel_id=1, source_target_pairs={{0,15},{1,2},{2,1},{3,4},{4,3},{5,6},{6,5},{7,8},{8,7},{9,10},{10,... | collective-permute-start | bytes 233480 | tf_op jit(solution)/shard_map/ppermute | solution.py:722
  11.5 0.0 collective-permute-start
  11.5 3.8 %collective-permute-start.3 = (f32[48,256]{1,0:T(8,128)S(1)}, f32[48,256]{1,0:T(8,128)S(1)}, u32[]{:S(2)}, u32[]{:S(2)}) collective-permute-start(f32[48,256]{1,0:T(8,128)S(1)} %get-tuple-element.49), channel_id=1, source_target_pairs={{0,1},{1,0},{2,3},{3,2},{4,5},{5,4},{6,7},{7,6},{8,9},{9,8},{10,11... | collective-permute-start | bytes 147464 | tf_op jit(solution)/shard_map/ppermute | solution.py:722
  15.3 0.0 collective-permute-start.2
  15.3 0.0 copy-done
  15.3 0.0 copy-done.1
  15.3 0.0 copy-done.2
  15.3 0.0 copy-start.3
  15.4 5.0 %shard_map.79 = (f32[2,8,2,168,128]{4,3,2,1,0:T(8,128)S(1)}, f32[152,128]{1,0:T(8,128)S(1)}, f32[152,128]{1,0:T(8,128)S(1)}, f32[2,3,8,2,152,128]{5,4,3,2,1,0:T(...) custom-call(f32[2,8,2,168,128]{4,3,2,1,0:T(8,128)S(1)} %get-tuple-el, ...), custom_call_target="tpu_custom_call", output_to_operand_aliasing={{0}: (5, {}), {1}: (6, {}), {2}: (7, {}), {3}: (8, {}), {4}... | custom-call | flops 40000000 | bytes 9961472 | tf_op jit(solution)/shard_map/pallas_call | solution.py:758
  20.3 0.0 collective-permute-done.3.rows_b.faces_b
  20.3 0.0 collective-permute-done.2.rows_a.faces_a
  20.4 0.0 collective-permute-done.1.got_b.first_b
  20.4 0.0 collective-permute-done.got_a.first_a
  20.4 0.0 copy-done.3
  20.4 1.2 %shard_map.80 = (f32[2,8,2,168,128]{4,3,2,1,0:T(8,128)S(1)}, f32[152,128]{1,0:T(8,128)S(1)}, f32[152,128]{1,0:T(8,128)S(1)}, f32[32,256]{1,0:T(8,128)S(1)}, f32[...) custom-call(f32[152,128]{1,0:T(8,128)S(1)} %collective-permute-done.got_a.first_a, ...), custom_call_target="tpu_custom_call", output_to_operand_aliasing={{0}: (10, {})} | custom-call | flops 1000000 | bytes 1000000 | tf_op jit(solution)/shard_map/pallas_call | solution.py:767
  21.6 3.8 %shard_map.81 = (f32[2,8,2,168,128]{4,3,2,1,0:T(8,128)S(1)}, f32[152,128]{1,0:T(8,128)S(1)}, f32[152,128]{1,0:T(8,128)S(1)}, f32[32,256]{1,0:T(8,128)S(1)}, f32[...) custom-call(f32[2,8,2,168,128]{4,3,2,1,0:T(8,128)S(1)} %get-tuple-el, ...), custom_call_target="tpu_custom_call", output_to_operand_aliasing={{0}: (0, {}), {1}: (1, {}), {2}: (2, {}), {3}: (3, {}), {4}... | custom-call | flops 10000000 | bytes 2490368 | tf_op jit(solution)/shard_map/pallas_call | solution.py:777
  25.4 0.7 %collective-permute-start.4 = (f32[152,128]{1,0:T(8,128)S(1)}, f32[152,128]{1,0:T(8,128)S(1)}, u32[]{:S(2)}, u32[]{:S(2)}) collective-permute-start(f32[152,128]{1,0:T(8,128)S(1)} %get-tuple-element.70.sent), channel_id=1, source_target_pairs={{0,1},{1,0},{2,3},{3,2},{4,5},{5,4},{6,7},{7,6},{8,9},{9,8},{10,11... | collective-permute-start | bytes 233480 | tf_op jit(solution)/shard_map/ppermute | solution.py:722
  26.1 2.2 %collective-permute-start.5 = (f32[152,128]{1,0:T(8,128)S(1)}, f32[152,128]{1,0:T(8,128)S(1)}, u32[]{:S(2)}, u32[]{:S(2)}) collective-permute-start(f32[152,128]{1,0:T(8,128)S(1)} %get-tuple-element.71), channel_id=1, source_target_pairs={{0,15},{1,2},{2,1},{3,4},{4,3},{5,6},{6,5},{7,8},{8,7},{9,10},{10,... | collective-permute-start | bytes 233480 | tf_op jit(solution)/shard_map/ppermute | solution.py:722
  28.4 1.1 %collective-permute-start.6 = (f32[32,256]{1,0:T(8,128)S(1)}, f32[32,256]{1,0:T(8,128)S(1)}, u32[]{:S(2)}, u32[]{:S(2)}) collective-permute-start(f32[32,256]{1,0:T(8,128)S(1)} %get-tuple-element.72), channel_id=1, source_target_pairs={{0,16},{1,17},{2,18},{3,19},{4,20},{5,21},{6,22},{7,23},{8,24},{9,... | collective-permute-start | bytes 98312 | tf_op jit(solution)/shard_map/ppermute | solution.py:722
  29.4 1.1 %collective-permute-start.7 = (f32[32,256]{1,0:T(8,128)S(1)}, f32[32,256]{1,0:T(8,128)S(1)}, u32[]{:S(2)}, u32[]{:S(2)}) collective-permute-start(f32[32,256]{1,0:T(8,128)S(1)} %get-tuple-element.73), channel_id=1, source_target_pairs={{0,1},{1,0},{2,3},{3,2},{4,5},{5,4},{6,7},{7,6},{8,9},{9,8},{10,11... | collective-permute-start | bytes 98312 | tf_op jit(solution)/shard_map/ppermute | solution.py:722
  30.6 2.0 %shard_map.82 = (f32[2,8,2,168,128]{4,3,2,1,0:T(8,128)S(1)}, f32[2,8,2,152,128]{4,3,2,1,0:T(8,128)S(1)}, f32[2,8,2,160,128]{4,3,2,1,0:T(8,128)S(1)}, f32[2,8,2,1...) custom-call(f32[2,8,2,168,128]{4,3,2,1,0:T(8,128)S(1)} %get-tuple-el, ...), custom_call_target="tpu_custom_call", output_to_operand_aliasing={{0}: (0, {}), {1}: (1, {}), {2}: (2, {}), {3}: (3, {}), {4}... | custom-call | flops 40000000 | bytes 9961472 | tf_op jit(solution)/shard_map/pallas_call | solution.py:788
  32.6 0.0 collective-permute-done.6.rows_a
  32.6 1.7 %collective-permute-done.7.rows_b = f32[32,256]{1,0:T(8,128)S(1)} collective-permute-done((f32[32,256]{1,0:T(8,128)S(1)}, f32[32,256]{1,0:T(8,128)S(1)}, u32[]{:S(2)}, u32[]{:S(2)}) %collective-permute-start.7) | collective-permute-done | bytes 32800 | tf_op jit(solution)/shard_map/ppermute | solution.py:722
  34.3 0.0 collective-permute-done.4.got_a
  34.3 0.0 collective-permute-done.5.got_b
  34.3 2.4 %shard_map.83 = (f32[2,8,152,256]{3,2,1,0:T(8,128)}, f32[8,152,256]{2,1,0:T(8,128)}, f32[2,8,2,152,128]{4,3,2,1,0:T(8,128)S(1)}) custom-call(f32[152,128]{1,0:T(8,128)S(1)} %collective-permute-done.4.got_a, f32[152,128]{1,0:T(8,128)S(1)} %collective-permute-done.5.got_b, f32[152,128]{1,0:T(8,128)S(1)} %get-tuple-element.70.sent, ...), custom_call_target="tpu_custom_call", output_to_operand_aliasing={{2}: (14, {})} | custom-call | flops 4000000 | bytes 4980736 | tf_op jit(solution)/shard_map/pallas_call | solution.py:797
Async XLA Ops:
  0.6 2.8 %copy-start.4 = (f32[7]{0:T(128)S(1)}, f32[7]{0:T(128)}, u32[]{:S(2)}) copy-start(f32[7]{0:T(128)} %mix.3) | copy-start | bytes 88
  3.4 11.9 %copy-start = (f32[2,8,152,256]{3,2,1,0:T(8,128)S(1)}, f32[2,8,152,256]{3,2,1,0:T(8,128)}, u32[]{:S(2)}) copy-start(f32[2,8,152,256]{3,2,1,0:T(8,128)} %east.5) | copy-start | bytes 7471108
  3.4 11.9 %copy-start.1 = (f32[2,8,152,256]{3,2,1,0:T(8,128)S(1)}, f32[2,8,152,256]{3,2,1,0:T(8,128)}, u32[]{:S(2)}) copy-start(f32[2,8,152,256]{3,2,1,0:T(8,128)} %north.5) | copy-start | bytes 7471108
  3.4 11.9 %copy-start.2 = (s32[8,152,256]{2,1,0:T(8,128)S(1)}, s32[8,152,256]{2,1,0:T(8,128)}, u32[]{:S(2)}) copy-start(s32[8,152,256]{2,1,0:T(8,128)} %mask.3) | copy-start | bytes 3735556
  8.9 11.4 %collective-permute-start.1 = (f32[152,128]{1,0:T(8,128)S(1)}, f32[152,128]{1,0:T(8,128)S(1)}, u32[]{:S(2)}, u32[]{:S(2)}) collective-permute-start(f32[152,128]{1,0:T(8,128)S(1)} %get-tuple-element.47), channel_id=1, source_target_pairs={{0,15},{1,2},{2,1},{3,4},{4,3},{5,6},{6,5},{7,8},{8,7},{9,10},{10,... | collective-permute-start | bytes 233480 | tf_op jit(solution)/shard_map/ppermute | solution.py:722
  11.5 8.8 %collective-permute-start = (f32[152,128]{1,0:T(8,128)S(1)}, f32[152,128]{1,0:T(8,128)S(1)}, u32[]{:S(2)}, u32[]{:S(2)}) collective-permute-start(f32[152,128]{1,0:T(8,128)S(1)} %get-tuple-element.43.sent), channel_id=1, source_target_pairs={{0,1},{1,0},{2,3},{3,2},{4,5},{5,4},{6,7},{7,6},{8,9},{9,8},{10,11... | collective-permute-start | bytes 233480 | tf_op jit(solution)/shard_map/ppermute | solution.py:722
  11.5 8.8 %collective-permute-start.3 = (f32[48,256]{1,0:T(8,128)S(1)}, f32[48,256]{1,0:T(8,128)S(1)}, u32[]{:S(2)}, u32[]{:S(2)}) collective-permute-start(f32[48,256]{1,0:T(8,128)S(1)} %get-tuple-element.49), channel_id=1, source_target_pairs={{0,1},{1,0},{2,3},{3,2},{4,5},{5,4},{6,7},{7,6},{8,9},{9,8},{10,11... | collective-permute-start | bytes 147464 | tf_op jit(solution)/shard_map/ppermute | solution.py:722
  15.3 5.0 %collective-permute-start.2 = (f32[48,256]{1,0:T(8,128)S(1)}, f32[48,256]{1,0:T(8,128)S(1)}, u32[]{:S(2)}, u32[]{:S(2)}) collective-permute-start(f32[48,256]{1,0:T(8,128)S(1)} %get-tuple-element.48), channel_id=1, source_target_pairs={{0,16},{1,17},{2,18},{3,19},{4,20},{5,21},{6,22},{7,23},{8,24},{9,... | collective-permute-start | bytes 147464 | tf_op jit(solution)/shard_map/ppermute | solution.py:722
  15.3 5.0 %copy-start.3 = (s32[256]{0:T(256)S(1)}, s32[256]{0:T(256)}, u32[]{:S(2)}) copy-start(s32[256]{0:T(256)} %param.10) | copy-start | bytes 3076
  25.4 8.9 %collective-permute-start.4 = (f32[152,128]{1,0:T(8,128)S(1)}, f32[152,128]{1,0:T(8,128)S(1)}, u32[]{:S(2)}, u32[]{:S(2)}) collective-permute-start(f32[152,128]{1,0:T(8,128)S(1)} %get-tuple-element.70.sent), channel_id=1, source_target_pairs={{0,1},{1,0},{2,3},{3,2},{4,5},{5,4},{6,7},{7,6},{8,9},{9,8},{10,11... | collective-permute-start | bytes 233480 | tf_op jit(solution)/shard_map/ppermute | solution.py:722
  26.1 8.2 %collective-permute-start.5 = (f32[152,128]{1,0:T(8,128)S(1)}, f32[152,128]{1,0:T(8,128)S(1)}, u32[]{:S(2)}, u32[]{:S(2)}) collective-permute-start(f32[152,128]{1,0:T(8,128)S(1)} %get-tuple-element.71), channel_id=1, source_target_pairs={{0,15},{1,2},{2,1},{3,4},{4,3},{5,6},{6,5},{7,8},{8,7},{9,10},{10,... | collective-permute-start | bytes 233480 | tf_op jit(solution)/shard_map/ppermute | solution.py:722
  28.4 4.2 %collective-permute-start.6 = (f32[32,256]{1,0:T(8,128)S(1)}, f32[32,256]{1,0:T(8,128)S(1)}, u32[]{:S(2)}, u32[]{:S(2)}) collective-permute-start(f32[32,256]{1,0:T(8,128)S(1)} %get-tuple-element.72), channel_id=1, source_target_pairs={{0,16},{1,17},{2,18},{3,19},{4,20},{5,21},{6,22},{7,23},{8,24},{9,... | collective-permute-start | bytes 98312 | tf_op jit(solution)/shard_map/ppermute | solution.py:722
  29.4 4.9 %collective-permute-start.7 = (f32[32,256]{1,0:T(8,128)S(1)}, f32[32,256]{1,0:T(8,128)S(1)}, u32[]{:S(2)}, u32[]{:S(2)}) collective-permute-start(f32[32,256]{1,0:T(8,128)S(1)} %get-tuple-element.73), channel_id=1, source_target_pairs={{0,1},{1,0},{2,3},{3,2},{4,5},{5,4},{6,7},{7,6},{8,9},{9,8},{10,11... | collective-permute-start | bytes 98312 | tf_op jit(solution)/shard_map/ppermute | solution.py:722
